TPU v7x, 32 devices: a whole 2x2x4 slice. The times are simulated.
32 devices in a mesh: blk: 8 (over y, x, core), dom: 4 (over z).
Axes of the slice: x: 2, y: 2, z: 4, core: 2. Of those that a mesh axis runs over, the one named last changes fastest.
Arguments:
- pno_basis: float32 [256, 64, 256], P(('blk', 'dom')), may hold values from -0.375 to 0.375
- amplitudes: float32 [256, 4096], P(('blk', 'dom')), may hold values from -6 to 6
- send_list: int32 [8, 4, 8, 1], P('blk', 'dom'), may hold values from 0 to 7
- couple: int32 [256, 8], P(('blk', 'dom')), may hold values from 0 to 7, as said below
- couple_weight: float32 [256, 8], P(('blk', 'dom')), may hold values from 0.25 to 1
- fit_weight: float32 [256, 16], P(('blk', 'dom')), may hold values from 0.25 to 1
- fit_blocks: float32 [16, 2, 256, 256], P('blk', None, 'dom'), may hold values from -0.375 to 0.375
Outputs:
- updated: float32 [256, 4096], P(('blk', 'dom'))
Inputs may be any that keep to these rules, and one draw needn't show every extreme that they name: `couple`: slot j of a device holds what peer j // 1 of blk sent it in its place j % 1; on every device each slot is named by at least one coupling.
All inputs are finite; a program needn't handle non-finite values.
Results may differ from a plain program's by a relative error of at most 0.0003.
Values sent between devices are 32-bit elements; how exact they have to be, the bound alone decides.
No kernel may reach another device: no remote copies, remote signals or barrier semaphores. Data moves between devices by JAX's collectives and lax.ppermute only.
A program may use at most 64 MiB of HBM per device.

v0:
```python
import jax
import jax.numpy as jnp
from jax import lax
from jax.experimental import pallas as pl
from jax.experimental.pallas import tpu as pltpu
from jax.sharding import PartitionSpec as P

HIGHEST = lax.Precision.HIGHEST
SET = 4
NN = (((1,), (0,)), ((), ()))
NT = (((1,), (1,)), ((), ()))


def halves(x):
    high = x.astype(jnp.bfloat16)
    return high, (x - high.astype(jnp.float32)).astype(jnp.bfloat16)


def dot(a, b, dims):
    return lax.dot_general(a, b, dims, preferred_element_type=jnp.float32)


def dot3(a, b, dims):
    (a_high, a_low), (b_high, b_low) = a, b
    return dot(a_high, b_high, dims) + (dot(a_high, b_low, dims) + dot(a_low, b_high, dims))


def stack(parts, axis=0):
    return jnp.concatenate(parts, axis=axis)


def from_partner(x, axis, flip):
    return lax.ppermute(x, axis, [(i, i ^ flip) for i in range(lax.axis_size(axis))])


def from_behind(x, axis, by):
    count = lax.axis_size(axis)
    return lax.ppermute(x, axis, [(i, (i + by) % count) for i in range(count)])


def vmem(count):
    return [pl.BlockSpec(memory_space=pltpu.VMEM)] * count


def pack_kernel(send, basis, amps, out):
    peer_count, row_count, lane_count = out.shape
    pno_count = basis.shape[1]
    for peer in range(peer_count):
        pair = send[peer]
        out[peer, :pno_count] = basis[pair]
        for i in range(row_count - pno_count):
            at = pno_count + i
            out[peer, at:at + 1, :] = amps[pl.ds(pair, 1), i * lane_count:(i + 1) * lane_count]


def pack_pairs(send_order, basis, amps):
    _, pno_count, orbital_count = basis.shape
    rows = pno_count + amps.shape[1] // orbital_count
    return pl.pallas_call(
        pack_kernel,
        out_shape=jax.ShapeDtypeStruct((send_order.shape[0], rows, orbital_count), jnp.float32),
        in_specs=[pl.BlockSpec(memory_space=pltpu.SMEM), *vmem(2)],
        out_specs=vmem(1)[0],
        compiler_params=pltpu.CompilerParams(vmem_limit_bytes=62 * 2**20),
        cost_estimate=pl.CostEstimate(flops=0, bytes_accessed=4 * basis.size, transcendentals=0),
    )(send_order, basis, amps)


def dress_kernel(couple, couple_weight, fit_weight, basis, amps, coupled, dressed, result, turned, paired, partners):
    pair_count, pno_count, orbital_count = basis.shape
    half = pno_count // 2
    slot_count = coupled.shape[0]
    width = 2 * pno_count
    for i in range(half):
        paired[pl.ds(i, pair_count, stride=half), :] = amps[:, i * width:(i + 1) * width]
    for pair in range(pair_count):
        packed = paired[pair * half:(pair + 1) * half]
        for i in range(2):
            turned[pair, pl.ds(i, half, stride=2), :] = packed[:, i * pno_count:(i + 1) * pno_count]
    own = halves(basis[...].reshape(pair_count * pno_count, orbital_count))
    others = halves(coupled[:, :pno_count].reshape(slot_count * pno_count, orbital_count))
    overlap = halves(dot3(own, others, NT))
    left, slot_weight = [], []
    for slot in range(slot_count):
        cols = slice(slot * pno_count, (slot + 1) * pno_count)
        packed = coupled[slot, pno_count:]
        step = orbital_count // pno_count
        for i in range(step):
            lanes = slice(i * pno_count, (i + 1) * pno_count)
            partners[slot, pl.ds(i, packed.shape[0], stride=step), :] = packed[:, lanes]
        left.append(dot3([x[:, cols] for x in overlap], halves(partners[slot]), NN))
        named = jnp.where(couple[...] == slot, couple_weight[...], 0.0)
        slot_weight.append(jnp.sum(named, axis=1, keepdims=True))
    dressed[:, half:, :] = jnp.zeros((pair_count, dressed.shape[1] - half, 2 * pno_count), jnp.float32)
    for pair in range(pair_count):
        rows = slice(pair * pno_count, (pair + 1) * pno_count)
        scaled = stack([x[rows] * w[pair:pair + 1] for x, w in zip(left, slot_weight)], 1)
        total = turned[pair] + dot3(halves(scaled), [x[rows] for x in overlap], NT)
        dressed[pair, :half] = stack([total[:half], total[half:]], 1)
        turned[pair] = total
        result[pair] = two_to_one(turned, pair, half)
        dressed[pair, half:half + 1, : fit_weight.shape[1]] = fit_weight[pair:pair + 1, :]


def two_to_one(ref, pair, half):
    return stack([ref[pair, pl.ds(i, half, stride=2), :] for i in range(2)], 1)


def dress(couple, couple_weight, fit_weight, basis, amps, coupled):
    pair_count, pno_count, _ = basis.shape
    return pl.pallas_call(
        dress_kernel,
        out_shape=tuple(
            jax.ShapeDtypeStruct((pair_count, pno_count // 2 + more, 2 * pno_count), jnp.float32) for more in (8, 0)
        ),
        in_specs=vmem(6),
        out_specs=tuple(vmem(2)),
        scratch_shapes=[
            pltpu.VMEM((pair_count, pno_count, pno_count), jnp.float32),
            pltpu.VMEM((pair_count * pno_count // 2, 2 * pno_count), jnp.float32),
            pltpu.VMEM((coupled.shape[0], pno_count, pno_count), jnp.float32),
        ],
        compiler_params=pltpu.CompilerParams(vmem_limit_bytes=10 * 2**20),
        cost_estimate=pl.CostEstimate(flops=4 * 10**9, bytes_accessed=8 * basis.size, transcendentals=0),
    )(couple, couple_weight, fit_weight, basis, amps, coupled)


def fold(x):
    return x + pltpu.roll(x, x.shape[1] // 2, 1)


def left_lanes(x):
    return lax.broadcasted_iota(jnp.int32, x.shape, 1) < x.shape[1] // 2


def split(x):
    high = x.astype(jnp.bfloat16)
    wide = high.astype(jnp.float32)
    return high, wide, x - wide


def high_low(x):
    _, high, low = split(x)
    return jnp.where(left_lanes(x), high, low).astype(jnp.bfloat16)


def split_blocks(pieces, block_cat):
    dom_count = len(pieces)
    block_count, part_count, row_count, orbital_count = pieces[0].shape
    place = lax.axis_index("dom")
    for shift, piece in enumerate(pieces):
        start = lax.rem(place + dom_count - shift, dom_count) * row_count
        for b in range(block_count):
            for m in range(part_count):
                high, low = halves(piece[b, m])
                for i, x in enumerate((high, high, low)):
                    at = pl.multiple_of(start + i * orbital_count, row_count)
                    block_cat[m, b, pl.ds(at, row_count), :] = x


def split_basis(basis, wide):
    orbital_count = basis.shape[2]
    high, low = halves(basis[...])
    for i, x in enumerate((high, low, high)):
        wide[:, :, i * orbital_count:(i + 1) * orbital_count] = x


def project_slice(wide, block, projected, at):
    pair_count, pno_count, lane_count = wide.shape
    orbital_count = block.shape[1]
    basis = wide[...].reshape(pair_count * pno_count, lane_count)
    product = halves(dot(basis, block[...], NN).reshape(pair_count, pno_count, orbital_count))
    for i in range(2):
        projected[:, at:at + pno_count, i * orbital_count:(i + 1) * orbital_count] = product[i]


def inner_pair(wide, projected, inner_left, inner_right, pair, here):
    _, pno_count, lane_count = wide.shape
    orbital_count = lane_count // 3
    size = inner_left.shape[1]
    both = stack([wide[pair, :, i * orbital_count:(i + 1) * orbital_count] for i in range(2)])
    product = [projected[pair, :, i * orbital_count:(i + 1) * orbital_count] for i in range(2)]
    inner = fold(dot(product[0], both, NT) + dot(product[1], both, NT))
    inner_left[here] = high_low(inner[:size])
    high, _, low = split(inner[size:])
    low = jnp.where(left_lanes(low), low, 0.0).astype(jnp.bfloat16)
    for b in range(size // pno_count):
        rows = slice(b * pno_count, (b + 1) * pno_count)
        lanes = slice(b * 2 * pno_count, (b + 1) * 2 * pno_count)
        inner_right[here, :pno_count, lanes] = high[rows]
        inner_right[here, pno_count:, lanes] = low[rows]


def project_all(bases, pieces, inner_left, inner_right, scratch):
    block_cat, wide, projected = scratch
    pair_count, pno_count, _ = bases[0].shape
    part_count, block_count = block_cat.shape[:2]
    split_blocks(pieces, block_cat)
    for member, basis in enumerate(bases):
        split_basis(basis, wide.at[pl.ds(member * pair_count, pair_count)])
    for m in range(part_count):
        for b in range(block_count):
            project_slice(wide, block_cat.at[m, b], projected, (m * block_count + b) * pno_count)
    for pair in range(len(bases) * pair_count):
        inner_pair(wide, projected, inner_left, inner_right, pair, pair)


def project_kernel(member_count, *refs):
    bases, refs = refs[:member_count], refs[member_count:]
    *pieces, inner_left, inner_right = refs[:-3]
    project_all(bases, pieces, inner_left, inner_right, refs[-3:])


def inner_shapes(pairs, pno_count, block_count):
    return (
        ((pairs, block_count * pno_count, 2 * pno_count), jnp.bfloat16),
        ((pairs, 2 * pno_count, block_count * 2 * pno_count), jnp.bfloat16),
    )


def project_scratch(bases, pieces):
    pair_count, pno_count, _ = bases[0].shape
    block_count, part_count, _, orbital_count = pieces[0].shape
    return [
        pltpu.VMEM((part_count, block_count, 3 * orbital_count, orbital_count), jnp.bfloat16),
        pltpu.VMEM((len(bases) * pair_count, pno_count, 3 * orbital_count), jnp.bfloat16),
        pltpu.VMEM((len(bases) * pair_count, part_count * block_count * pno_count, 2 * orbital_count), jnp.bfloat16),
    ]


def project_flops(bases, pieces):
    pair_count, pno_count, _ = bases[0].shape
    block_count, part_count, _, orbital_count = pieces[0].shape
    rows = len(bases) * pair_count * pno_count * block_count * part_count
    return 6 * rows * orbital_count * (orbital_count + pno_count)


def project(bases, pieces):
    pair_count, pno_count, _ = bases[0].shape
    shapes = inner_shapes(len(bases) * pair_count, pno_count, pieces[0].shape[0])
    return pl.pallas_call(
        lambda *refs: project_kernel(len(bases), *refs),
        out_shape=tuple(jax.ShapeDtypeStruct(*x) for x in shapes),
        in_specs=vmem(len(bases) + len(pieces)),
        out_specs=tuple(vmem(2)),
        scratch_shapes=project_scratch(bases, pieces),
        compiler_params=pltpu.CompilerParams(vmem_limit_bytes=28 * 2**20),
        cost_estimate=pl.CostEstimate(flops=project_flops(bases, pieces), bytes_accessed=2**20, transcendentals=0),
    )(*bases, *pieces)


def finish_kernel(members, group_count, dom_count, *refs):
    count = len(members)
    groups, refs = refs[:2 * group_count], refs[2 * group_count:]
    bases, pieces, refs = refs[:count], refs[count:count + dom_count], refs[count + dom_count:]
    dressed, after, scratch = refs[:count], refs[count:2 * count], refs[2 * count:]
    inner_left, inner_right, square, moved, total = scratch[:5]
    groups = [*groups, inner_left, inner_right]
    group_count += 1
    pair_count, _, lane_count = dressed[0].shape
    pno_count = lane_count // 2
    half = pno_count // 2
    block_count = inner_left.shape[1] // pno_count
    group_total = lax.axis_size("blk")
    me = lax.axis_index("blk")
    pairs = [(index, pair) for index in range(count) for pair in range(pair_count)]

    def row_of(group, at):
        full = group < group_count - 1
        return members[at // pair_count] * pair_count + at % pair_count if full else at

    weights = []
    for index, member in enumerate(members):
        row = dressed[index][:, half:half + 1, :]
        lane = lax.broadcasted_iota(jnp.int32, row.shape, 2)
        for group in range(group_count):
            stop = lax.rem((me ^ member) + 2 * group_total + group * SET - me, group_total)
            for b in range(block_count):
                kept = jnp.where(lane == stop * block_count + b, row, 0.0)
                weights.append(jnp.sum(kept, axis=2, keepdims=True))
    project_all(bases, pieces, inner_left, inner_right, scratch[5:])
    for at, (index, pair) in enumerate(pairs):
        packed = dressed[index][pair, :half]
        other = pltpu.roll(packed, pno_count, 1)
        keep = left_lanes(packed)
        _, high, low = split(stack([jnp.where(keep, packed, other), jnp.where(keep, other, packed)]))
        square[at, :pno_count] = jnp.where(left_lanes(low), high, low).astype(jnp.bfloat16)
        square[at, pno_count:] = jnp.where(left_lanes(low), high, 0.0).astype(jnp.bfloat16)
    for at, (index, pair) in enumerate(pairs):
        for group in range(group_count):
            product = fold(dot(groups[2 * group][row_of(group, at)], square[at], NN))
            for b in range(block_count):
                weight = weights[(index * group_count + group) * block_count + b][pair]
                lanes = slice(b * lane_count, (b + 1) * lane_count)
                moved[at, group, :, lanes] = high_low(product[b * pno_count:(b + 1) * pno_count] * weight)
    for at, (index, pair) in enumerate(pairs):
        terms = [dot(moved[at, group], groups[2 * group + 1][row_of(group, at)], NT) for group in range(group_count)]
        total[at] = fold(sum(terms[1:], terms[0]))
    for at, (index, pair) in enumerate(pairs):
        rows = [total[at, pl.ds(i, half, stride=2), :] for i in range(2)]
        after[index][pair] = jnp.where(left_lanes(rows[0]), *rows)


def finish(members, groups, bases, pieces, dressed):
    pair_count, _, lane_count = dressed[0].shape
    pno_count = lane_count // 2
    pairs = len(members) * pair_count
    group_count = len(groups)
    block_count = pieces[0].shape[0]
    operands = [x for group in groups for x in group] + bases + pieces + dressed
    products = pairs * pno_count**3 * 2 * (group_count + 1) * block_count
    shapes = inner_shapes(pairs, pno_count, block_count)
    return pl.pallas_call(
        lambda *refs: finish_kernel(members, group_count, len(pieces), *refs),
        out_shape=[jax.ShapeDtypeStruct((pair_count, pno_count // 2, lane_count), jnp.float32)] * len(members),
        in_specs=vmem(len(operands)),
        out_specs=vmem(len(members)),
        scratch_shapes=[
            *[pltpu.VMEM(*x) for x in shapes],
            pltpu.VMEM((pairs, lane_count, lane_count), jnp.bfloat16),
            pltpu.VMEM((pairs, group_count + 1, pno_count, block_count * lane_count), jnp.bfloat16),
            pltpu.VMEM((pairs, pno_count, lane_count), jnp.float32),
            *project_scratch(bases, pieces),
        ],
        compiler_params=pltpu.CompilerParams(vmem_limit_bytes=24 * 2**20),
        cost_estimate=pl.CostEstimate(
            flops=project_flops(bases, pieces) + 6 * products, bytes_accessed=2**20, transcendentals=0
        ),
    )(*operands)


def gather_pieces(mine, axis):
    count = lax.axis_size(axis)
    up, down = [mine], []
    for shift in range(1, count):
        if shift <= (count - 1) // 2:
            up.append(from_behind(up[-1], axis, 1))
        else:
            down.append(from_behind(down[-1] if down else mine, axis, count - 1))
    return up + down[::-1]


def on_device_shared(pno_basis, amplitudes, send_list, couple, couple_weight, fit_weight, fit_blocks):
    pair_count, pno_count, _ = pno_basis.shape
    group_total = lax.axis_size("blk")
    pieces = gather_pieces(fit_blocks, "dom")
    across = from_partner(pno_basis, "blk", 2)
    far = [([from_behind(fit_blocks, "blk", by)], by) for by in range(SET, group_total, SET)]
    sent = pack_pairs(send_list.reshape(-1), pno_basis, amplitudes)
    sent, *heads = lax.optimization_barrier((sent, *[group[0] for group, _ in far]))
    far = [([head], by) for head, (_, by) in zip(heads, far)]
    coupled = lax.all_to_all(sent, "blk", split_axis=0, concat_axis=0, tiled=True)
    across, pieces[1], pieces[-1] = lax.optimization_barrier((across, pieces[1], pieces[-1]))
    bases = [pno_basis, from_partner(pno_basis, "blk", 1), across, from_partner(across, "blk", 1)]
    coupled, *bases = lax.optimization_barrier((coupled, *bases))
    own, updated = dress(couple, couple_weight, fit_weight, pno_basis, amplitudes, coupled)
    last = len(pieces) // 2
    _, pieces[last] = lax.optimization_barrier((own, pieces[last]))
    groups = [pieces]
    for group, by in far:
        group += [from_behind(x, "blk", by) for x in pieces[1:]]
        if last > 1:
            source, pieces[-1] = lax.optimization_barrier((group[0], pieces[-1]))
            group[-1] = from_behind(source, "dom", len(pieces) - 1)
        groups.append(group)
    inner = [project(bases, group) for group in groups[:-1]]
    final = groups[-1]
    dressed = [own, *[from_partner(own, "blk", flip) for flip in range(1, SET)]]
    for members in ((2, 3), (0, 1)):
        partial = finish(
            members, inner, [bases[member] for member in members], final, [dressed[member] for member in members]
        )
        if members[0]:
            partial, *final = lax.optimization_barrier((partial, *final))
            for member, x in zip(members, partial):
                updated = updated + from_partner(x, "blk", member)
        else:
            mine, beside = partial
            updated, mine, beside = lax.optimization_barrier((updated, mine, from_partner(beside, "blk", 1)))
            updated = updated + mine + beside
    return updated.reshape(pair_count, pno_count * pno_count)


def dress_with(pair_amps, intersection, partner_amps, weights):
    half_product = jnp.einsum("pcab,pcbe->pcae", intersection, partner_amps, precision=HIGHEST)
    sandwich = jnp.einsum("pcae,pcfe->pcaf", half_product, intersection, precision=HIGHEST)
    return pair_amps + jnp.einsum("pc,pcaf->paf", weights, sandwich, precision=HIGHEST)


def fit_term(pair_basis, dressed, blocks, weights):
    pair_count, pno_count, orbital_count = pair_basis.shape
    flat_basis = pair_basis.reshape(pair_count * pno_count, orbital_count)
    stacked = blocks.reshape(2 * orbital_count, orbital_count)
    projected = jnp.dot(
        flat_basis, stacked.T, precision=HIGHEST, preferred_element_type=jnp.float32
    )
    projected = projected.reshape(pair_count, pno_count, 2, orbital_count)
    inner_blocks = jnp.einsum("par,pbmr->mpab", pair_basis, projected, precision=HIGHEST)
    left_product = jnp.einsum("pai,pij->paj", inner_blocks[0], dressed, precision=HIGHEST)
    fit_contrib = jnp.einsum("paj,pbj->pab", left_product, inner_blocks[1], precision=HIGHEST)
    return weights[:, None, None] * fit_contrib


def on_device_ring(pno_basis, amplitudes, send_list, couple, couple_weight, fit_weight, fit_blocks):
    pair_count, pno_count, _ = pno_basis.shape
    block_count = fit_blocks.shape[0]
    pair_amps = amplitudes.reshape(pair_count, pno_count, pno_count)
    send_order = send_list.reshape(-1)
    basis_in = lax.all_to_all(jnp.take(pno_basis, send_order, axis=0), "blk", split_axis=0, concat_axis=0, tiled=True)
    amps_in = lax.all_to_all(jnp.take(pair_amps, send_order, axis=0), "blk", split_axis=0, concat_axis=0, tiled=True)
    partner_basis = jnp.take(basis_in, couple, axis=0)
    intersection = jnp.einsum("par,pcbr->pcab", pno_basis, partner_basis, precision=HIGHEST)
    dressed = dress_with(pair_amps, intersection, jnp.take(amps_in, couple, axis=0), couple_weight)
    updated = dressed
    current = lax.all_gather(fit_blocks, "dom", axis=2, tiled=True)
    for stop in range(fit_weight.shape[1] // block_count):
        if stop > 0:
            current = from_behind(current, "blk", 1)
        for b in range(block_count):
            updated = updated + fit_term(pno_basis, dressed, current[b], fit_weight[:, stop * block_count + b])
    return updated.reshape(pair_count, pno_count * pno_count)


def solution(mesh):
    placed = (
        P(("blk", "dom"), None, None),
        P(("blk", "dom"), None),
        P("blk", "dom", None, None),
        P(("blk", "dom"), None),
        P(("blk", "dom"), None),
        P(("blk", "dom"), None),
        P("blk", None, "dom", None),
    )

    def on_device(*args):
        send_list, fit_weight, fit_blocks = args[2], args[5], args[6]
        group_total = mesh.shape["blk"]
        meets_all = fit_weight.shape[1] == group_total * fit_blocks.shape[0]
        if meets_all and group_total % SET == 0 and group_total > SET and group_total & (group_total - 1) == 0 and send_list.shape[3] == 1:
            return on_device_shared(*args)
        return on_device_ring(*args)

    return jax.shard_map(
        on_device, mesh=mesh, in_specs=placed, out_specs=P(("blk", "dom"), None), check_vma=False
    )
```

profile of v0, /device:TPU:0, one launch (start us, length us, event | category | flops | bytes accessed | tf_op | source)
XLA Modules:
  0.0 52.4 jit_solution(5539864443787489496)
XLA Ops:
  0.0 0.0 copy-start
  0.0 3.0 %collective-permute-start.2 = (f32[8,64,256]{2,1,0:T(8,128)}, f32[8,64,256]{2,1,0:T(8,128)S(1)}, u32[]{:S(2)}, u32[]{:S(2)}) collective-permute-start(f32[8,64,256]{2,1,0:T(8,128)} %refs_2_), channel_id=1, source_target_pairs={{0,8},{4,12},{8,0},{12,4},{16,24},{20,28},{24,16},{28,20},{1,9},{5... | collective-permute-start | bytes 1572872 | tf_op jit(solution)/shard_map/ppermute | solution.py:33
  3.0 1.5 %collective-permute-start = (f32[2,2,64,256]{3,2,1,0:T(8,128)}, f32[2,2,64,256]{3,2,1,0:T(8,128)S(1)}, u32[]{:S(2)}, u32[]{:S(2)}) collective-permute-start(f32[2,2,64,256]{3,2,1,0:T(8,128)} %refs_4_.1), channel_id=1, source_target_pairs={{0,16},{4,20},{8,24},{12,28},{16,0},{20,4},{24,8},{28,12},{1,17},{... | collective-permute-start | bytes 786440 | tf_op jit(solution)/shard_map/ppermute | solution.py:38
  4.6 1.6 %collective-permute-start.3 = (f32[2,2,64,256]{3,2,1,0:T(8,128)}, f32[2,2,64,256]{3,2,1,0:T(8,128)}, u32[]{:S(2)}, u32[]{:S(2)}) collective-permute-start(f32[2,2,64,256]{3,2,1,0:T(8,128)} %refs_4_.1), channel_id=1, source_target_pairs={{0,1},{1,2},{2,3},{3,0},{4,5},{5,6},{6,7},{7,4},{8,9},{9,10},{10,1... | collective-permute-start | bytes 786440 | tf_op jit(solution)/shard_map/ppermute | solution.py:38
  6.1 2.2 %collective-permute-start.4 = (f32[2,2,64,256]{3,2,1,0:T(8,128)}, f32[2,2,64,256]{3,2,1,0:T(8,128)}, u32[]{:S(2)}, u32[]{:S(2)}) collective-permute-start(f32[2,2,64,256]{3,2,1,0:T(8,128)} %refs_4_.1), channel_id=1, source_target_pairs={{0,3},{1,0},{2,1},{3,2},{4,7},{5,4},{6,5},{7,6},{8,11},{9,8},{10,9... | collective-permute-start | bytes 786440 | tf_op jit(solution)/shard_map/ppermute | solution.py:38
  8.4 2.0 %shard_map.73 = f32[8,80,256]{2,1,0:T(8,128)} custom-call(s32[8]{0:T(128)} %bitcast.6, f32[8,64,256]{2,1,0:T(8,128)} %refs_2_, f32[8,4096]{1,0:T(8,128)} %amps.3), custom_call_target="tpu_custom_call" | custom-call | bytes 524288 | tf_op jit(solution)/shard_map/pallas_call | solution.py:59
  10.4 0.6 %collective-permute-done.refs_4_ = f32[2,2,64,256]{3,2,1,0:T(8,128)S(1)} collective-permute-done((f32[2,2,64,256]{3,2,1,0:T(8,128)}, f32[2,2,64,256]{3,2,1,0:T(8,128)S(1)}, u32[]{:S(2)}, u32[]{:S(2)}) %collective-permute-start) | collective-permute-done | bytes 262176 | tf_op jit(solution)/shard_map/ppermute | solution.py:38
  11.0 3.5 %all-to-all-start = ((f32[8,80,256]{2,1,0:T(8,128)}), f32[8,80,256]{2,1,0:T(8,128)S(1)}, u32[]{:S(2)}, u32[]{:S(2)}) async-start(f32[8,80,256]{2,1,0:T(8,128)} %shard_map.73), calls=%async_computation | async-start | bytes 1310720 | tf_op jit(solution)/shard_map/all_to_all | solution.py:352
  14.6 0.0 copy-done
  14.6 0.0 copy-start.2
  14.6 0.4 collective-permute-start.1
  15.0 0.9 %collective-permute-done.3.refs_5_ = f32[2,2,64,256]{3,2,1,0:T(8,128)} collective-permute-done((f32[2,2,64,256]{3,2,1,0:T(8,128)}, f32[2,2,64,256]{3,2,1,0:T(8,128)}, u32[]{:S(2)}, u32[]{:S(2)}) %collective-permute-start.3) | collective-permute-done | bytes 262176 | tf_op jit(solution)/shard_map/ppermute | solution.py:38
  16.0 3.3 %collective-permute-done.4.refs_7_ = f32[2,2,64,256]{3,2,1,0:T(8,128)} collective-permute-done((f32[2,2,64,256]{3,2,1,0:T(8,128)}, f32[2,2,64,256]{3,2,1,0:T(8,128)}, u32[]{:S(2)}, u32[]{:S(2)}) %collective-permute-start.4) | collective-permute-done | bytes 262176 | tf_op jit(solution)/shard_map/ppermute | solution.py:38
  19.3 0.0 collective-permute-done.2.refs_2_
  19.3 0.0 collective-permute-start.5
  19.3 2.4 %collective-permute-start.6 = (f32[2,2,64,256]{3,2,1,0:T(8,128)}, f32[2,2,64,256]{3,2,1,0:T(8,128)}, u32[]{:S(2)}, u32[]{:S(2)}) collective-permute-start(f32[2,2,64,256]{3,2,1,0:T(8,128)} %collective-permute-done.4.refs_7_), channel_id=1, source_target_pairs={{0,3},{1,0},{2,1},{3,2},{4,7},{5,4},{6,5},{7,6},{8,11},{9,8},{10,9... | collective-permute-start | bytes 786440 | tf_op jit(solution)/shard_map/ppermute | solution.py:38
  21.6 0.5 collective-permute-start.7
  22.2 0.4 collective-permute-start.9
  22.6 0.0 collective-permute-done.1.refs_1_.refs_3_
  22.6 3.1 %all-to-all-done.coupled = f32[8,80,256]{2,1,0:T(8,128)S(1)} async-done(((f32[8,80,256]{2,1,0:T(8,128)}), f32[8,80,256]{2,1,0:T(8,128)S(1)}, u32[]{:S(2)}, u32[]{:S(2)}) %all-to-all-start) | async-done | bytes 655392 | tf_op jit(solution)/shard_map/all_to_all | solution.py:352
  25.7 0.0 collective-permute-done.5.refs_3_
  25.7 0.0 copy-done.1
  25.7 0.0 copy-done.3
  25.8 0.0 copy-done.4
  25.8 0.0 copy-done.5
  25.8 2.3 %shard_map.74 = (f32[8,40,128]{2,1,0:T(8,128)S(1)}, f32[8,32,128]{2,1,0:T(8,128)S(1)}) custom-call(s32[8,8]{1,0:T(8,128)S(1)} %copy-done.3, f32[8,8]{1,0:T(8,128)S(1)} %copy-done.4, f32[8,16]{1,0:T(8,128)S(1)} %copy-done.5, f32[8,64,256]{2,1,0:T(8,128)S(1)} %copy-done, f32[8,4096]{1,0:T(8,128)S(1)} %copy-done.1, f32[8,80,256]{2,1,0:T(8,128)S(1)} %all-to-all-done.coupled), custom_call_target="tpu_custom_call" | custom-call | flops 4000000000 | bytes 1048576 | tf_op jit(solution)/shard_map/pallas_call | solution.py:111
  28.1 0.6 %collective-permute-start.10 = (f32[8,40,128]{2,1,0:T(8,128)S(1)}, f32[8,40,128]{2,1,0:T(8,128)S(1)}, u32[]{:S(2)}, u32[]{:S(2)}) collective-permute-start(f32[8,40,128]{2,1,0:T(8,128)S(1)} %get-tuple-element.44.refs_8_), channel_id=1, source_target_pairs={{0,8},{4,12},{8,0},{12,4},{16,24},{20,28},{24,16},{28,20},{1,9},{5... | collective-permute-start | bytes 491528 | tf_op jit(solution)/shard_map/ppermute | solution.py:33
  28.7 0.0 collective-permute-start.11
  28.7 0.0 collective-permute-done.6.refs_6_
  28.7 0.5 collective-permute-start.8
  29.2 0.0 copy-done.2
  29.2 6.9 %shard_map.75 = (bf16[32,128,128]{2,1,0:T(8,128)(2,1)S(1)}, bf16[32,128,256]{2,1,0:T(8,128)(2,1)S(1)}) custom-call(f32[8,64,256]{2,1,0:T(8,128)S(1)} %copy-done, f32[8,64,256]{2,1,0:T(8,128)S(1)} %collective-permute-done.1.refs_1_.refs_3_, f32[8,64,256]{2,1,0:T(8,128)S(1)} %collective-permute-done.2.refs_2_, ...), custom_call_target="tpu_custom_call" | custom-call | flops 4026531840 | bytes 1048576 | tf_op jit(solution)/shard_map/pallas_call | solution.py:241
  36.1 0.0 collective-permute-done.7.refs_5_
  36.1 1.4 %collective-permute-start.14 = (f32[8,40,128]{2,1,0:T(8,128)S(1)}, f32[8,40,128]{2,1,0:T(8,128)S(1)}, u32[]{:S(2)}, u32[]{:S(2)}) collective-permute-start(f32[8,40,128]{2,1,0:T(8,128)S(1)} %get-tuple-element.44.refs_8_), channel_id=1, source_target_pairs={{0,4},{4,0},{8,12},{12,8},{16,20},{20,16},{24,28},{28,24},{1,5},{5... | collective-permute-start | bytes 491528 | tf_op jit(solution)/shard_map/ppermute | solution.py:33
  37.6 0.0 collective-permute-done.9.refs_7_
  37.6 0.0 collective-permute-done.10.refs_8_
  37.6 0.0 collective-permute-done.11.refs_9_
  37.6 0.0 collective-permute-done.8.refs_6_
  37.6 5.2 %shard_map.76 = (f32[8,32,128]{2,1,0:T(8,128)S(1)}, f32[8,32,128]{2,1,0:T(8,128)S(1)}) custom-call(bf16[32,128,128]{2,1,0:T(8,128)(2,1)S(1)} %get-tuple-element.49.refs_0_, bf16[32,128,256]{2,1,0:T(8,128)(2,1)S(1)} %get-tuple-element.50.refs_1_, f32[8,64,256]{2,1,0:T(8,128)S(1)} %collective-permute-done.2.refs_2_, ...), custom_call_target="tpu_custom_call" | custom-call | flops 2214592512 | bytes 1048576 | tf_op jit(solution)/shard_map/pallas_call | solution.py:313
  42.8 1.1 %collective-permute-start.13 = (f32[8,32,128]{2,1,0:T(8,128)S(1)}, f32[8,32,128]{2,1,0:T(8,128)S(1)}, u32[]{:S(2)}, u32[]{:S(2)}) collective-permute-start(f32[8,32,128]{2,1,0:T(8,128)S(1)} %get-tuple-element.55), channel_id=1, source_target_pairs={{0,12},{4,8},{8,4},{12,0},{16,28},{20,24},{24,20},{28,16},{1,13},{... | collective-permute-start | bytes 393224 | tf_op jit(solution)/shard_map/ppermute | solution.py:33
  43.9 0.9 %collective-permute-start.12 = (f32[8,32,128]{2,1,0:T(8,128)S(1)}, f32[8,32,128]{2,1,0:T(8,128)S(1)}, u32[]{:S(2)}, u32[]{:S(2)}) collective-permute-start(f32[8,32,128]{2,1,0:T(8,128)S(1)} %get-tuple-element.54), channel_id=1, source_target_pairs={{0,8},{4,12},{8,0},{12,4},{16,24},{20,28},{24,16},{28,20},{1,9},{5... | collective-permute-start | bytes 393224 | tf_op jit(solution)/shard_map/ppermute | solution.py:33
  44.8 0.0 collective-permute-done.14.refs_9_
  44.8 5.4 %shard_map.77 = (f32[8,32,128]{2,1,0:T(8,128)S(1)}, f32[8,32,128]{2,1,0:T(8,128)S(1)}) custom-call(bf16[32,128,128]{2,1,0:T(8,128)(2,1)S(1)} %get-tuple-element.49.refs_0_, bf16[32,128,256]{2,1,0:T(8,128)(2,1)S(1)} %get-tuple-element.50.refs_1_, f32[8,64,256]{2,1,0:T(8,128)S(1)} %copy-done, f32[8,64,256]{2,1,0:T(8,128)S(1)} %collective-permute-done.1.refs_1_.refs_3_, ...), custom_call_target="tpu_custom_call" | custom-call | flops 2214592512 | bytes 1048576 | tf_op jit(solution)/shard_map/pallas_call | solution.py:313
  50.2 0.1 collective-permute-start.15
  50.2 0.0 collective-permute-done.13
  50.3 1.2 %collective-permute-done.12 = f32[8,32,128]{2,1,0:T(8,128)S(1)} collective-permute-done((f32[8,32,128]{2,1,0:T(8,128)S(1)}, f32[8,32,128]{2,1,0:T(8,128)S(1)}, u32[]{:S(2)}, u32[]{:S(2)}) %collective-permute-start.12) | collective-permute-done | bytes 131104 | tf_op jit(solution)/shard_map/ppermute | solution.py:33
  51.5 0.1 collective-permute-done.15
  51.6 0.7 %copy.10 = f32[1,8,32,128]{3,1,2,0:T(8,128)} copy(f32[1,8,32,128]{3,2,1,0:T(8,128)S(1)} %add_bitcast_fusion) | data formatting | bytes 262144
  (6 shorter events, 0.1 us)
Async XLA Ops:
  0.0 14.6 %copy-start = (f32[8,64,256]{2,1,0:T(8,128)S(1)}, f32[8,64,256]{2,1,0:T(8,128)}, u32[]{:S(2)}) copy-start(f32[8,64,256]{2,1,0:T(8,128)} %refs_2_) | copy-start | bytes 1572868
  0.0 25.7 %copy-start.1 = (f32[8,4096]{1,0:T(8,128)S(1)}, f32[8,4096]{1,0:T(8,128)}, u32[]{:S(2)}) copy-start(f32[8,4096]{1,0:T(8,128)} %amps.3) | copy-start | bytes 393220
  0.0 25.7 %copy-start.3 = (s32[8,8]{1,0:T(8,128)S(1)}, s32[8,8]{1,0:T(8,128)}, u32[]{:S(2)}) copy-start(s32[8,8]{1,0:T(8,128)} %couple.1) | copy-start | bytes 772
  0.0 25.8 %copy-start.4 = (f32[8,8]{1,0:T(8,128)S(1)}, f32[8,8]{1,0:T(8,128)}, u32[]{:S(2)}) copy-start(f32[8,8]{1,0:T(8,128)} %couple_weight.1) | copy-start | bytes 772
  0.0 25.8 %copy-start.5 = (f32[8,16]{1,0:T(8,128)S(1)}, f32[8,16]{1,0:T(8,128)}, u32[]{:S(2)}) copy-start(f32[8,16]{1,0:T(8,128)} %fit_weight.1) | copy-start | bytes 1540
  0.0 19.3 %collective-permute-start.2 = (f32[8,64,256]{2,1,0:T(8,128)}, f32[8,64,256]{2,1,0:T(8,128)S(1)}, u32[]{:S(2)}, u32[]{:S(2)}) collective-permute-start(f32[8,64,256]{2,1,0:T(8,128)} %refs_2_), channel_id=1, source_target_pairs={{0,8},{4,12},{8,0},{12,4},{16,24},{20,28},{24,16},{28,20},{1,9},{5... | collective-permute-start | bytes 1572872 | tf_op jit(solution)/shard_map/ppermute | solution.py:33
  3.0 8.0 %collective-permute-start = (f32[2,2,64,256]{3,2,1,0:T(8,128)}, f32[2,2,64,256]{3,2,1,0:T(8,128)S(1)}, u32[]{:S(2)}, u32[]{:S(2)}) collective-permute-start(f32[2,2,64,256]{3,2,1,0:T(8,128)} %refs_4_.1), channel_id=1, source_target_pairs={{0,16},{4,20},{8,24},{12,28},{16,0},{20,4},{24,8},{28,12},{1,17},{... | collective-permute-start | bytes 786440 | tf_op jit(solution)/shard_map/ppermute | solution.py:38
  4.6 11.4 %collective-permute-start.3 = (f32[2,2,64,256]{3,2,1,0:T(8,128)}, f32[2,2,64,256]{3,2,1,0:T(8,128)}, u32[]{:S(2)}, u32[]{:S(2)}) collective-permute-start(f32[2,2,64,256]{3,2,1,0:T(8,128)} %refs_4_.1), channel_id=1, source_target_pairs={{0,1},{1,2},{2,3},{3,0},{4,5},{5,6},{6,7},{7,4},{8,9},{9,10},{10,1... | collective-permute-start | bytes 786440 | tf_op jit(solution)/shard_map/ppermute | solution.py:38
  6.1 13.1 %collective-permute-start.4 = (f32[2,2,64,256]{3,2,1,0:T(8,128)}, f32[2,2,64,256]{3,2,1,0:T(8,128)}, u32[]{:S(2)}, u32[]{:S(2)}) collective-permute-start(f32[2,2,64,256]{3,2,1,0:T(8,128)} %refs_4_.1), channel_id=1, source_target_pairs={{0,3},{1,0},{2,1},{3,2},{4,7},{5,4},{6,5},{7,6},{8,11},{9,8},{10,9... | collective-permute-start | bytes 786440 | tf_op jit(solution)/shard_map/ppermute | solution.py:38
  11.0 14.7 %all-to-all-start = ((f32[8,80,256]{2,1,0:T(8,128)}), f32[8,80,256]{2,1,0:T(8,128)S(1)}, u32[]{:S(2)}, u32[]{:S(2)}) async-start(f32[8,80,256]{2,1,0:T(8,128)} %shard_map.73), calls=%async_computation | async-start | bytes 1310720 | tf_op jit(solution)/shard_map/all_to_all | solution.py:352
  14.6 14.6 %copy-start.2 = (f32[2,2,64,256]{3,2,1,0:T(8,128)S(1)}, f32[2,2,64,256]{3,2,1,0:T(8,128)}, u32[]{:S(2)}) copy-start(f32[2,2,64,256]{3,2,1,0:T(8,128)} %refs_4_.1) | copy-start | bytes 786436
  14.6 8.0 %collective-permute-start.1 = (f32[8,64,256]{2,1,0:T(8,128)S(1)}, f32[8,64,256]{2,1,0:T(8,128)S(1)}, u32[]{:S(2)}, u32[]{:S(2)}) collective-permute-start(f32[8,64,256]{2,1,0:T(8,128)S(1)} %copy-done), channel_id=1, source_target_pairs={{0,4},{4,0},{8,12},{12,8},{16,20},{20,16},{24,28},{28,24},{1,5},{5... | collective-permute-start | bytes 1572872 | tf_op jit(solution)/shard_map/ppermute | solution.py:33
  19.3 6.5 %collective-permute-start.5 = (f32[8,64,256]{2,1,0:T(8,128)S(1)}, f32[8,64,256]{2,1,0:T(8,128)S(1)}, u32[]{:S(2)}, u32[]{:S(2)}) collective-permute-start(f32[8,64,256]{2,1,0:T(8,128)S(1)} %collective-permute-done.2.refs_2_), channel_id=1, source_target_pairs={{0,4},{4,0},{8,12},{12,8},{16,20},{20,16},{24,28},{28,24},{1,5},{5... | collective-permute-start | bytes 1572872 | tf_op jit(solution)/shard_map/ppermute | solution.py:33
  19.3 9.4 %collective-permute-start.6 = (f32[2,2,64,256]{3,2,1,0:T(8,128)}, f32[2,2,64,256]{3,2,1,0:T(8,128)}, u32[]{:S(2)}, u32[]{:S(2)}) collective-permute-start(f32[2,2,64,256]{3,2,1,0:T(8,128)} %collective-permute-done.4.refs_7_), channel_id=1, source_target_pairs={{0,3},{1,0},{2,1},{3,2},{4,7},{5,4},{6,5},{7,6},{8,11},{9,8},{10,9... | collective-permute-start | bytes 786440 | tf_op jit(solution)/shard_map/ppermute | solution.py:38
  21.6 14.5 %collective-permute-start.7 = (f32[2,2,64,256]{3,2,1,0:T(8,128)}, f32[2,2,64,256]{3,2,1,0:T(8,128)}, u32[]{:S(2)}, u32[]{:S(2)}) collective-permute-start(f32[2,2,64,256]{3,2,1,0:T(8,128)} %collective-permute-done.3.refs_5_), channel_id=1, source_target_pairs={{0,16},{4,20},{8,24},{12,28},{16,0},{20,4},{24,8},{28,12},{1,17},{... | collective-permute-start | bytes 786440 | tf_op jit(solution)/shard_map/ppermute | solution.py:38
  22.2 15.4 %collective-permute-start.9 = (f32[2,2,64,256]{3,2,1,0:T(8,128)S(1)}, f32[2,2,64,256]{3,2,1,0:T(8,128)}, u32[]{:S(2)}, u32[]{:S(2)}) collective-permute-start(f32[2,2,64,256]{3,2,1,0:T(8,128)S(1)} %collective-permute-done.refs_4_), channel_id=1, source_target_pairs={{0,3},{1,0},{2,1},{3,2},{4,7},{5,4},{6,5},{7,6},{8,11},{9,8},{10,9... | collective-permute-start | bytes 786440 | tf_op jit(solution)/shard_map/ppermute | solution.py:38
  28.1 9.5 %collective-permute-start.10 = (f32[8,40,128]{2,1,0:T(8,128)S(1)}, f32[8,40,128]{2,1,0:T(8,128)S(1)}, u32[]{:S(2)}, u32[]{:S(2)}) collective-permute-start(f32[8,40,128]{2,1,0:T(8,128)S(1)} %get-tuple-element.44.refs_8_), channel_id=1, source_target_pairs={{0,8},{4,12},{8,0},{12,4},{16,24},{20,28},{24,16},{28,20},{1,9},{5... | collective-permute-start | bytes 491528 | tf_op jit(solution)/shard_map/ppermute | solution.py:33
  28.7 8.9 %collective-permute-start.11 = (f32[8,40,128]{2,1,0:T(8,128)S(1)}, f32[8,40,128]{2,1,0:T(8,128)S(1)}, u32[]{:S(2)}, u32[]{:S(2)}) collective-permute-start(f32[8,40,128]{2,1,0:T(8,128)S(1)} %get-tuple-element.44.refs_8_), channel_id=1, source_target_pairs={{0,12},{4,8},{8,4},{12,0},{16,28},{20,24},{24,20},{28,16},{1,13},{... | collective-permute-start | bytes 491528 | tf_op jit(solution)/shard_map/ppermute | solution.py:33
  28.7 8.9 %collective-permute-start.8 = (f32[2,2,64,256]{3,2,1,0:T(8,128)}, f32[2,2,64,256]{3,2,1,0:T(8,128)S(1)}, u32[]{:S(2)}, u32[]{:S(2)}) collective-permute-start(f32[2,2,64,256]{3,2,1,0:T(8,128)} %collective-permute-done.6.refs_6_), channel_id=1, source_target_pairs={{0,16},{4,20},{8,24},{12,28},{16,0},{20,4},{24,8},{28,12},{1,17},{... | collective-permute-start | bytes 786440 | tf_op jit(solution)/shard_map/ppermute | solution.py:38
  36.1 8.6 %collective-permute-start.14 = (f32[8,40,128]{2,1,0:T(8,128)S(1)}, f32[8,40,128]{2,1,0:T(8,128)S(1)}, u32[]{:S(2)}, u32[]{:S(2)}) collective-permute-start(f32[8,40,128]{2,1,0:T(8,128)S(1)} %get-tuple-element.44.refs_8_), channel_id=1, source_target_pairs={{0,4},{4,0},{8,12},{12,8},{16,20},{20,16},{24,28},{28,24},{1,5},{5... | collective-permute-start | bytes 491528 | tf_op jit(solution)/shard_map/ppermute | solution.py:33
  42.8 7.5 %collective-permute-start.13 = (f32[8,32,128]{2,1,0:T(8,128)S(1)}, f32[8,32,128]{2,1,0:T(8,128)S(1)}, u32[]{:S(2)}, u32[]{:S(2)}) collective-permute-start(f32[8,32,128]{2,1,0:T(8,128)S(1)} %get-tuple-element.55), channel_id=1, source_target_pairs={{0,12},{4,8},{8,4},{12,0},{16,28},{20,24},{24,20},{28,16},{1,13},{... | collective-permute-start | bytes 393224 | tf_op jit(solution)/shard_map/ppermute | solution.py:33
  43.9 7.5 %collective-permute-start.12 = (f32[8,32,128]{2,1,0:T(8,128)S(1)}, f32[8,32,128]{2,1,0:T(8,128)S(1)}, u32[]{:S(2)}, u32[]{:S(2)}) collective-permute-start(f32[8,32,128]{2,1,0:T(8,128)S(1)} %get-tuple-element.54), channel_id=1, source_target_pairs={{0,8},{4,12},{8,0},{12,4},{16,24},{20,28},{24,16},{28,20},{1,9},{5... | collective-permute-start | bytes 393224 | tf_op jit(solution)/shard_map/ppermute | solution.py:33
  50.2 1.4 %collective-permute-start.15 = (f32[8,32,128]{2,1,0:T(8,128)S(1)}, f32[8,32,128]{2,1,0:T(8,128)S(1)}, u32[]{:S(2)}, u32[]{:S(2)}) collective-permute-start(f32[8,32,128]{2,1,0:T(8,128)S(1)} %get-tuple-element.61), channel_id=1, source_target_pairs={{0,4},{4,0},{8,12},{12,8},{16,20},{20,16},{24,28},{28,24},{1,5},{5... | collective-permute-start | bytes 393224 | tf_op jit(solution)/shard_map/ppermute | solution.py:33
where the time goes:
time: 52.6 us; the launch traced here: 52.4 us
  Pallas kernels  21.8 us (41%)
  starting transfers between devices  20.2 us (38%)
  waiting for transfers between devices  9.35 us (18%)
  local copies, waits for them, and re-layouts  0.76 us (1%)
    pallas_call x2, Pallas kernels, finish(): pl.pallas_call(lambda *refs: finish_kernel(members, group_count, len(piec...  10.5 us
    ppermute x7, starting transfers between devices, from_behind(): return lax.ppermute(x, axis, [(i, (i + by) % count) for i in range(count)])  9.17 us
    ppermute x9, starting transfers between devices, from_partner(): lax.ppermute(x, axis, [(i, i ^ flip) for i in range(lax.axis_size(axis))])  7.54 us
    pallas_call x1, Pallas kernels, project(): pl.pallas_call(lambda *refs: project_kernel(len(bases), *refs), out_shape...  6.92 us
    ppermute x7, waiting for transfers between devices, from_behind(): return lax.ppermute(x, axis, [(i, (i + by) % count) for i in range(count)])  4.9 us
    all_to_all x1, starting transfers between devices, on_device_shared(): lax.all_to_all(sent, 'blk', split_axis=0, concat_axis=0, tiled=True)  3.54 us
    all_to_all x1, waiting for transfers between devices, on_device_shared(): lax.all_to_all(sent, 'blk', split_axis=0, concat_axis=0, tiled=True)  3.14 us
    pallas_call x1, Pallas kernels, dress(): pl.pallas_call(dress_kernel, out_shape=tuple((jax.ShapeDtypeStruct((pair_...  2.32 us
  transfers between devices with their start and end apart: 17, of which 6 were waited for; matrix products, arithmetic and copies ran while one was open for 0% of the time, Pallas kernels for 42%

commit v1 on v0

--- a/solution.py
+++ b/solution.py
@@ -80,22 +80,32 @@
     own = halves(basis[...].reshape(pair_count * pno_count, orbital_count))
     others = halves(coupled[:, :pno_count].reshape(slot_count * pno_count, orbital_count))
     overlap = halves(dot3(own, others, NT))
+    step = orbital_count // pno_count
     left, slot_weight = [], []
-    for slot in range(slot_count):
-        cols = slice(slot * pno_count, (slot + 1) * pno_count)
-        packed = coupled[slot, pno_count:]
-        step = orbital_count // pno_count
-        for i in range(step):
-            lanes = slice(i * pno_count, (i + 1) * pno_count)
-            partners[slot, pl.ds(i, packed.shape[0], stride=step), :] = packed[:, lanes]
-        left.append(dot3([x[:, cols] for x in overlap], halves(partners[slot]), NN))
-        named = jnp.where(couple[...] == slot, couple_weight[...], 0.0)
-        slot_weight.append(jnp.sum(named, axis=1, keepdims=True))
+    for both in range(slot_count // 2):
+        named = []
+        for j in range(2):
+            packed = coupled[2 * both + j, pno_count:]
+            for i in range(step):
+                rows = pl.ds(j * pno_count + i, packed.shape[0], stride=step)
+                block = packed[:, i * pno_count:(i + 1) * pno_count]
+                none = jnp.zeros_like(block)
+                partners[both, rows, :] = stack([none, block] if j else [block, none], 1)
+            weight = jnp.where(couple[...] == 2 * both + j, couple_weight[...], 0.0)
+            named.append(jnp.sum(weight, axis=1, keepdims=True))
+        lane = lax.broadcasted_iota(jnp.int32, (pair_count, width), 1)
+        slot_weight.append(jnp.where(lane < pno_count, *named))
+        high, low = [x[:, both * width:(both + 1) * width] for x in overlap]
+        diagonal = halves(partners[both])
+        product = dot(high, stack(diagonal, 1), NN)
+        left.append(product[:, :width] + (product[:, width:] + dot(low, diagonal[0], NN)))
     dressed[:, half:, :] = jnp.zeros((pair_count, dressed.shape[1] - half, 2 * pno_count), jnp.float32)
     for pair in range(pair_count):
         rows = slice(pair * pno_count, (pair + 1) * pno_count)
-        scaled = stack([x[rows] * w[pair:pair + 1] for x, w in zip(left, slot_weight)], 1)
-        total = turned[pair] + dot3(halves(scaled), [x[rows] for x in overlap], NT)
+        high, low = halves(stack([x[rows] * w[pair:pair + 1] for x, w in zip(left, slot_weight)], 1))
+        right = [x[rows] for x in overlap]
+        product = dot(high, stack(right), NT)
+        total = turned[pair] + product[:, :pno_count] + (product[:, pno_count:] + dot(low, right[0], NT))
         dressed[pair, :half] = stack([total[:half], total[half:]], 1)
         turned[pair] = total
         result[pair] = two_to_one(turned, pair, half)
@@ -118,7 +128,7 @@
         scratch_shapes=[
             pltpu.VMEM((pair_count, pno_count, pno_count), jnp.float32),
             pltpu.VMEM((pair_count * pno_count // 2, 2 * pno_count), jnp.float32),
-            pltpu.VMEM((coupled.shape[0], pno_count, pno_count), jnp.float32),
+            pltpu.VMEM((coupled.shape[0] // 2, 2 * pno_count, 2 * pno_count), jnp.float32),
         ],
         compiler_params=pltpu.CompilerParams(vmem_limit_bytes=10 * 2**20),
         cost_estimate=pl.CostEstimate(flops=4 * 10**9, bytes_accessed=8 * basis.size, transcendentals=0),

time: 52.6 us -> 52.9 us (level)
  waiting for transfers between devices: 9.35 us -> 10.8 us
    ppermute x7, waiting for transfers between devices: 4.9 us -> 6.37 us  [from_behind(): return lax.ppermute(x, axis, [(i, (i + by) % count) for i in range(count)])]
    ppermute x9, starting transfers between devices: 7.54 us -> 6.95 us  [from_partner(): lax.ppermute(x, axis, [(i, i ^ flip) for i in range(lax.axis_size(axis))])]
    pallas_call x1, Pallas kernels: 2.32 us -> 1.78 us  [dress(): pl.pallas_call(dress_kernel, out_shape=tuple((jax.ShapeDtypeStruct((pair_...]
  transfers between devices with their start and end apart: 17 -> 17, of which waited for: 6 -> 7; matrix products, arithmetic and copies ran while one was open for 0% -> 0% of each run, Pallas kernels for 42% -> 40%
where the time goes in v1:
time: 52.9 us; the launch traced here: 52.6 us
  Pallas kernels  21.3 us (40%)
  starting transfers between devices  19.7 us (37%)
  waiting for transfers between devices  10.8 us (20%)
  local copies, waits for them, and re-layouts  0.76 us (1%)
    pallas_call x2, Pallas kernels, finish(): pl.pallas_call(lambda *refs: finish_kernel(members, group_count, len(piec...  10.5 us
    ppermute x7, starting transfers between devices, from_behind(): return lax.ppermute(x, axis, [(i, (i + by) % count) for i in range(count)])  9.17 us
    ppermute x9, starting transfers between devices, from_partner(): lax.ppermute(x, axis, [(i, i ^ flip) for i in range(lax.axis_size(axis))])  6.95 us
    pallas_call x1, Pallas kernels, project(): pl.pallas_call(lambda *refs: project_kernel(len(bases), *refs), out_shape...  6.92 us
    ppermute x7, waiting for transfers between devices, from_behind(): return lax.ppermute(x, axis, [(i, (i + by) % count) for i in range(count)])  6.37 us
    all_to_all x1, starting transfers between devices, on_device_shared(): lax.all_to_all(sent, 'blk', split_axis=0, concat_axis=0, tiled=True)  3.54 us
    all_to_all x1, waiting for transfers between devices, on_device_shared(): lax.all_to_all(sent, 'blk', split_axis=0, concat_axis=0, tiled=True)  3.14 us
    pallas_call x1, Pallas kernels, pack_pairs(): pl.pallas_call(pack_kernel, out_shape=jax.ShapeDtypeStruct((send_order.sh...  2.02 us
  transfers between devices with their start and end apart: 17, of which 7 were waited for; matrix products, arithmetic and copies ran while one was open for 0% of the time, Pallas kernels for 40%

profile of v1, /device:TPU:0, one launch (start us, length us, event | category | flops | bytes accessed | tf_op | source)
XLA Modules:
  0.0 52.6 jit_solution(8560078076495248247)
XLA Ops:
  0.0 0.0 copy-start.1
  0.0 3.0 %collective-permute-start.2 = (f32[8,64,256]{2,1,0:T(8,128)}, f32[8,64,256]{2,1,0:T(8,128)S(1)}, u32[]{:S(2)}, u32[]{:S(2)}) collective-permute-start(f32[8,64,256]{2,1,0:T(8,128)} %refs_2_), channel_id=1, source_target_pairs={{0,8},{4,12},{8,0},{12,4},{16,24},{20,28},{24,16},{28,20},{1,9},{5... | collective-permute-start | bytes 1572872 | tf_op jit(solution)/shard_map/ppermute | solution.py:33
  3.0 1.5 %collective-permute-start = (f32[2,2,64,256]{3,2,1,0:T(8,128)}, f32[2,2,64,256]{3,2,1,0:T(8,128)S(1)}, u32[]{:S(2)}, u32[]{:S(2)}) collective-permute-start(f32[2,2,64,256]{3,2,1,0:T(8,128)} %refs_4_.1), channel_id=1, source_target_pairs={{0,16},{4,20},{8,24},{12,28},{16,0},{20,4},{24,8},{28,12},{1,17},{... | collective-permute-start | bytes 786440 | tf_op jit(solution)/shard_map/ppermute | solution.py:38
  4.6 1.6 %collective-permute-start.3 = (f32[2,2,64,256]{3,2,1,0:T(8,128)}, f32[2,2,64,256]{3,2,1,0:T(8,128)}, u32[]{:S(2)}, u32[]{:S(2)}) collective-permute-start(f32[2,2,64,256]{3,2,1,0:T(8,128)} %refs_4_.1), channel_id=1, source_target_pairs={{0,1},{1,2},{2,3},{3,0},{4,5},{5,6},{6,7},{7,4},{8,9},{9,10},{10,1... | collective-permute-start | bytes 786440 | tf_op jit(solution)/shard_map/ppermute | solution.py:38
  6.1 2.2 %collective-permute-start.4 = (f32[2,2,64,256]{3,2,1,0:T(8,128)}, f32[2,2,64,256]{3,2,1,0:T(8,128)}, u32[]{:S(2)}, u32[]{:S(2)}) collective-permute-start(f32[2,2,64,256]{3,2,1,0:T(8,128)} %refs_4_.1), channel_id=1, source_target_pairs={{0,3},{1,0},{2,1},{3,2},{4,7},{5,4},{6,5},{7,6},{8,11},{9,8},{10,9... | collective-permute-start | bytes 786440 | tf_op jit(solution)/shard_map/ppermute | solution.py:38
  8.4 2.0 %shard_map.73 = f32[8,80,256]{2,1,0:T(8,128)} custom-call(s32[8]{0:T(128)} %bitcast.6, f32[8,64,256]{2,1,0:T(8,128)} %refs_2_, f32[8,4096]{1,0:T(8,128)} %amps.3), custom_call_target="tpu_custom_call" | custom-call | bytes 524288 | tf_op jit(solution)/shard_map/pallas_call | solution.py:59
  10.4 0.6 %collective-permute-done.refs_4_ = f32[2,2,64,256]{3,2,1,0:T(8,128)S(1)} collective-permute-done((f32[2,2,64,256]{3,2,1,0:T(8,128)}, f32[2,2,64,256]{3,2,1,0:T(8,128)S(1)}, u32[]{:S(2)}, u32[]{:S(2)}) %collective-permute-start) | collective-permute-done | bytes 262176 | tf_op jit(solution)/shard_map/ppermute | solution.py:38
  11.0 3.5 %all-to-all-start = ((f32[8,80,256]{2,1,0:T(8,128)}), f32[8,80,256]{2,1,0:T(8,128)S(1)}, u32[]{:S(2)}, u32[]{:S(2)}) async-start(f32[8,80,256]{2,1,0:T(8,128)} %shard_map.73), calls=%async_computation | async-start | bytes 1310720 | tf_op jit(solution)/shard_map/all_to_all | solution.py:362
  14.6 0.0 copy-done
  14.6 0.0 copy-start.2
  14.6 0.4 collective-permute-start.1
  15.0 0.9 %collective-permute-done.3.refs_5_ = f32[2,2,64,256]{3,2,1,0:T(8,128)} collective-permute-done((f32[2,2,64,256]{3,2,1,0:T(8,128)}, f32[2,2,64,256]{3,2,1,0:T(8,128)}, u32[]{:S(2)}, u32[]{:S(2)}) %collective-permute-start.3) | collective-permute-done | bytes 262176 | tf_op jit(solution)/shard_map/ppermute | solution.py:38
  16.0 3.3 %collective-permute-done.4.refs_7_ = f32[2,2,64,256]{3,2,1,0:T(8,128)} collective-permute-done((f32[2,2,64,256]{3,2,1,0:T(8,128)}, f32[2,2,64,256]{3,2,1,0:T(8,128)}, u32[]{:S(2)}, u32[]{:S(2)}) %collective-permute-start.4) | collective-permute-done | bytes 262176 | tf_op jit(solution)/shard_map/ppermute | solution.py:38
  19.3 0.0 collective-permute-done.2.refs_2_
  19.3 0.0 collective-permute-start.5
  19.3 2.4 %collective-permute-start.6 = (f32[2,2,64,256]{3,2,1,0:T(8,128)}, f32[2,2,64,256]{3,2,1,0:T(8,128)}, u32[]{:S(2)}, u32[]{:S(2)}) collective-permute-start(f32[2,2,64,256]{3,2,1,0:T(8,128)} %collective-permute-done.4.refs_7_), channel_id=1, source_target_pairs={{0,3},{1,0},{2,1},{3,2},{4,7},{5,4},{6,5},{7,6},{8,11},{9,8},{10,9... | collective-permute-start | bytes 786440 | tf_op jit(solution)/shard_map/ppermute | solution.py:38
  21.6 0.5 collective-permute-start.7
  22.2 0.4 collective-permute-start.9
  22.6 0.0 collective-permute-done.1.refs_1_.refs_3_
  22.6 3.1 %all-to-all-done.coupled = f32[8,80,256]{2,1,0:T(8,128)S(1)} async-done(((f32[8,80,256]{2,1,0:T(8,128)}), f32[8,80,256]{2,1,0:T(8,128)S(1)}, u32[]{:S(2)}, u32[]{:S(2)}) %all-to-all-start) | async-done | bytes 655392 | tf_op jit(solution)/shard_map/all_to_all | solution.py:362
  25.7 0.0 collective-permute-done.5.refs_3_
  25.7 0.0 copy-done.1
  25.7 0.0 copy-done.3
  25.8 0.0 copy-done.4
  25.8 0.0 copy-done.5
  25.8 1.8 %shard_map.74 = (f32[8,40,128]{2,1,0:T(8,128)S(1)}, f32[8,32,128]{2,1,0:T(8,128)S(1)}) custom-call(s32[8,8]{1,0:T(8,128)S(1)} %copy-done.3, f32[8,8]{1,0:T(8,128)S(1)} %copy-done.4, f32[8,16]{1,0:T(8,128)S(1)} %copy-done.5, f32[8,64,256]{2,1,0:T(8,128)S(1)} %copy-done, f32[8,4096]{1,0:T(8,128)S(1)} %copy-done.1, f32[8,80,256]{2,1,0:T(8,128)S(1)} %all-to-all-done.coupled), custom_call_target="tpu_custom_call" | custom-call | flops 4000000000 | bytes 1048576 | tf_op jit(solution)/shard_map/pallas_call | solution.py:121
  27.6 0.6 %collective-permute-start.10 = (f32[8,40,128]{2,1,0:T(8,128)S(1)}, f32[8,40,128]{2,1,0:T(8,128)S(1)}, u32[]{:S(2)}, u32[]{:S(2)}) collective-permute-start(f32[8,40,128]{2,1,0:T(8,128)S(1)} %get-tuple-element.44.refs_8_), channel_id=1, source_target_pairs={{0,8},{4,12},{8,0},{12,4},{16,24},{20,28},{24,16},{28,20},{1,9},{5... | collective-permute-start | bytes 491528 | tf_op jit(solution)/shard_map/ppermute | solution.py:33
  28.1 0.0 collective-permute-start.11
  28.1 0.6 %collective-permute-done.6.refs_6_ = f32[2,2,64,256]{3,2,1,0:T(8,128)} collective-permute-done((f32[2,2,64,256]{3,2,1,0:T(8,128)}, f32[2,2,64,256]{3,2,1,0:T(8,128)}, u32[]{:S(2)}, u32[]{:S(2)}) %collective-permute-start.6) | collective-permute-done | bytes 262176 | tf_op jit(solution)/shard_map/ppermute | solution.py:38
  28.7 0.5 collective-permute-start.8
  29.2 0.0 copy-done.2
  29.2 6.9 %shard_map.75 = (bf16[32,128,128]{2,1,0:T(8,128)(2,1)S(1)}, bf16[32,128,256]{2,1,0:T(8,128)(2,1)S(1)}) custom-call(f32[8,64,256]{2,1,0:T(8,128)S(1)} %copy-done, f32[8,64,256]{2,1,0:T(8,128)S(1)} %collective-permute-done.1.refs_1_.refs_3_, f32[8,64,256]{2,1,0:T(8,128)S(1)} %collective-permute-done.2.refs_2_, ...), custom_call_target="tpu_custom_call" | custom-call | flops 4026531840 | bytes 1048576 | tf_op jit(solution)/shard_map/pallas_call | solution.py:251
  36.1 0.0 collective-permute-done.7.refs_5_
  36.1 0.9 %collective-permute-start.14 = (f32[8,40,128]{2,1,0:T(8,128)S(1)}, f32[8,40,128]{2,1,0:T(8,128)S(1)}, u32[]{:S(2)}, u32[]{:S(2)}) collective-permute-start(f32[8,40,128]{2,1,0:T(8,128)S(1)} %get-tuple-element.44.refs_8_), channel_id=1, source_target_pairs={{0,4},{4,0},{8,12},{12,8},{16,20},{20,16},{24,28},{28,24},{1,5},{5... | collective-permute-start | bytes 491528 | tf_op jit(solution)/shard_map/ppermute | solution.py:33
  37.0 0.0 collective-permute-done.9.refs_7_
  37.0 0.0 collective-permute-done.10.refs_8_
  37.0 0.0 collective-permute-done.11.refs_9_
  37.0 0.9 %collective-permute-done.8.refs_6_ = f32[2,2,64,256]{3,2,1,0:T(8,128)S(1)} collective-permute-done((f32[2,2,64,256]{3,2,1,0:T(8,128)}, f32[2,2,64,256]{3,2,1,0:T(8,128)S(1)}, u32[]{:S(2)}, u32[]{:S(2)}) %collective-permute-start.8) | collective-permute-done | bytes 262176 | tf_op jit(solution)/shard_map/ppermute | solution.py:38
  38.0 5.2 %shard_map.76 = (f32[8,32,128]{2,1,0:T(8,128)S(1)}, f32[8,32,128]{2,1,0:T(8,128)S(1)}) custom-call(bf16[32,128,128]{2,1,0:T(8,128)(2,1)S(1)} %get-tuple-element.49.refs_0_, bf16[32,128,256]{2,1,0:T(8,128)(2,1)S(1)} %get-tuple-element.50.refs_1_, f32[8,64,256]{2,1,0:T(8,128)S(1)} %collective-permute-done.2.refs_2_, ...), custom_call_target="tpu_custom_call" | custom-call | flops 2214592512 | bytes 1048576 | tf_op jit(solution)/shard_map/pallas_call | solution.py:323
  43.2 0.2 collective-permute-start.13
  43.4 1.6 %collective-permute-start.12 = (f32[8,32,128]{2,1,0:T(8,128)S(1)}, f32[8,32,128]{2,1,0:T(8,128)S(1)}, u32[]{:S(2)}, u32[]{:S(2)}) collective-permute-start(f32[8,32,128]{2,1,0:T(8,128)S(1)} %get-tuple-element.54), channel_id=1, source_target_pairs={{0,8},{4,12},{8,0},{12,4},{16,24},{20,28},{24,16},{28,20},{1,9},{5... | collective-permute-start | bytes 393224 | tf_op jit(solution)/shard_map/ppermute | solution.py:33
  45.0 0.0 collective-permute-done.14.refs_9_
  45.0 5.4 %shard_map.77 = (f32[8,32,128]{2,1,0:T(8,128)S(1)}, f32[8,32,128]{2,1,0:T(8,128)S(1)}) custom-call(bf16[32,128,128]{2,1,0:T(8,128)(2,1)S(1)} %get-tuple-element.49.refs_0_, bf16[32,128,256]{2,1,0:T(8,128)(2,1)S(1)} %get-tuple-element.50.refs_1_, f32[8,64,256]{2,1,0:T(8,128)S(1)} %copy-done, f32[8,64,256]{2,1,0:T(8,128)S(1)} %collective-permute-done.1.refs_1_.refs_3_, ...), custom_call_target="tpu_custom_call" | custom-call | flops 2214592512 | bytes 1048576 | tf_op jit(solution)/shard_map/pallas_call | solution.py:323
  50.4 0.2 collective-permute-start.15
  50.6 0.0 collective-permute-done.13
  50.6 1.2 %collective-permute-done.12 = f32[8,32,128]{2,1,0:T(8,128)S(1)} collective-permute-done((f32[8,32,128]{2,1,0:T(8,128)S(1)}, f32[8,32,128]{2,1,0:T(8,128)S(1)}, u32[]{:S(2)}, u32[]{:S(2)}) %collective-permute-start.12) | collective-permute-done | bytes 131104 | tf_op jit(solution)/shard_map/ppermute | solution.py:33
  51.9 0.0 collective-permute-done.15
  51.9 0.7 %copy.10 = f32[1,8,32,128]{3,1,2,0:T(8,128)} copy(f32[1,8,32,128]{3,2,1,0:T(8,128)S(1)} %add_bitcast_fusion) | data formatting | bytes 262144
  (6 shorter events, 0.1 us)
Async XLA Ops:
  0.0 14.6 %copy-start = (f32[8,64,256]{2,1,0:T(8,128)S(1)}, f32[8,64,256]{2,1,0:T(8,128)}, u32[]{:S(2)}) copy-start(f32[8,64,256]{2,1,0:T(8,128)} %refs_2_) | copy-start | bytes 1572868
  0.0 25.7 %copy-start.1 = (f32[8,4096]{1,0:T(8,128)S(1)}, f32[8,4096]{1,0:T(8,128)}, u32[]{:S(2)}) copy-start(f32[8,4096]{1,0:T(8,128)} %amps.3) | copy-start | bytes 393220
  0.0 25.7 %copy-start.3 = (s32[8,8]{1,0:T(8,128)S(1)}, s32[8,8]{1,0:T(8,128)}, u32[]{:S(2)}) copy-start(s32[8,8]{1,0:T(8,128)} %couple.1) | copy-start | bytes 772
  0.0 25.8 %copy-start.4 = (f32[8,8]{1,0:T(8,128)S(1)}, f32[8,8]{1,0:T(8,128)}, u32[]{:S(2)}) copy-start(f32[8,8]{1,0:T(8,128)} %couple_weight.1) | copy-start | bytes 772
  0.0 25.8 %copy-start.5 = (f32[8,16]{1,0:T(8,128)S(1)}, f32[8,16]{1,0:T(8,128)}, u32[]{:S(2)}) copy-start(f32[8,16]{1,0:T(8,128)} %fit_weight.1) | copy-start | bytes 1540
  0.0 19.3 %collective-permute-start.2 = (f32[8,64,256]{2,1,0:T(8,128)}, f32[8,64,256]{2,1,0:T(8,128)S(1)}, u32[]{:S(2)}, u32[]{:S(2)}) collective-permute-start(f32[8,64,256]{2,1,0:T(8,128)} %refs_2_), channel_id=1, source_target_pairs={{0,8},{4,12},{8,0},{12,4},{16,24},{20,28},{24,16},{28,20},{1,9},{5... | collective-permute-start | bytes 1572872 | tf_op jit(solution)/shard_map/ppermute | solution.py:33
  3.0 8.0 %collective-permute-start = (f32[2,2,64,256]{3,2,1,0:T(8,128)}, f32[2,2,64,256]{3,2,1,0:T(8,128)S(1)}, u32[]{:S(2)}, u32[]{:S(2)}) collective-permute-start(f32[2,2,64,256]{3,2,1,0:T(8,128)} %refs_4_.1), channel_id=1, source_target_pairs={{0,16},{4,20},{8,24},{12,28},{16,0},{20,4},{24,8},{28,12},{1,17},{... | collective-permute-start | bytes 786440 | tf_op jit(solution)/shard_map/ppermute | solution.py:38
  4.6 11.4 %collective-permute-start.3 = (f32[2,2,64,256]{3,2,1,0:T(8,128)}, f32[2,2,64,256]{3,2,1,0:T(8,128)}, u32[]{:S(2)}, u32[]{:S(2)}) collective-permute-start(f32[2,2,64,256]{3,2,1,0:T(8,128)} %refs_4_.1), channel_id=1, source_target_pairs={{0,1},{1,2},{2,3},{3,0},{4,5},{5,6},{6,7},{7,4},{8,9},{9,10},{10,1... | collective-permute-start | bytes 786440 | tf_op jit(solution)/shard_map/ppermute | solution.py:38
  6.1 13.1 %collective-permute-start.4 = (f32[2,2,64,256]{3,2,1,0:T(8,128)}, f32[2,2,64,256]{3,2,1,0:T(8,128)}, u32[]{:S(2)}, u32[]{:S(2)}) collective-permute-start(f32[2,2,64,256]{3,2,1,0:T(8,128)} %refs_4_.1), channel_id=1, source_target_pairs={{0,3},{1,0},{2,1},{3,2},{4,7},{5,4},{6,5},{7,6},{8,11},{9,8},{10,9... | collective-permute-start | bytes 786440 | tf_op jit(solution)/shard_map/ppermute | solution.py:38
  11.0 14.7 %all-to-all-start = ((f32[8,80,256]{2,1,0:T(8,128)}), f32[8,80,256]{2,1,0:T(8,128)S(1)}, u32[]{:S(2)}, u32[]{:S(2)}) async-start(f32[8,80,256]{2,1,0:T(8,128)} %shard_map.73), calls=%async_computation | async-start | bytes 1310720 | tf_op jit(solution)/shard_map/all_to_all | solution.py:362
  14.6 14.6 %copy-start.2 = (f32[2,2,64,256]{3,2,1,0:T(8,128)S(1)}, f32[2,2,64,256]{3,2,1,0:T(8,128)}, u32[]{:S(2)}) copy-start(f32[2,2,64,256]{3,2,1,0:T(8,128)} %refs_4_.1) | copy-start | bytes 786436
  14.6 8.0 %collective-permute-start.1 = (f32[8,64,256]{2,1,0:T(8,128)S(1)}, f32[8,64,256]{2,1,0:T(8,128)S(1)}, u32[]{:S(2)}, u32[]{:S(2)}) collective-permute-start(f32[8,64,256]{2,1,0:T(8,128)S(1)} %copy-done), channel_id=1, source_target_pairs={{0,4},{4,0},{8,12},{12,8},{16,20},{20,16},{24,28},{28,24},{1,5},{5... | collective-permute-start | bytes 1572872 | tf_op jit(solution)/shard_map/ppermute | solution.py:33
  19.3 6.5 %collective-permute-start.5 = (f32[8,64,256]{2,1,0:T(8,128)S(1)}, f32[8,64,256]{2,1,0:T(8,128)S(1)}, u32[]{:S(2)}, u32[]{:S(2)}) collective-permute-start(f32[8,64,256]{2,1,0:T(8,128)S(1)} %collective-permute-done.2.refs_2_), channel_id=1, source_target_pairs={{0,4},{4,0},{8,12},{12,8},{16,20},{20,16},{24,28},{28,24},{1,5},{5... | collective-permute-start | bytes 1572872 | tf_op jit(solution)/shard_map/ppermute | solution.py:33
  19.3 9.4 %collective-permute-start.6 = (f32[2,2,64,256]{3,2,1,0:T(8,128)}, f32[2,2,64,256]{3,2,1,0:T(8,128)}, u32[]{:S(2)}, u32[]{:S(2)}) collective-permute-start(f32[2,2,64,256]{3,2,1,0:T(8,128)} %collective-permute-done.4.refs_7_), channel_id=1, source_target_pairs={{0,3},{1,0},{2,1},{3,2},{4,7},{5,4},{6,5},{7,6},{8,11},{9,8},{10,9... | collective-permute-start | bytes 786440 | tf_op jit(solution)/shard_map/ppermute | solution.py:38
  21.6 14.5 %collective-permute-start.7 = (f32[2,2,64,256]{3,2,1,0:T(8,128)}, f32[2,2,64,256]{3,2,1,0:T(8,128)}, u32[]{:S(2)}, u32[]{:S(2)}) collective-permute-start(f32[2,2,64,256]{3,2,1,0:T(8,128)} %collective-permute-done.3.refs_5_), channel_id=1, source_target_pairs={{0,16},{4,20},{8,24},{12,28},{16,0},{20,4},{24,8},{28,12},{1,17},{... | collective-permute-start | bytes 786440 | tf_op jit(solution)/shard_map/ppermute | solution.py:38
  22.2 14.9 %collective-permute-start.9 = (f32[2,2,64,256]{3,2,1,0:T(8,128)S(1)}, f32[2,2,64,256]{3,2,1,0:T(8,128)}, u32[]{:S(2)}, u32[]{:S(2)}) collective-permute-start(f32[2,2,64,256]{3,2,1,0:T(8,128)S(1)} %collective-permute-done.refs_4_), channel_id=1, source_target_pairs={{0,3},{1,0},{2,1},{3,2},{4,7},{5,4},{6,5},{7,6},{8,11},{9,8},{10,9... | collective-permute-start | bytes 786440 | tf_op jit(solution)/shard_map/ppermute | solution.py:38
  27.6 9.5 %collective-permute-start.10 = (f32[8,40,128]{2,1,0:T(8,128)S(1)}, f32[8,40,128]{2,1,0:T(8,128)S(1)}, u32[]{:S(2)}, u32[]{:S(2)}) collective-permute-start(f32[8,40,128]{2,1,0:T(8,128)S(1)} %get-tuple-element.44.refs_8_), channel_id=1, source_target_pairs={{0,8},{4,12},{8,0},{12,4},{16,24},{20,28},{24,16},{28,20},{1,9},{5... | collective-permute-start | bytes 491528 | tf_op jit(solution)/shard_map/ppermute | solution.py:33
  28.1 8.9 %collective-permute-start.11 = (f32[8,40,128]{2,1,0:T(8,128)S(1)}, f32[8,40,128]{2,1,0:T(8,128)S(1)}, u32[]{:S(2)}, u32[]{:S(2)}) collective-permute-start(f32[8,40,128]{2,1,0:T(8,128)S(1)} %get-tuple-element.44.refs_8_), channel_id=1, source_target_pairs={{0,12},{4,8},{8,4},{12,0},{16,28},{20,24},{24,20},{28,16},{1,13},{... | collective-permute-start | bytes 491528 | tf_op jit(solution)/shard_map/ppermute | solution.py:33
  28.7 9.3 %collective-permute-start.8 = (f32[2,2,64,256]{3,2,1,0:T(8,128)}, f32[2,2,64,256]{3,2,1,0:T(8,128)S(1)}, u32[]{:S(2)}, u32[]{:S(2)}) collective-permute-start(f32[2,2,64,256]{3,2,1,0:T(8,128)} %collective-permute-done.6.refs_6_), channel_id=1, source_target_pairs={{0,16},{4,20},{8,24},{12,28},{16,0},{20,4},{24,8},{28,12},{1,17},{... | collective-permute-start | bytes 786440 | tf_op jit(solution)/shard_map/ppermute | solution.py:38
  36.1 8.8 %collective-permute-start.14 = (f32[8,40,128]{2,1,0:T(8,128)S(1)}, f32[8,40,128]{2,1,0:T(8,128)S(1)}, u32[]{:S(2)}, u32[]{:S(2)}) collective-permute-start(f32[8,40,128]{2,1,0:T(8,128)S(1)} %get-tuple-element.44.refs_8_), channel_id=1, source_target_pairs={{0,4},{4,0},{8,12},{12,8},{16,20},{20,16},{24,28},{28,24},{1,5},{5... | collective-permute-start | bytes 491528 | tf_op jit(solution)/shard_map/ppermute | solution.py:33
  43.2 7.4 %collective-permute-start.13 = (f32[8,32,128]{2,1,0:T(8,128)S(1)}, f32[8,32,128]{2,1,0:T(8,128)S(1)}, u32[]{:S(2)}, u32[]{:S(2)}) collective-permute-start(f32[8,32,128]{2,1,0:T(8,128)S(1)} %get-tuple-element.55), channel_id=1, source_target_pairs={{0,12},{4,8},{8,4},{12,0},{16,28},{20,24},{24,20},{28,16},{1,13},{... | collective-permute-start | bytes 393224 | tf_op jit(solution)/shard_map/ppermute | solution.py:33
  43.4 8.5 %collective-permute-start.12 = (f32[8,32,128]{2,1,0:T(8,128)S(1)}, f32[8,32,128]{2,1,0:T(8,128)S(1)}, u32[]{:S(2)}, u32[]{:S(2)}) collective-permute-start(f32[8,32,128]{2,1,0:T(8,128)S(1)} %get-tuple-element.54), channel_id=1, source_target_pairs={{0,8},{4,12},{8,0},{12,4},{16,24},{20,28},{24,16},{28,20},{1,9},{5... | collective-permute-start | bytes 393224 | tf_op jit(solution)/shard_map/ppermute | solution.py:33
  50.4 1.5 %collective-permute-start.15 = (f32[8,32,128]{2,1,0:T(8,128)S(1)}, f32[8,32,128]{2,1,0:T(8,128)S(1)}, u32[]{:S(2)}, u32[]{:S(2)}) collective-permute-start(f32[8,32,128]{2,1,0:T(8,128)S(1)} %get-tuple-element.61), channel_id=1, source_target_pairs={{0,4},{4,0},{8,12},{12,8},{16,20},{20,16},{24,28},{28,24},{1,5},{5... | collective-permute-start | bytes 393224 | tf_op jit(solution)/shard_map/ppermute | solution.py:33

commit v2 on v1

--- a/solution.py
+++ b/solution.py
@@ -175,13 +175,16 @@
         wide[:, :, i * orbital_count:(i + 1) * orbital_count] = x
 
 
-def project_slice(wide, block, projected, at):
+def project_slice(wide, block, projected, at, together=4):
     pair_count, pno_count, lane_count = wide.shape
     orbital_count = block.shape[1]
-    basis = wide[...].reshape(pair_count * pno_count, lane_count)
-    product = halves(dot(basis, block[...], NN).reshape(pair_count, pno_count, orbital_count))
-    for i in range(2):
-        projected[:, at:at + pno_count, i * orbital_count:(i + 1) * orbital_count] = product[i]
+    for first in range(0, pair_count, together):
+        span = slice(first, min(first + together, pair_count))
+        basis = wide[span]
+        shape = (basis.shape[0], pno_count, orbital_count)
+        product = halves(dot(basis.reshape(shape[0] * pno_count, lane_count), block[...], NN).reshape(shape))
+        for i in range(2):
+            projected[span, at:at + pno_count, i * orbital_count:(i + 1) * orbital_count] = product[i]
 
 
 def inner_pair(wide, projected, inner_left, inner_right, pair, here):
@@ -297,15 +300,15 @@
         square[at, :pno_count] = jnp.where(left_lanes(low), high, low).astype(jnp.bfloat16)
         square[at, pno_count:] = jnp.where(left_lanes(low), high, 0.0).astype(jnp.bfloat16)
     for at, (index, pair) in enumerate(pairs):
-        for group in range(group_count):
-            product = fold(dot(groups[2 * group][row_of(group, at)], square[at], NN))
-            for b in range(block_count):
-                weight = weights[(index * group_count + group) * block_count + b][pair]
-                lanes = slice(b * lane_count, (b + 1) * lane_count)
-                moved[at, group, :, lanes] = high_low(product[b * pno_count:(b + 1) * pno_count] * weight)
+        lefts = [groups[2 * group][row_of(group, at)] for group in range(group_count)]
+        product = fold(dot(stack(lefts), square[at], NN))
+        for term in range(group_count * block_count):
+            weight = weights[index * group_count * block_count + term][pair]
+            rows, lanes = (slice(term * size, (term + 1) * size) for size in (pno_count, lane_count))
+            moved[at, :, lanes] = high_low(product[rows] * weight)
     for at, (index, pair) in enumerate(pairs):
-        terms = [dot(moved[at, group], groups[2 * group + 1][row_of(group, at)], NT) for group in range(group_count)]
-        total[at] = fold(sum(terms[1:], terms[0]))
+        rights = [groups[2 * group + 1][row_of(group, at)] for group in range(group_count)]
+        total[at] = fold(dot(moved[at], stack(rights, 1), NT))
     for at, (index, pair) in enumerate(pairs):
         rows = [total[at, pl.ds(i, half, stride=2), :] for i in range(2)]
         after[index][pair] = jnp.where(left_lanes(rows[0]), *rows)
@@ -328,7 +331,7 @@
         scratch_shapes=[
             *[pltpu.VMEM(*x) for x in shapes],
             pltpu.VMEM((pairs, lane_count, lane_count), jnp.bfloat16),
-            pltpu.VMEM((pairs, group_count + 1, pno_count, block_count * lane_count), jnp.bfloat16),
+            pltpu.VMEM((pairs, pno_count, (group_count + 1) * block_count * lane_count), jnp.bfloat16),
             pltpu.VMEM((pairs, pno_count, lane_count), jnp.float32),
             *project_scratch(bases, pieces),
         ],

time: 52.9 us -> 53 us (level)
  transfers between devices with their start and end apart: 17 -> 17, of which waited for: 7 -> 7; matrix products, arithmetic and copies ran while one was open for 0% -> 0% of each run, Pallas kernels for 40% -> 41%
where the time goes in v2:
time: 53 us; the launch traced here: 52.8 us
  Pallas kernels  21.6 us (41%)
  starting transfers between devices  19.7 us (37%)
  waiting for transfers between devices  10.6 us (20%)
  local copies, waits for them, and re-layouts  0.76 us (1%)
    pallas_call x2, Pallas kernels, finish(): pl.pallas_call(lambda *refs: finish_kernel(members, group_count, len(piec...  10.7 us
    ppermute x7, starting transfers between devices, from_behind(): return lax.ppermute(x, axis, [(i, (i + by) % count) for i in range(count)])  9.17 us
    pallas_call x1, Pallas kernels, project(): pl.pallas_call(lambda *refs: project_kernel(len(bases), *refs), out_shape...  7.01 us
    ppermute x9, starting transfers between devices, from_partner(): lax.ppermute(x, axis, [(i, i ^ flip) for i in range(lax.axis_size(axis))])  6.94 us
    ppermute x7, waiting for transfers between devices, from_behind(): return lax.ppermute(x, axis, [(i, (i + by) % count) for i in range(count)])  6.28 us
    all_to_all x1, starting transfers between devices, on_device_shared(): lax.all_to_all(sent, 'blk', split_axis=0, concat_axis=0, tiled=True)  3.54 us
    all_to_all x1, waiting for transfers between devices, on_device_shared(): lax.all_to_all(sent, 'blk', split_axis=0, concat_axis=0, tiled=True)  3.14 us
    pallas_call x1, Pallas kernels, pack_pairs(): pl.pallas_call(pack_kernel, out_shape=jax.ShapeDtypeStruct((send_order.sh...  2.02 us
  transfers between devices with their start and end apart: 17, of which 7 were waited for; matrix products, arithmetic and copies ran while one was open for 0% of the time, Pallas kernels for 41%

profile of v2, /device:TPU:0, one launch (start us, length us, event | category | flops | bytes accessed | tf_op | source)
XLA Modules:
  0.0 52.8 jit_solution(16971060636072804981)
XLA Ops:
  0.0 0.0 copy-start
  0.0 3.0 %collective-permute-start.2 = (f32[8,64,256]{2,1,0:T(8,128)}, f32[8,64,256]{2,1,0:T(8,128)S(1)}, u32[]{:S(2)}, u32[]{:S(2)}) collective-permute-start(f32[8,64,256]{2,1,0:T(8,128)} %refs_2_), channel_id=1, source_target_pairs={{0,8},{4,12},{8,0},{12,4},{16,24},{20,28},{24,16},{28,20},{1,9},{5... | collective-permute-start | bytes 1572872 | tf_op jit(solution)/shard_map/ppermute | solution.py:33
  3.0 1.5 %collective-permute-start = (f32[2,2,64,256]{3,2,1,0:T(8,128)}, f32[2,2,64,256]{3,2,1,0:T(8,128)S(1)}, u32[]{:S(2)}, u32[]{:S(2)}) collective-permute-start(f32[2,2,64,256]{3,2,1,0:T(8,128)} %refs_4_.1), channel_id=1, source_target_pairs={{0,16},{4,20},{8,24},{12,28},{16,0},{20,4},{24,8},{28,12},{1,17},{... | collective-permute-start | bytes 786440 | tf_op jit(solution)/shard_map/ppermute | solution.py:38
  4.6 1.6 %collective-permute-start.3 = (f32[2,2,64,256]{3,2,1,0:T(8,128)}, f32[2,2,64,256]{3,2,1,0:T(8,128)}, u32[]{:S(2)}, u32[]{:S(2)}) collective-permute-start(f32[2,2,64,256]{3,2,1,0:T(8,128)} %refs_4_.1), channel_id=1, source_target_pairs={{0,1},{1,2},{2,3},{3,0},{4,5},{5,6},{6,7},{7,4},{8,9},{9,10},{10,1... | collective-permute-start | bytes 786440 | tf_op jit(solution)/shard_map/ppermute | solution.py:38
  6.1 2.2 %collective-permute-start.4 = (f32[2,2,64,256]{3,2,1,0:T(8,128)}, f32[2,2,64,256]{3,2,1,0:T(8,128)}, u32[]{:S(2)}, u32[]{:S(2)}) collective-permute-start(f32[2,2,64,256]{3,2,1,0:T(8,128)} %refs_4_.1), channel_id=1, source_target_pairs={{0,3},{1,0},{2,1},{3,2},{4,7},{5,4},{6,5},{7,6},{8,11},{9,8},{10,9... | collective-permute-start | bytes 786440 | tf_op jit(solution)/shard_map/ppermute | solution.py:38
  8.4 2.0 %shard_map.73 = f32[8,80,256]{2,1,0:T(8,128)} custom-call(s32[8]{0:T(128)} %bitcast.6, f32[8,64,256]{2,1,0:T(8,128)} %refs_2_, f32[8,4096]{1,0:T(8,128)} %amps.3), custom_call_target="tpu_custom_call" | custom-call | bytes 524288 | tf_op jit(solution)/shard_map/pallas_call | solution.py:59
  10.4 0.6 %collective-permute-done.refs_4_ = f32[2,2,64,256]{3,2,1,0:T(8,128)S(1)} collective-permute-done((f32[2,2,64,256]{3,2,1,0:T(8,128)}, f32[2,2,64,256]{3,2,1,0:T(8,128)S(1)}, u32[]{:S(2)}, u32[]{:S(2)}) %collective-permute-start) | collective-permute-done | bytes 262176 | tf_op jit(solution)/shard_map/ppermute | solution.py:38
  11.0 3.5 %all-to-all-start = ((f32[8,80,256]{2,1,0:T(8,128)}), f32[8,80,256]{2,1,0:T(8,128)S(1)}, u32[]{:S(2)}, u32[]{:S(2)}) async-start(f32[8,80,256]{2,1,0:T(8,128)} %shard_map.73), calls=%async_computation | async-start | bytes 1310720 | tf_op jit(solution)/shard_map/all_to_all | solution.py:365
  14.6 0.0 copy-done
  14.6 0.0 copy-start.2
  14.6 0.4 collective-permute-start.1
  15.0 0.9 %collective-permute-done.3.refs_5_ = f32[2,2,64,256]{3,2,1,0:T(8,128)} collective-permute-done((f32[2,2,64,256]{3,2,1,0:T(8,128)}, f32[2,2,64,256]{3,2,1,0:T(8,128)}, u32[]{:S(2)}, u32[]{:S(2)}) %collective-permute-start.3) | collective-permute-done | bytes 262176 | tf_op jit(solution)/shard_map/ppermute | solution.py:38
  16.0 3.3 %collective-permute-done.4.refs_7_ = f32[2,2,64,256]{3,2,1,0:T(8,128)} collective-permute-done((f32[2,2,64,256]{3,2,1,0:T(8,128)}, f32[2,2,64,256]{3,2,1,0:T(8,128)}, u32[]{:S(2)}, u32[]{:S(2)}) %collective-permute-start.4) | collective-permute-done | bytes 262176 | tf_op jit(solution)/shard_map/ppermute | solution.py:38
  19.3 0.0 collective-permute-done.2.refs_2_
  19.3 0.0 collective-permute-start.5
  19.3 2.4 %collective-permute-start.6 = (f32[2,2,64,256]{3,2,1,0:T(8,128)}, f32[2,2,64,256]{3,2,1,0:T(8,128)}, u32[]{:S(2)}, u32[]{:S(2)}) collective-permute-start(f32[2,2,64,256]{3,2,1,0:T(8,128)} %collective-permute-done.4.refs_7_), channel_id=1, source_target_pairs={{0,3},{1,0},{2,1},{3,2},{4,7},{5,4},{6,5},{7,6},{8,11},{9,8},{10,9... | collective-permute-start | bytes 786440 | tf_op jit(solution)/shard_map/ppermute | solution.py:38
  21.6 0.5 collective-permute-start.7
  22.2 0.4 collective-permute-start.9
  22.6 0.0 collective-permute-done.1.refs_1_.refs_3_
  22.6 3.1 %all-to-all-done.coupled = f32[8,80,256]{2,1,0:T(8,128)S(1)} async-done(((f32[8,80,256]{2,1,0:T(8,128)}), f32[8,80,256]{2,1,0:T(8,128)S(1)}, u32[]{:S(2)}, u32[]{:S(2)}) %all-to-all-start) | async-done | bytes 655392 | tf_op jit(solution)/shard_map/all_to_all | solution.py:365
  25.7 0.0 collective-permute-done.5.refs_3_
  25.7 0.0 copy-done.1
  25.7 0.0 copy-done.3
  25.8 0.0 copy-done.4
  25.8 0.0 copy-done.5
  25.8 1.8 %shard_map.74 = (f32[8,40,128]{2,1,0:T(8,128)S(1)}, f32[8,32,128]{2,1,0:T(8,128)S(1)}) custom-call(s32[8,8]{1,0:T(8,128)S(1)} %copy-done.3, f32[8,8]{1,0:T(8,128)S(1)} %copy-done.4, f32[8,16]{1,0:T(8,128)S(1)} %copy-done.5, f32[8,64,256]{2,1,0:T(8,128)S(1)} %copy-done, f32[8,4096]{1,0:T(8,128)S(1)} %copy-done.1, f32[8,80,256]{2,1,0:T(8,128)S(1)} %all-to-all-done.coupled), custom_call_target="tpu_custom_call" | custom-call | flops 4000000000 | bytes 1048576 | tf_op jit(solution)/shard_map/pallas_call | solution.py:121
  27.6 0.6 %collective-permute-start.10 = (f32[8,40,128]{2,1,0:T(8,128)S(1)}, f32[8,40,128]{2,1,0:T(8,128)S(1)}, u32[]{:S(2)}, u32[]{:S(2)}) collective-permute-start(f32[8,40,128]{2,1,0:T(8,128)S(1)} %get-tuple-element.44.refs_8_), channel_id=1, source_target_pairs={{0,8},{4,12},{8,0},{12,4},{16,24},{20,28},{24,16},{28,20},{1,9},{5... | collective-permute-start | bytes 491528 | tf_op jit(solution)/shard_map/ppermute | solution.py:33
  28.1 0.0 collective-permute-start.11
  28.1 0.6 %collective-permute-done.6.refs_6_ = f32[2,2,64,256]{3,2,1,0:T(8,128)} collective-permute-done((f32[2,2,64,256]{3,2,1,0:T(8,128)}, f32[2,2,64,256]{3,2,1,0:T(8,128)}, u32[]{:S(2)}, u32[]{:S(2)}) %collective-permute-start.6) | collective-permute-done | bytes 262176 | tf_op jit(solution)/shard_map/ppermute | solution.py:38
  28.7 0.5 collective-permute-start.8
  29.2 0.0 copy-done.2
  29.2 7.0 %shard_map.75 = (bf16[32,128,128]{2,1,0:T(8,128)(2,1)S(1)}, bf16[32,128,256]{2,1,0:T(8,128)(2,1)S(1)}) custom-call(f32[8,64,256]{2,1,0:T(8,128)S(1)} %copy-done, f32[8,64,256]{2,1,0:T(8,128)S(1)} %collective-permute-done.1.refs_1_.refs_3_, f32[8,64,256]{2,1,0:T(8,128)S(1)} %collective-permute-done.2.refs_2_, ...), custom_call_target="tpu_custom_call" | custom-call | flops 4026531840 | bytes 1048576 | tf_op jit(solution)/shard_map/pallas_call | solution.py:254
  36.2 0.0 collective-permute-done.7.refs_5_
  36.2 0.9 %collective-permute-start.14 = (f32[8,40,128]{2,1,0:T(8,128)S(1)}, f32[8,40,128]{2,1,0:T(8,128)S(1)}, u32[]{:S(2)}, u32[]{:S(2)}) collective-permute-start(f32[8,40,128]{2,1,0:T(8,128)S(1)} %get-tuple-element.44.refs_8_), channel_id=1, source_target_pairs={{0,4},{4,0},{8,12},{12,8},{16,20},{20,16},{24,28},{28,24},{1,5},{5... | collective-permute-start | bytes 491528 | tf_op jit(solution)/shard_map/ppermute | solution.py:33
  37.1 0.0 collective-permute-done.9.refs_7_
  37.1 0.0 collective-permute-done.10.refs_8_
  37.1 0.0 collective-permute-done.11.refs_9_
  37.1 0.8 %collective-permute-done.8.refs_6_ = f32[2,2,64,256]{3,2,1,0:T(8,128)S(1)} collective-permute-done((f32[2,2,64,256]{3,2,1,0:T(8,128)}, f32[2,2,64,256]{3,2,1,0:T(8,128)S(1)}, u32[]{:S(2)}, u32[]{:S(2)}) %collective-permute-start.8) | collective-permute-done | bytes 262176 | tf_op jit(solution)/shard_map/ppermute | solution.py:38
  38.0 5.3 %shard_map.76 = (f32[8,32,128]{2,1,0:T(8,128)S(1)}, f32[8,32,128]{2,1,0:T(8,128)S(1)}) custom-call(bf16[32,128,128]{2,1,0:T(8,128)(2,1)S(1)} %get-tuple-element.49.refs_0_, bf16[32,128,256]{2,1,0:T(8,128)(2,1)S(1)} %get-tuple-element.50.refs_1_, f32[8,64,256]{2,1,0:T(8,128)S(1)} %collective-permute-done.2.refs_2_, ...), custom_call_target="tpu_custom_call" | custom-call | flops 2214592512 | bytes 1048576 | tf_op jit(solution)/shard_map/pallas_call | solution.py:326
  43.3 0.2 collective-permute-start.13
  43.5 1.6 %collective-permute-start.12 = (f32[8,32,128]{2,1,0:T(8,128)S(1)}, f32[8,32,128]{2,1,0:T(8,128)S(1)}, u32[]{:S(2)}, u32[]{:S(2)}) collective-permute-start(f32[8,32,128]{2,1,0:T(8,128)S(1)} %get-tuple-element.54), channel_id=1, source_target_pairs={{0,8},{4,12},{8,0},{12,4},{16,24},{20,28},{24,16},{28,20},{1,9},{5... | collective-permute-start | bytes 393224 | tf_op jit(solution)/shard_map/ppermute | solution.py:33
  45.1 0.0 collective-permute-done.14.refs_9_
  45.1 5.5 %shard_map.77 = (f32[8,32,128]{2,1,0:T(8,128)S(1)}, f32[8,32,128]{2,1,0:T(8,128)S(1)}) custom-call(bf16[32,128,128]{2,1,0:T(8,128)(2,1)S(1)} %get-tuple-element.49.refs_0_, bf16[32,128,256]{2,1,0:T(8,128)(2,1)S(1)} %get-tuple-element.50.refs_1_, f32[8,64,256]{2,1,0:T(8,128)S(1)} %copy-done, f32[8,64,256]{2,1,0:T(8,128)S(1)} %collective-permute-done.1.refs_1_.refs_3_, ...), custom_call_target="tpu_custom_call" | custom-call | flops 2214592512 | bytes 1048576 | tf_op jit(solution)/shard_map/pallas_call | solution.py:326
  50.6 0.2 collective-permute-start.15
  50.8 0.0 collective-permute-done.13
  50.8 1.2 %collective-permute-done.12 = f32[8,32,128]{2,1,0:T(8,128)S(1)} collective-permute-done((f32[8,32,128]{2,1,0:T(8,128)S(1)}, f32[8,32,128]{2,1,0:T(8,128)S(1)}, u32[]{:S(2)}, u32[]{:S(2)}) %collective-permute-start.12) | collective-permute-done | bytes 131104 | tf_op jit(solution)/shard_map/ppermute | solution.py:33
  52.0 0.0 collective-permute-done.15
  52.0 0.7 %copy.10 = f32[1,8,32,128]{3,1,2,0:T(8,128)} copy(f32[1,8,32,128]{3,2,1,0:T(8,128)S(1)} %add_bitcast_fusion) | data formatting | bytes 262144
  (6 shorter events, 0.1 us)
Async XLA Ops:
  0.0 14.6 %copy-start = (f32[8,64,256]{2,1,0:T(8,128)S(1)}, f32[8,64,256]{2,1,0:T(8,128)}, u32[]{:S(2)}) copy-start(f32[8,64,256]{2,1,0:T(8,128)} %refs_2_) | copy-start | bytes 1572868
  0.0 25.7 %copy-start.1 = (f32[8,4096]{1,0:T(8,128)S(1)}, f32[8,4096]{1,0:T(8,128)}, u32[]{:S(2)}) copy-start(f32[8,4096]{1,0:T(8,128)} %amps.3) | copy-start | bytes 393220
  0.0 25.7 %copy-start.3 = (s32[8,8]{1,0:T(8,128)S(1)}, s32[8,8]{1,0:T(8,128)}, u32[]{:S(2)}) copy-start(s32[8,8]{1,0:T(8,128)} %couple.1) | copy-start | bytes 772
  0.0 25.8 %copy-start.4 = (f32[8,8]{1,0:T(8,128)S(1)}, f32[8,8]{1,0:T(8,128)}, u32[]{:S(2)}) copy-start(f32[8,8]{1,0:T(8,128)} %couple_weight.1) | copy-start | bytes 772
  0.0 25.8 %copy-start.5 = (f32[8,16]{1,0:T(8,128)S(1)}, f32[8,16]{1,0:T(8,128)}, u32[]{:S(2)}) copy-start(f32[8,16]{1,0:T(8,128)} %fit_weight.1) | copy-start | bytes 1540
  0.0 19.3 %collective-permute-start.2 = (f32[8,64,256]{2,1,0:T(8,128)}, f32[8,64,256]{2,1,0:T(8,128)S(1)}, u32[]{:S(2)}, u32[]{:S(2)}) collective-permute-start(f32[8,64,256]{2,1,0:T(8,128)} %refs_2_), channel_id=1, source_target_pairs={{0,8},{4,12},{8,0},{12,4},{16,24},{20,28},{24,16},{28,20},{1,9},{5... | collective-permute-start | bytes 1572872 | tf_op jit(solution)/shard_map/ppermute | solution.py:33
  3.0 8.0 %collective-permute-start = (f32[2,2,64,256]{3,2,1,0:T(8,128)}, f32[2,2,64,256]{3,2,1,0:T(8,128)S(1)}, u32[]{:S(2)}, u32[]{:S(2)}) collective-permute-start(f32[2,2,64,256]{3,2,1,0:T(8,128)} %refs_4_.1), channel_id=1, source_target_pairs={{0,16},{4,20},{8,24},{12,28},{16,0},{20,4},{24,8},{28,12},{1,17},{... | collective-permute-start | bytes 786440 | tf_op jit(solution)/shard_map/ppermute | solution.py:38
  4.6 11.4 %collective-permute-start.3 = (f32[2,2,64,256]{3,2,1,0:T(8,128)}, f32[2,2,64,256]{3,2,1,0:T(8,128)}, u32[]{:S(2)}, u32[]{:S(2)}) collective-permute-start(f32[2,2,64,256]{3,2,1,0:T(8,128)} %refs_4_.1), channel_id=1, source_target_pairs={{0,1},{1,2},{2,3},{3,0},{4,5},{5,6},{6,7},{7,4},{8,9},{9,10},{10,1... | collective-permute-start | bytes 786440 | tf_op jit(solution)/shard_map/ppermute | solution.py:38
  6.1 13.1 %collective-permute-start.4 = (f32[2,2,64,256]{3,2,1,0:T(8,128)}, f32[2,2,64,256]{3,2,1,0:T(8,128)}, u32[]{:S(2)}, u32[]{:S(2)}) collective-permute-start(f32[2,2,64,256]{3,2,1,0:T(8,128)} %refs_4_.1), channel_id=1, source_target_pairs={{0,3},{1,0},{2,1},{3,2},{4,7},{5,4},{6,5},{7,6},{8,11},{9,8},{10,9... | collective-permute-start | bytes 786440 | tf_op jit(solution)/shard_map/ppermute | solution.py:38
  11.0 14.7 %all-to-all-start = ((f32[8,80,256]{2,1,0:T(8,128)}), f32[8,80,256]{2,1,0:T(8,128)S(1)}, u32[]{:S(2)}, u32[]{:S(2)}) async-start(f32[8,80,256]{2,1,0:T(8,128)} %shard_map.73), calls=%async_computation | async-start | bytes 1310720 | tf_op jit(solution)/shard_map/all_to_all | solution.py:365
  14.6 14.6 %copy-start.2 = (f32[2,2,64,256]{3,2,1,0:T(8,128)S(1)}, f32[2,2,64,256]{3,2,1,0:T(8,128)}, u32[]{:S(2)}) copy-start(f32[2,2,64,256]{3,2,1,0:T(8,128)} %refs_4_.1) | copy-start | bytes 786436
  14.6 8.0 %collective-permute-start.1 = (f32[8,64,256]{2,1,0:T(8,128)S(1)}, f32[8,64,256]{2,1,0:T(8,128)S(1)}, u32[]{:S(2)}, u32[]{:S(2)}) collective-permute-start(f32[8,64,256]{2,1,0:T(8,128)S(1)} %copy-done), channel_id=1, source_target_pairs={{0,4},{4,0},{8,12},{12,8},{16,20},{20,16},{24,28},{28,24},{1,5},{5... | collective-permute-start | bytes 1572872 | tf_op jit(solution)/shard_map/ppermute | solution.py:33
  19.3 6.5 %collective-permute-start.5 = (f32[8,64,256]{2,1,0:T(8,128)S(1)}, f32[8,64,256]{2,1,0:T(8,128)S(1)}, u32[]{:S(2)}, u32[]{:S(2)}) collective-permute-start(f32[8,64,256]{2,1,0:T(8,128)S(1)} %collective-permute-done.2.refs_2_), channel_id=1, source_target_pairs={{0,4},{4,0},{8,12},{12,8},{16,20},{20,16},{24,28},{28,24},{1,5},{5... | collective-permute-start | bytes 1572872 | tf_op jit(solution)/shard_map/ppermute | solution.py:33
  19.3 9.4 %collective-permute-start.6 = (f32[2,2,64,256]{3,2,1,0:T(8,128)}, f32[2,2,64,256]{3,2,1,0:T(8,128)}, u32[]{:S(2)}, u32[]{:S(2)}) collective-permute-start(f32[2,2,64,256]{3,2,1,0:T(8,128)} %collective-permute-done.4.refs_7_), channel_id=1, source_target_pairs={{0,3},{1,0},{2,1},{3,2},{4,7},{5,4},{6,5},{7,6},{8,11},{9,8},{10,9... | collective-permute-start | bytes 786440 | tf_op jit(solution)/shard_map/ppermute | solution.py:38
  21.6 14.6 %collective-permute-start.7 = (f32[2,2,64,256]{3,2,1,0:T(8,128)}, f32[2,2,64,256]{3,2,1,0:T(8,128)}, u32[]{:S(2)}, u32[]{:S(2)}) collective-permute-start(f32[2,2,64,256]{3,2,1,0:T(8,128)} %collective-permute-done.3.refs_5_), channel_id=1, source_target_pairs={{0,16},{4,20},{8,24},{12,28},{16,0},{20,4},{24,8},{28,12},{1,17},{... | collective-permute-start | bytes 786440 | tf_op jit(solution)/shard_map/ppermute | solution.py:38
  22.2 15.0 %collective-permute-start.9 = (f32[2,2,64,256]{3,2,1,0:T(8,128)S(1)}, f32[2,2,64,256]{3,2,1,0:T(8,128)}, u32[]{:S(2)}, u32[]{:S(2)}) collective-permute-start(f32[2,2,64,256]{3,2,1,0:T(8,128)S(1)} %collective-permute-done.refs_4_), channel_id=1, source_target_pairs={{0,3},{1,0},{2,1},{3,2},{4,7},{5,4},{6,5},{7,6},{8,11},{9,8},{10,9... | collective-permute-start | bytes 786440 | tf_op jit(solution)/shard_map/ppermute | solution.py:38
  27.6 9.6 %collective-permute-start.10 = (f32[8,40,128]{2,1,0:T(8,128)S(1)}, f32[8,40,128]{2,1,0:T(8,128)S(1)}, u32[]{:S(2)}, u32[]{:S(2)}) collective-permute-start(f32[8,40,128]{2,1,0:T(8,128)S(1)} %get-tuple-element.44.refs_8_), channel_id=1, source_target_pairs={{0,8},{4,12},{8,0},{12,4},{16,24},{20,28},{24,16},{28,20},{1,9},{5... | collective-permute-start | bytes 491528 | tf_op jit(solution)/shard_map/ppermute | solution.py:33
  28.1 9.0 %collective-permute-start.11 = (f32[8,40,128]{2,1,0:T(8,128)S(1)}, f32[8,40,128]{2,1,0:T(8,128)S(1)}, u32[]{:S(2)}, u32[]{:S(2)}) collective-permute-start(f32[8,40,128]{2,1,0:T(8,128)S(1)} %get-tuple-element.44.refs_8_), channel_id=1, source_target_pairs={{0,12},{4,8},{8,4},{12,0},{16,28},{20,24},{24,20},{28,16},{1,13},{... | collective-permute-start | bytes 491528 | tf_op jit(solution)/shard_map/ppermute | solution.py:33
  28.7 9.3 %collective-permute-start.8 = (f32[2,2,64,256]{3,2,1,0:T(8,128)}, f32[2,2,64,256]{3,2,1,0:T(8,128)S(1)}, u32[]{:S(2)}, u32[]{:S(2)}) collective-permute-start(f32[2,2,64,256]{3,2,1,0:T(8,128)} %collective-permute-done.6.refs_6_), channel_id=1, source_target_pairs={{0,16},{4,20},{8,24},{12,28},{16,0},{20,4},{24,8},{28,12},{1,17},{... | collective-permute-start | bytes 786440 | tf_op jit(solution)/shard_map/ppermute | solution.py:38
  36.2 8.8 %collective-permute-start.14 = (f32[8,40,128]{2,1,0:T(8,128)S(1)}, f32[8,40,128]{2,1,0:T(8,128)S(1)}, u32[]{:S(2)}, u32[]{:S(2)}) collective-permute-start(f32[8,40,128]{2,1,0:T(8,128)S(1)} %get-tuple-element.44.refs_8_), channel_id=1, source_target_pairs={{0,4},{4,0},{8,12},{12,8},{16,20},{20,16},{24,28},{28,24},{1,5},{5... | collective-permute-start | bytes 491528 | tf_op jit(solution)/shard_map/ppermute | solution.py:33
  43.3 7.5 %collective-permute-start.13 = (f32[8,32,128]{2,1,0:T(8,128)S(1)}, f32[8,32,128]{2,1,0:T(8,128)S(1)}, u32[]{:S(2)}, u32[]{:S(2)}) collective-permute-start(f32[8,32,128]{2,1,0:T(8,128)S(1)} %get-tuple-element.55), channel_id=1, source_target_pairs={{0,12},{4,8},{8,4},{12,0},{16,28},{20,24},{24,20},{28,16},{1,13},{... | collective-permute-start | bytes 393224 | tf_op jit(solution)/shard_map/ppermute | solution.py:33
  43.5 8.5 %collective-permute-start.12 = (f32[8,32,128]{2,1,0:T(8,128)S(1)}, f32[8,32,128]{2,1,0:T(8,128)S(1)}, u32[]{:S(2)}, u32[]{:S(2)}) collective-permute-start(f32[8,32,128]{2,1,0:T(8,128)S(1)} %get-tuple-element.54), channel_id=1, source_target_pairs={{0,8},{4,12},{8,0},{12,4},{16,24},{20,28},{24,16},{28,20},{1,9},{5... | collective-permute-start | bytes 393224 | tf_op jit(solution)/shard_map/ppermute | solution.py:33
  50.6 1.4 %collective-permute-start.15 = (f32[8,32,128]{2,1,0:T(8,128)S(1)}, f32[8,32,128]{2,1,0:T(8,128)S(1)}, u32[]{:S(2)}, u32[]{:S(2)}) collective-permute-start(f32[8,32,128]{2,1,0:T(8,128)S(1)} %get-tuple-element.61), channel_id=1, source_target_pairs={{0,4},{4,0},{8,12},{12,8},{16,20},{20,16},{24,28},{28,24},{1,5},{5... | collective-permute-start | bytes 393224 | tf_op jit(solution)/shard_map/ppermute | solution.py:33

commit v3 on v1

--- a/solution.py
+++ b/solution.py
@@ -376,7 +376,7 @@
     inner = [project(bases, group) for group in groups[:-1]]
     final = groups[-1]
     dressed = [own, *[from_partner(own, "blk", flip) for flip in range(1, SET)]]
-    for members in ((2, 3), (0, 1)):
+    for members in ((3,), (2,), (0, 1)):
         partial = finish(
             members, inner, [bases[member] for member in members], final, [dressed[member] for member in members]
         )

time: 52.9 us -> 51.3 us (0.970)
  Pallas kernels: 21.3 us -> 19.8 us
  waiting for transfers between devices: 10.8 us -> 9.79 us
  local copies, waits for them, and re-layouts: 0.76 us -> 1.57 us
    pallas_call x2 -> x3, Pallas kernels: 10.5 us -> 9.04 us  [finish(): pl.pallas_call(lambda *refs: finish_kernel(members, group_count, len(piec...]
    unnamed x13 -> x17, local copies, waits for them, and re-layouts: 0.76 us -> 1.57 us
    all_to_all x1, waiting for transfers between devices: 3.14 us -> 2.33 us  [on_device_shared(): lax.all_to_all(sent, 'blk', split_axis=0, concat_axis=0, tiled=True)]
  transfers between devices with their start and end apart: 17 -> 17, of which waited for: 7 -> 8; matrix products, arithmetic and copies ran while one was open for 0% -> 0% of each run, Pallas kernels for 40% -> 39%
where the time goes in v3:
time: 51.3 us; the launch traced here: 51 us
  Pallas kernels  19.8 us (39%)
  starting transfers between devices  19.7 us (38%)
  waiting for transfers between devices  9.79 us (19%)
  local copies, waits for them, and re-layouts  1.57 us (3%)
    ppermute x7, starting transfers between devices, from_behind(): return lax.ppermute(x, axis, [(i, (i + by) % count) for i in range(count)])  9.17 us
    pallas_call x3, Pallas kernels, finish(): pl.pallas_call(lambda *refs: finish_kernel(members, group_count, len(piec...  9.04 us
    ppermute x9, starting transfers between devices, from_partner(): lax.ppermute(x, axis, [(i, i ^ flip) for i in range(lax.axis_size(axis))])  7 us
    pallas_call x1, Pallas kernels, project(): pl.pallas_call(lambda *refs: project_kernel(len(bases), *refs), out_shape...  6.93 us
    ppermute x7, waiting for transfers between devices, from_behind(): return lax.ppermute(x, axis, [(i, (i + by) % count) for i in range(count)])  6.49 us
    all_to_all x1, starting transfers between devices, on_device_shared(): lax.all_to_all(sent, 'blk', split_axis=0, concat_axis=0, tiled=True)  3.54 us
    all_to_all x1, waiting for transfers between devices, on_device_shared(): lax.all_to_all(sent, 'blk', split_axis=0, concat_axis=0, tiled=True)  2.33 us
    pallas_call x1, Pallas kernels, pack_pairs(): pl.pallas_call(pack_kernel, out_shape=jax.ShapeDtypeStruct((send_order.sh...  2.02 us
  transfers between devices with their start and end apart: 17, of which 8 were waited for; matrix products, arithmetic and copies ran while one was open for 0% of the time, Pallas kernels for 39%

profile of v3, /device:TPU:0, one launch (start us, length us, event | category | flops | bytes accessed | tf_op | source)
XLA Modules:
  0.0 51.0 jit_solution(8711676783050576874)
XLA Ops:
  0.0 3.0 %collective-permute-start.2 = (f32[8,64,256]{2,1,0:T(8,128)}, f32[8,64,256]{2,1,0:T(8,128)S(1)}, u32[]{:S(2)}, u32[]{:S(2)}) collective-permute-start(f32[8,64,256]{2,1,0:T(8,128)} %refs_2_), channel_id=1, source_target_pairs={{0,8},{4,12},{8,0},{12,4},{16,24},{20,28},{24,16},{28,20},{1,9},{5... | collective-permute-start | bytes 1572872 | tf_op jit(solution)/shard_map/ppermute | solution.py:33
  3.0 1.5 %collective-permute-start = (f32[2,2,64,256]{3,2,1,0:T(8,128)}, f32[2,2,64,256]{3,2,1,0:T(8,128)S(1)}, u32[]{:S(2)}, u32[]{:S(2)}) collective-permute-start(f32[2,2,64,256]{3,2,1,0:T(8,128)} %refs_4_.1), channel_id=1, source_target_pairs={{0,16},{4,20},{8,24},{12,28},{16,0},{20,4},{24,8},{28,12},{1,17},{... | collective-permute-start | bytes 786440 | tf_op jit(solution)/shard_map/ppermute | solution.py:38
  4.6 1.6 %collective-permute-start.3 = (f32[2,2,64,256]{3,2,1,0:T(8,128)}, f32[2,2,64,256]{3,2,1,0:T(8,128)}, u32[]{:S(2)}, u32[]{:S(2)}) collective-permute-start(f32[2,2,64,256]{3,2,1,0:T(8,128)} %refs_4_.1), channel_id=1, source_target_pairs={{0,1},{1,2},{2,3},{3,0},{4,5},{5,6},{6,7},{7,4},{8,9},{9,10},{10,1... | collective-permute-start | bytes 786440 | tf_op jit(solution)/shard_map/ppermute | solution.py:38
  6.1 2.2 %collective-permute-start.4 = (f32[2,2,64,256]{3,2,1,0:T(8,128)}, f32[2,2,64,256]{3,2,1,0:T(8,128)}, u32[]{:S(2)}, u32[]{:S(2)}) collective-permute-start(f32[2,2,64,256]{3,2,1,0:T(8,128)} %refs_4_.1), channel_id=1, source_target_pairs={{0,3},{1,0},{2,1},{3,2},{4,7},{5,4},{6,5},{7,6},{8,11},{9,8},{10,9... | collective-permute-start | bytes 786440 | tf_op jit(solution)/shard_map/ppermute | solution.py:38
  8.4 2.0 %shard_map.73 = f32[8,80,256]{2,1,0:T(8,128)} custom-call(s32[8]{0:T(128)} %bitcast.6, f32[8,64,256]{2,1,0:T(8,128)} %refs_2_, f32[8,4096]{1,0:T(8,128)} %amps.3), custom_call_target="tpu_custom_call" | custom-call | bytes 524288 | tf_op jit(solution)/shard_map/pallas_call | solution.py:59
  10.4 0.6 %collective-permute-done.refs_3_.refs_4_ = f32[2,2,64,256]{3,2,1,0:T(8,128)S(1)} collective-permute-done((f32[2,2,64,256]{3,2,1,0:T(8,128)}, f32[2,2,64,256]{3,2,1,0:T(8,128)S(1)}, u32[]{:S(2)}, u32[]{:S(2)}) %collective-permute-start) | collective-permute-done | bytes 262176 | tf_op jit(solution)/shard_map/ppermute | solution.py:38
  11.0 3.5 %all-to-all-start = ((f32[8,80,256]{2,1,0:T(8,128)}), f32[8,80,256]{2,1,0:T(8,128)S(1)}, u32[]{:S(2)}, u32[]{:S(2)}) async-start(f32[8,80,256]{2,1,0:T(8,128)} %shard_map.73), calls=%async_computation | async-start | bytes 1310720 | tf_op jit(solution)/shard_map/all_to_all | solution.py:362
  14.6 0.0 copy-done
  14.6 0.0 copy-start.4
  14.6 0.4 collective-permute-start.1
  15.0 0.9 %collective-permute-done.3.refs_5_ = f32[2,2,64,256]{3,2,1,0:T(8,128)} collective-permute-done((f32[2,2,64,256]{3,2,1,0:T(8,128)}, f32[2,2,64,256]{3,2,1,0:T(8,128)}, u32[]{:S(2)}, u32[]{:S(2)}) %collective-permute-start.3) | collective-permute-done | bytes 262176 | tf_op jit(solution)/shard_map/ppermute | solution.py:38
  16.0 3.3 %collective-permute-done.4.refs_7_ = f32[2,2,64,256]{3,2,1,0:T(8,128)} collective-permute-done((f32[2,2,64,256]{3,2,1,0:T(8,128)}, f32[2,2,64,256]{3,2,1,0:T(8,128)}, u32[]{:S(2)}, u32[]{:S(2)}) %collective-permute-start.4) | collective-permute-done | bytes 262176 | tf_op jit(solution)/shard_map/ppermute | solution.py:38
  19.3 0.0 collective-permute-done.2.refs_2_
  19.3 0.0 collective-permute-start.5
  19.3 2.4 %collective-permute-start.6 = (f32[2,2,64,256]{3,2,1,0:T(8,128)}, f32[2,2,64,256]{3,2,1,0:T(8,128)}, u32[]{:S(2)}, u32[]{:S(2)}) collective-permute-start(f32[2,2,64,256]{3,2,1,0:T(8,128)} %collective-permute-done.4.refs_7_), channel_id=1, source_target_pairs={{0,3},{1,0},{2,1},{3,2},{4,7},{5,4},{6,5},{7,6},{8,11},{9,8},{10,9... | collective-permute-start | bytes 786440 | tf_op jit(solution)/shard_map/ppermute | solution.py:38
  21.6 0.5 collective-permute-start.7
  22.2 0.4 collective-permute-start.9
  22.6 0.0 collective-permute-done.1.refs_1_.refs_3_
  22.6 0.8 %copy-done.2 = f32[8,64,256]{2,1,0:T(8,128)} copy-done((f32[8,64,256]{2,1,0:T(8,128)}, f32[8,64,256]{2,1,0:T(8,128)S(1)}, u32[]{:S(2)}) %copy-start.2) | copy-done | bytes 524312
  23.4 2.3 %all-to-all-done.coupled = f32[8,80,256]{2,1,0:T(8,128)S(1)} async-done(((f32[8,80,256]{2,1,0:T(8,128)}), f32[8,80,256]{2,1,0:T(8,128)S(1)}, u32[]{:S(2)}, u32[]{:S(2)}) %all-to-all-start) | async-done | bytes 655392 | tf_op jit(solution)/shard_map/all_to_all | solution.py:362
  25.7 0.0 collective-permute-done.5.refs_3_.refs_2_
  25.7 0.0 copy-done.1
  25.8 0.0 copy-done.5
  25.8 0.0 copy-done.6
  25.8 0.0 copy-done.7
  25.8 1.8 %shard_map.74 = (f32[8,40,128]{2,1,0:T(8,128)S(1)}, f32[8,32,128]{2,1,0:T(8,128)S(1)}) custom-call(s32[8,8]{1,0:T(8,128)S(1)} %copy-done.5, f32[8,8]{1,0:T(8,128)S(1)} %copy-done.6, f32[8,16]{1,0:T(8,128)S(1)} %copy-done.7, f32[8,64,256]{2,1,0:T(8,128)S(1)} %copy-done, f32[8,4096]{1,0:T(8,128)S(1)} %copy-done.1, f32[8,80,256]{2,1,0:T(8,128)S(1)} %all-to-all-done.coupled), custom_call_target="tpu_custom_call" | custom-call | flops 4000000000 | bytes 1048576 | tf_op jit(solution)/shard_map/pallas_call | solution.py:121
  27.6 0.3 collective-permute-start.10
  27.9 0.3 collective-permute-start.12
  28.2 0.5 collective-permute-done.6.refs_6_
  28.7 0.5 collective-permute-start.8
  29.2 6.9 %shard_map.75 = (bf16[32,128,128]{2,1,0:T(8,128)(2,1)S(1)}, bf16[32,128,256]{2,1,0:T(8,128)(2,1)S(1)}) custom-call(f32[8,64,256]{2,1,0:T(8,128)S(1)} %copy-done, f32[8,64,256]{2,1,0:T(8,128)S(1)} %copy-done.3, f32[8,64,256]{2,1,0:T(8,128)S(1)} %collective-permute-done.2.refs_2_, f32[8,64,256]{2,1,0:T(8,128)S(1)} %collective-permute-done.5.refs_3_.refs_2_, ...), custom_call_target="tpu_custom_call" | custom-call | flops 4026531840 | bytes 1048576 | tf_op jit(solution)/shard_map/pallas_call | solution.py:251
  36.1 0.0 collective-permute-done.7.refs_4_.refs_5_
  36.2 0.6 %collective-permute-start.14 = (f32[8,40,128]{2,1,0:T(8,128)S(1)}, f32[8,40,128]{2,1,0:T(8,128)S(1)}, u32[]{:S(2)}, u32[]{:S(2)}) collective-permute-start(f32[8,40,128]{2,1,0:T(8,128)S(1)} %get-tuple-element.46.refs_8_), channel_id=1, source_target_pairs={{0,4},{4,0},{8,12},{12,8},{16,20},{20,16},{24,28},{28,24},{1,5},{5... | collective-permute-start | bytes 491528 | tf_op jit(solution)/shard_map/ppermute | solution.py:33
  36.8 0.0 collective-permute-done.9.refs_6_.refs_7_
  36.8 0.0 collective-permute-done.10.refs_7_
  36.8 1.1 %collective-permute-done.8.refs_5_.refs_6_ = f32[2,2,64,256]{3,2,1,0:T(8,128)S(1)} collective-permute-done((f32[2,2,64,256]{3,2,1,0:T(8,128)}, f32[2,2,64,256]{3,2,1,0:T(8,128)S(1)}, u32[]{:S(2)}, u32[]{:S(2)}) %collective-permute-start.8) | collective-permute-done | bytes 262176 | tf_op jit(solution)/shard_map/ppermute | solution.py:38
  37.9 2.4 %shard_map.76 = f32[8,32,128]{2,1,0:T(8,128)S(1)} custom-call(bf16[32,128,128]{2,1,0:T(8,128)(2,1)S(1)} %get-tuple-element.51.refs_0_, bf16[32,128,256]{2,1,0:T(8,128)(2,1)S(1)} %get-tuple-element.52.refs_1_, f32[8,64,256]{2,1,0:T(8,128)S(1)} %collective-permute-done.5.refs_3_.refs_2_, f32[2,2,64,256]{3,2,1,0:T(8,128)S(1)} %collective-permute-done.refs_3_.refs_4_, ...), custom_call_target="tpu_custom_call" | custom-call | flops 1107296256 | bytes 1048576 | tf_op jit(solution)/shard_map/pallas_call | solution.py:323
  40.3 0.0 collective-permute-done.12.refs_7_
  40.3 2.4 %shard_map.77 = f32[8,32,128]{2,1,0:T(8,128)S(1)} custom-call(bf16[32,128,128]{2,1,0:T(8,128)(2,1)S(1)} %get-tuple-element.51.refs_0_, bf16[32,128,256]{2,1,0:T(8,128)(2,1)S(1)} %get-tuple-element.52.refs_1_, f32[8,64,256]{2,1,0:T(8,128)S(1)} %collective-permute-done.2.refs_2_, f32[2,2,64,256]{3,2,1,0:T(8,128)S(1)} %collective-permute-done.refs_3_.refs_4_, ...), custom_call_target="tpu_custom_call" | custom-call | flops 1107296256 | bytes 1048576 | tf_op jit(solution)/shard_map/pallas_call | solution.py:323
  42.6 0.6 %collective-permute-start.13 = (f32[8,32,128]{2,1,0:T(8,128)S(1)}, f32[8,32,128]{2,1,0:T(8,128)S(1)}, u32[]{:S(2)}, u32[]{:S(2)}) collective-permute-start(f32[8,32,128]{2,1,0:T(8,128)S(1)} %shard_map.77), channel_id=1, source_target_pairs={{0,8},{4,12},{8,0},{12,4},{16,24},{20,28},{24,16},{28,20},{1,9},{5... | collective-permute-start | bytes 393224 | tf_op jit(solution)/shard_map/ppermute | solution.py:33
  43.2 0.8 %collective-permute-start.11 = (f32[8,32,128]{2,1,0:T(8,128)S(1)}, f32[8,32,128]{2,1,0:T(8,128)S(1)}, u32[]{:S(2)}, u32[]{:S(2)}) collective-permute-start(f32[8,32,128]{2,1,0:T(8,128)S(1)} %shard_map.76), channel_id=1, source_target_pairs={{0,12},{4,8},{8,4},{12,0},{16,28},{20,24},{24,20},{28,16},{1,13},{... | collective-permute-start | bytes 393224 | tf_op jit(solution)/shard_map/ppermute | solution.py:33
  44.0 0.0 collective-permute-done.14.refs_9_
  44.0 4.3 %shard_map.78 = (f32[8,32,128]{2,1,0:T(8,128)S(1)}, f32[8,32,128]{2,1,0:T(8,128)S(1)}) custom-call(bf16[32,128,128]{2,1,0:T(8,128)(2,1)S(1)} %get-tuple-element.51.refs_0_, bf16[32,128,256]{2,1,0:T(8,128)(2,1)S(1)} %get-tuple-element.52.refs_1_, f32[8,64,256]{2,1,0:T(8,128)S(1)} %copy-done, f32[8,64,256]{2,1,0:T(8,128)S(1)} %copy-done.3, ...), custom_call_target="tpu_custom_call" | custom-call | flops 2214592512 | bytes 1048576 | tf_op jit(solution)/shard_map/pallas_call | solution.py:323
  48.3 0.9 %collective-permute-start.15 = (f32[8,32,128]{2,1,0:T(8,128)S(1)}, f32[8,32,128]{2,1,0:T(8,128)S(1)}, u32[]{:S(2)}, u32[]{:S(2)}) collective-permute-start(f32[8,32,128]{2,1,0:T(8,128)S(1)} %get-tuple-element.65), channel_id=1, source_target_pairs={{0,4},{4,0},{8,12},{12,8},{16,20},{20,16},{24,28},{28,24},{1,5},{5... | collective-permute-start | bytes 393224 | tf_op jit(solution)/shard_map/ppermute | solution.py:33
  49.3 0.0 collective-permute-done.13
  49.3 0.6 %collective-permute-done.11 = f32[8,32,128]{2,1,0:T(8,128)S(1)} collective-permute-done((f32[8,32,128]{2,1,0:T(8,128)S(1)}, f32[8,32,128]{2,1,0:T(8,128)S(1)}, u32[]{:S(2)}, u32[]{:S(2)}) %collective-permute-start.11) | collective-permute-done | bytes 131104 | tf_op jit(solution)/shard_map/ppermute | solution.py:33
  49.9 0.4 collective-permute-done.15
  50.3 0.7 %copy.10 = f32[1,8,32,128]{3,1,2,0:T(8,128)} copy(f32[1,8,32,128]{3,2,1,0:T(8,128)S(1)} %add_bitcast_fusion) | data formatting | bytes 262144
  (11 shorter events, 0.1 us)
Async XLA Ops:
  0.0 14.6 %copy-start = (f32[8,64,256]{2,1,0:T(8,128)S(1)}, f32[8,64,256]{2,1,0:T(8,128)}, u32[]{:S(2)}) copy-start(f32[8,64,256]{2,1,0:T(8,128)} %refs_2_) | copy-start | bytes 1572868
  0.0 25.7 %copy-start.1 = (f32[8,4096]{1,0:T(8,128)S(1)}, f32[8,4096]{1,0:T(8,128)}, u32[]{:S(2)}) copy-start(f32[8,4096]{1,0:T(8,128)} %amps.3) | copy-start | bytes 393220
  0.0 25.8 %copy-start.5 = (s32[8,8]{1,0:T(8,128)S(1)}, s32[8,8]{1,0:T(8,128)}, u32[]{:S(2)}) copy-start(s32[8,8]{1,0:T(8,128)} %couple.1) | copy-start | bytes 772
  0.0 25.8 %copy-start.6 = (f32[8,8]{1,0:T(8,128)S(1)}, f32[8,8]{1,0:T(8,128)}, u32[]{:S(2)}) copy-start(f32[8,8]{1,0:T(8,128)} %couple_weight.1) | copy-start | bytes 772
  0.0 25.8 %copy-start.7 = (f32[8,16]{1,0:T(8,128)S(1)}, f32[8,16]{1,0:T(8,128)}, u32[]{:S(2)}) copy-start(f32[8,16]{1,0:T(8,128)} %fit_weight.1) | copy-start | bytes 1540
  0.0 19.3 %collective-permute-start.2 = (f32[8,64,256]{2,1,0:T(8,128)}, f32[8,64,256]{2,1,0:T(8,128)S(1)}, u32[]{:S(2)}, u32[]{:S(2)}) collective-permute-start(f32[8,64,256]{2,1,0:T(8,128)} %refs_2_), channel_id=1, source_target_pairs={{0,8},{4,12},{8,0},{12,4},{16,24},{20,28},{24,16},{28,20},{1,9},{5... | collective-permute-start | bytes 1572872 | tf_op jit(solution)/shard_map/ppermute | solution.py:33
  3.0 8.0 %collective-permute-start = (f32[2,2,64,256]{3,2,1,0:T(8,128)}, f32[2,2,64,256]{3,2,1,0:T(8,128)S(1)}, u32[]{:S(2)}, u32[]{:S(2)}) collective-permute-start(f32[2,2,64,256]{3,2,1,0:T(8,128)} %refs_4_.1), channel_id=1, source_target_pairs={{0,16},{4,20},{8,24},{12,28},{16,0},{20,4},{24,8},{28,12},{1,17},{... | collective-permute-start | bytes 786440 | tf_op jit(solution)/shard_map/ppermute | solution.py:38
  4.6 11.4 %collective-permute-start.3 = (f32[2,2,64,256]{3,2,1,0:T(8,128)}, f32[2,2,64,256]{3,2,1,0:T(8,128)}, u32[]{:S(2)}, u32[]{:S(2)}) collective-permute-start(f32[2,2,64,256]{3,2,1,0:T(8,128)} %refs_4_.1), channel_id=1, source_target_pairs={{0,1},{1,2},{2,3},{3,0},{4,5},{5,6},{6,7},{7,4},{8,9},{9,10},{10,1... | collective-permute-start | bytes 786440 | tf_op jit(solution)/shard_map/ppermute | solution.py:38
  6.1 13.1 %collective-permute-start.4 = (f32[2,2,64,256]{3,2,1,0:T(8,128)}, f32[2,2,64,256]{3,2,1,0:T(8,128)}, u32[]{:S(2)}, u32[]{:S(2)}) collective-permute-start(f32[2,2,64,256]{3,2,1,0:T(8,128)} %refs_4_.1), channel_id=1, source_target_pairs={{0,3},{1,0},{2,1},{3,2},{4,7},{5,4},{6,5},{7,6},{8,11},{9,8},{10,9... | collective-permute-start | bytes 786440 | tf_op jit(solution)/shard_map/ppermute | solution.py:38
  11.0 14.7 %all-to-all-start = ((f32[8,80,256]{2,1,0:T(8,128)}), f32[8,80,256]{2,1,0:T(8,128)S(1)}, u32[]{:S(2)}, u32[]{:S(2)}) async-start(f32[8,80,256]{2,1,0:T(8,128)} %shard_map.73), calls=%async_computation | async-start | bytes 1310720 | tf_op jit(solution)/shard_map/all_to_all | solution.py:362
  14.6 14.6 %copy-start.4 = (f32[2,2,64,256]{3,2,1,0:T(8,128)S(1)}, f32[2,2,64,256]{3,2,1,0:T(8,128)}, u32[]{:S(2)}) copy-start(f32[2,2,64,256]{3,2,1,0:T(8,128)} %refs_4_.1) | copy-start | bytes 786436
  14.6 8.0 %collective-permute-start.1 = (f32[8,64,256]{2,1,0:T(8,128)S(1)}, f32[8,64,256]{2,1,0:T(8,128)S(1)}, u32[]{:S(2)}, u32[]{:S(2)}) collective-permute-start(f32[8,64,256]{2,1,0:T(8,128)S(1)} %copy-done), channel_id=1, source_target_pairs={{0,4},{4,0},{8,12},{12,8},{16,20},{20,16},{24,28},{28,24},{1,5},{5... | collective-permute-start | bytes 1572872 | tf_op jit(solution)/shard_map/ppermute | solution.py:33
  19.3 6.5 %collective-permute-start.5 = (f32[8,64,256]{2,1,0:T(8,128)S(1)}, f32[8,64,256]{2,1,0:T(8,128)S(1)}, u32[]{:S(2)}, u32[]{:S(2)}) collective-permute-start(f32[8,64,256]{2,1,0:T(8,128)S(1)} %collective-permute-done.2.refs_2_), channel_id=1, source_target_pairs={{0,4},{4,0},{8,12},{12,8},{16,20},{20,16},{24,28},{28,24},{1,5},{5... | collective-permute-start | bytes 1572872 | tf_op jit(solution)/shard_map/ppermute | solution.py:33
  19.3 9.4 %collective-permute-start.6 = (f32[2,2,64,256]{3,2,1,0:T(8,128)}, f32[2,2,64,256]{3,2,1,0:T(8,128)}, u32[]{:S(2)}, u32[]{:S(2)}) collective-permute-start(f32[2,2,64,256]{3,2,1,0:T(8,128)} %collective-permute-done.4.refs_7_), channel_id=1, source_target_pairs={{0,3},{1,0},{2,1},{3,2},{4,7},{5,4},{6,5},{7,6},{8,11},{9,8},{10,9... | collective-permute-start | bytes 786440 | tf_op jit(solution)/shard_map/ppermute | solution.py:38
  21.6 14.5 %collective-permute-start.7 = (f32[2,2,64,256]{3,2,1,0:T(8,128)}, f32[2,2,64,256]{3,2,1,0:T(8,128)S(1)}, u32[]{:S(2)}, u32[]{:S(2)}) collective-permute-start(f32[2,2,64,256]{3,2,1,0:T(8,128)} %collective-permute-done.3.refs_5_), channel_id=1, source_target_pairs={{0,16},{4,20},{8,24},{12,28},{16,0},{20,4},{24,8},{28,12},{1,17},{... | collective-permute-start | bytes 786440 | tf_op jit(solution)/shard_map/ppermute | solution.py:38
  22.2 14.6 %collective-permute-start.9 = (f32[2,2,64,256]{3,2,1,0:T(8,128)S(1)}, f32[2,2,64,256]{3,2,1,0:T(8,128)S(1)}, u32[]{:S(2)}, u32[]{:S(2)}) collective-permute-start(f32[2,2,64,256]{3,2,1,0:T(8,128)S(1)} %collective-permute-done.refs_3_.refs_4_), channel_id=1, source_target_pairs={{0,3},{1,0},{2,1},{3,2},{4,7},{5,4},{6,5},{7,6},{8,11},{9,8},{10,9... | collective-permute-start | bytes 786440 | tf_op jit(solution)/shard_map/ppermute | solution.py:38
  22.6 0.8 %copy-start.2 = (f32[8,64,256]{2,1,0:T(8,128)}, f32[8,64,256]{2,1,0:T(8,128)S(1)}, u32[]{:S(2)}) copy-start(f32[8,64,256]{2,1,0:T(8,128)S(1)} %collective-permute-done.1.refs_1_.refs_3_) | copy-start | bytes 1572868
  25.7 3.5 %copy-start.3 = (f32[8,64,256]{2,1,0:T(8,128)S(1)}, f32[8,64,256]{2,1,0:T(8,128)}, u32[]{:S(2)}) copy-start(f32[8,64,256]{2,1,0:T(8,128)} %copy-done.2) | copy-start | bytes 1572868
  27.6 9.2 %collective-permute-start.10 = (f32[8,40,128]{2,1,0:T(8,128)S(1)}, f32[8,40,128]{2,1,0:T(8,128)S(1)}, u32[]{:S(2)}, u32[]{:S(2)}) collective-permute-start(f32[8,40,128]{2,1,0:T(8,128)S(1)} %get-tuple-element.46.refs_8_), channel_id=1, source_target_pairs={{0,12},{4,8},{8,4},{12,0},{16,28},{20,24},{24,20},{28,16},{1,13},{... | collective-permute-start | bytes 491528 | tf_op jit(solution)/shard_map/ppermute | solution.py:33
  27.9 12.4 %collective-permute-start.12 = (f32[8,40,128]{2,1,0:T(8,128)S(1)}, f32[8,40,128]{2,1,0:T(8,128)S(1)}, u32[]{:S(2)}, u32[]{:S(2)}) collective-permute-start(f32[8,40,128]{2,1,0:T(8,128)S(1)} %get-tuple-element.46.refs_8_), channel_id=1, source_target_pairs={{0,8},{4,12},{8,0},{12,4},{16,24},{20,28},{24,16},{28,20},{1,9},{5... | collective-permute-start | bytes 491528 | tf_op jit(solution)/shard_map/ppermute | solution.py:33
  28.7 9.2 %collective-permute-start.8 = (f32[2,2,64,256]{3,2,1,0:T(8,128)}, f32[2,2,64,256]{3,2,1,0:T(8,128)S(1)}, u32[]{:S(2)}, u32[]{:S(2)}) collective-permute-start(f32[2,2,64,256]{3,2,1,0:T(8,128)} %collective-permute-done.6.refs_6_), channel_id=1, source_target_pairs={{0,16},{4,20},{8,24},{12,28},{16,0},{20,4},{24,8},{28,12},{1,17},{... | collective-permute-start | bytes 786440 | tf_op jit(solution)/shard_map/ppermute | solution.py:38
  36.2 7.8 %collective-permute-start.14 = (f32[8,40,128]{2,1,0:T(8,128)S(1)}, f32[8,40,128]{2,1,0:T(8,128)S(1)}, u32[]{:S(2)}, u32[]{:S(2)}) collective-permute-start(f32[8,40,128]{2,1,0:T(8,128)S(1)} %get-tuple-element.46.refs_8_), channel_id=1, source_target_pairs={{0,4},{4,0},{8,12},{12,8},{16,20},{20,16},{24,28},{28,24},{1,5},{5... | collective-permute-start | bytes 491528 | tf_op jit(solution)/shard_map/ppermute | solution.py:33
  42.6 6.6 %collective-permute-start.13 = (f32[8,32,128]{2,1,0:T(8,128)S(1)}, f32[8,32,128]{2,1,0:T(8,128)S(1)}, u32[]{:S(2)}, u32[]{:S(2)}) collective-permute-start(f32[8,32,128]{2,1,0:T(8,128)S(1)} %shard_map.77), channel_id=1, source_target_pairs={{0,8},{4,12},{8,0},{12,4},{16,24},{20,28},{24,16},{28,20},{1,9},{5... | collective-permute-start | bytes 393224 | tf_op jit(solution)/shard_map/ppermute | solution.py:33
  43.2 6.6 %collective-permute-start.11 = (f32[8,32,128]{2,1,0:T(8,128)S(1)}, f32[8,32,128]{2,1,0:T(8,128)S(1)}, u32[]{:S(2)}, u32[]{:S(2)}) collective-permute-start(f32[8,32,128]{2,1,0:T(8,128)S(1)} %shard_map.76), channel_id=1, source_target_pairs={{0,12},{4,8},{8,4},{12,0},{16,28},{20,24},{24,20},{28,16},{1,13},{... | collective-permute-start | bytes 393224 | tf_op jit(solution)/shard_map/ppermute | solution.py:33
  48.3 1.9 %collective-permute-start.15 = (f32[8,32,128]{2,1,0:T(8,128)S(1)}, f32[8,32,128]{2,1,0:T(8,128)S(1)}, u32[]{:S(2)}, u32[]{:S(2)}) collective-permute-start(f32[8,32,128]{2,1,0:T(8,128)S(1)} %get-tuple-element.65), channel_id=1, source_target_pairs={{0,4},{4,0},{8,12},{12,8},{16,20},{20,16},{24,28},{28,24},{1,5},{5... | collective-permute-start | bytes 393224 | tf_op jit(solution)/shard_map/ppermute | solution.py:33

commit v4 on v3

--- a/solution.py
+++ b/solution.py
@@ -376,18 +376,17 @@
     inner = [project(bases, group) for group in groups[:-1]]
     final = groups[-1]
     dressed = [own, *[from_partner(own, "blk", flip) for flip in range(1, SET)]]
-    for members in ((3,), (2,), (0, 1)):
-        partial = finish(
-            members, inner, [bases[member] for member in members], final, [dressed[member] for member in members]
-        )
-        if members[0]:
+    for member in (3, 2, 1, 0):
+        partial = finish((member,), inner, [bases[member]], final, [dressed[member]])[0]
+        if member:
             partial, *final = lax.optimization_barrier((partial, *final))
-            for member, x in zip(members, partial):
-                updated = updated + from_partner(x, "blk", member)
+            partial = from_partner(partial, "blk", member)
+        if member == 1:
+            beside = partial
         else:
-            mine, beside = partial
-            updated, mine, beside = lax.optimization_barrier((updated, mine, from_partner(beside, "blk", 1)))
-            updated = updated + mine + beside
+            updated = updated + partial
+    updated, beside = lax.optimization_barrier((updated, beside))
+    updated = updated + beside
     return updated.reshape(pair_count, pno_count * pno_count)
 
 

time: 51.3 us -> 52.5 us (1.023)
  Pallas kernels: 19.8 us -> 21.5 us
  waiting for transfers between devices: 9.79 us -> 8.74 us
    pallas_call x3 -> x4, Pallas kernels: 9.04 us -> 10.6 us  [finish(): pl.pallas_call(lambda *refs: finish_kernel(members, group_count, len(piec...]
    ppermute x7, waiting for transfers between devices: 6.49 us -> 5.45 us  [from_behind(): return lax.ppermute(x, axis, [(i, (i + by) % count) for i in range(count)])]
    ppermute x9, waiting for transfers between devices: 0.97 us -> 0.15 us  [from_partner(): lax.ppermute(x, axis, [(i, i ^ flip) for i in range(lax.axis_size(axis))])]
    all_to_all x1, waiting for transfers between devices: 2.33 us -> 3.14 us  [on_device_shared(): lax.all_to_all(sent, 'blk', split_axis=0, concat_axis=0, tiled=True)]
    unnamed x17 -> x13, local copies, waits for them, and re-layouts: 1.57 us -> 1.7 us
  transfers between devices with their start and end apart: 17 -> 17, of which waited for: 8 -> 6; matrix products, arithmetic and copies ran while one was open for 0% -> 0% of each run, Pallas kernels for 39% -> 42%
where the time goes in v4:
time: 52.5 us; the launch traced here: 51.8 us
  Pallas kernels  21.5 us (41%)
  starting transfers between devices  19.6 us (37%)
  waiting for transfers between devices  8.74 us (17%)
  local copies, waits for them, and re-layouts  1.7 us (3%)
    pallas_call x4, Pallas kernels, finish(): pl.pallas_call(lambda *refs: finish_kernel(members, group_count, len(piec...  10.6 us
    ppermute x7, starting transfers between devices, from_behind(): return lax.ppermute(x, axis, [(i, (i + by) % count) for i in range(count)])  9.17 us
    pallas_call x1, Pallas kernels, project(): pl.pallas_call(lambda *refs: project_kernel(len(bases), *refs), out_shape...  7.08 us
    ppermute x9, starting transfers between devices, from_partner(): lax.ppermute(x, axis, [(i, i ^ flip) for i in range(lax.axis_size(axis))])  6.93 us
    ppermute x7, waiting for transfers between devices, from_behind(): return lax.ppermute(x, axis, [(i, (i + by) % count) for i in range(count)])  5.45 us
    all_to_all x1, starting transfers between devices, on_device_shared(): lax.all_to_all(sent, 'blk', split_axis=0, concat_axis=0, tiled=True)  3.54 us
    all_to_all x1, waiting for transfers between devices, on_device_shared(): lax.all_to_all(sent, 'blk', split_axis=0, concat_axis=0, tiled=True)  3.14 us
    pallas_call x1, Pallas kernels, pack_pairs(): pl.pallas_call(pack_kernel, out_shape=jax.ShapeDtypeStruct((send_order.sh...  2.03 us
  transfers between devices with their start and end apart: 17, of which 6 were waited for; matrix products, arithmetic and copies ran while one was open for 0% of the time, Pallas kernels for 42%

profile of v4, /device:TPU:0, one launch (start us, length us, event | category | flops | bytes accessed | tf_op | source)
XLA Modules:
  0.0 51.8 jit_solution(13578355952542280474)
XLA Ops:
  0.0 3.0 %collective-permute-start.2 = (f32[8,64,256]{2,1,0:T(8,128)}, f32[8,64,256]{2,1,0:T(8,128)S(1)}, u32[]{:S(2)}, u32[]{:S(2)}) collective-permute-start(f32[8,64,256]{2,1,0:T(8,128)} %refs_2_), channel_id=1, source_target_pairs={{0,8},{4,12},{8,0},{12,4},{16,24},{20,28},{24,16},{28,20},{1,9},{5... | collective-permute-start | bytes 1572872 | tf_op jit(solution)/shard_map/ppermute | solution.py:33
  3.0 1.5 %collective-permute-start = (f32[2,2,64,256]{3,2,1,0:T(8,128)}, f32[2,2,64,256]{3,2,1,0:T(8,128)S(1)}, u32[]{:S(2)}, u32[]{:S(2)}) collective-permute-start(f32[2,2,64,256]{3,2,1,0:T(8,128)} %refs_4_.1), channel_id=1, source_target_pairs={{0,16},{4,20},{8,24},{12,28},{16,0},{20,4},{24,8},{28,12},{1,17},{... | collective-permute-start | bytes 786440 | tf_op jit(solution)/shard_map/ppermute | solution.py:38
  4.6 1.6 %collective-permute-start.3 = (f32[2,2,64,256]{3,2,1,0:T(8,128)}, f32[2,2,64,256]{3,2,1,0:T(8,128)}, u32[]{:S(2)}, u32[]{:S(2)}) collective-permute-start(f32[2,2,64,256]{3,2,1,0:T(8,128)} %refs_4_.1), channel_id=1, source_target_pairs={{0,1},{1,2},{2,3},{3,0},{4,5},{5,6},{6,7},{7,4},{8,9},{9,10},{10,1... | collective-permute-start | bytes 786440 | tf_op jit(solution)/shard_map/ppermute | solution.py:38
  6.1 2.2 %collective-permute-start.4 = (f32[2,2,64,256]{3,2,1,0:T(8,128)}, f32[2,2,64,256]{3,2,1,0:T(8,128)}, u32[]{:S(2)}, u32[]{:S(2)}) collective-permute-start(f32[2,2,64,256]{3,2,1,0:T(8,128)} %refs_4_.1), channel_id=1, source_target_pairs={{0,3},{1,0},{2,1},{3,2},{4,7},{5,4},{6,5},{7,6},{8,11},{9,8},{10,9... | collective-permute-start | bytes 786440 | tf_op jit(solution)/shard_map/ppermute | solution.py:38
  8.4 2.0 %shard_map.73 = f32[8,80,256]{2,1,0:T(8,128)} custom-call(s32[8]{0:T(128)} %bitcast.6, f32[8,64,256]{2,1,0:T(8,128)} %refs_2_, f32[8,4096]{1,0:T(8,128)} %amps.3), custom_call_target="tpu_custom_call" | custom-call | bytes 524288 | tf_op jit(solution)/shard_map/pallas_call | solution.py:59
  10.4 0.6 %collective-permute-done.refs_3_ = f32[2,2,64,256]{3,2,1,0:T(8,128)S(1)} collective-permute-done((f32[2,2,64,256]{3,2,1,0:T(8,128)}, f32[2,2,64,256]{3,2,1,0:T(8,128)S(1)}, u32[]{:S(2)}, u32[]{:S(2)}) %collective-permute-start) | collective-permute-done | bytes 262176 | tf_op jit(solution)/shard_map/ppermute | solution.py:38
  11.0 3.5 %all-to-all-start = ((f32[8,80,256]{2,1,0:T(8,128)}), f32[8,80,256]{2,1,0:T(8,128)S(1)}, u32[]{:S(2)}, u32[]{:S(2)}) async-start(f32[8,80,256]{2,1,0:T(8,128)} %shard_map.73), calls=%async_computation | async-start | bytes 1310720 | tf_op jit(solution)/shard_map/all_to_all | solution.py:362
  14.6 0.0 copy-done
  14.6 0.4 collective-permute-start.1
  15.0 1.0 %collective-permute-done.3.refs_5_ = f32[2,2,64,256]{3,2,1,0:T(8,128)} collective-permute-done((f32[2,2,64,256]{3,2,1,0:T(8,128)}, f32[2,2,64,256]{3,2,1,0:T(8,128)}, u32[]{:S(2)}, u32[]{:S(2)}) %collective-permute-start.3) | collective-permute-done | bytes 262176 | tf_op jit(solution)/shard_map/ppermute | solution.py:38
  16.0 3.3 %collective-permute-done.4.refs_7_ = f32[2,2,64,256]{3,2,1,0:T(8,128)} collective-permute-done((f32[2,2,64,256]{3,2,1,0:T(8,128)}, f32[2,2,64,256]{3,2,1,0:T(8,128)}, u32[]{:S(2)}, u32[]{:S(2)}) %collective-permute-start.4) | collective-permute-done | bytes 262176 | tf_op jit(solution)/shard_map/ppermute | solution.py:38
  19.3 0.0 collective-permute-done.2.refs_2_
  19.3 0.0 collective-permute-start.5
  19.3 2.4 %collective-permute-start.6 = (f32[2,2,64,256]{3,2,1,0:T(8,128)}, f32[2,2,64,256]{3,2,1,0:T(8,128)}, u32[]{:S(2)}, u32[]{:S(2)}) collective-permute-start(f32[2,2,64,256]{3,2,1,0:T(8,128)} %collective-permute-done.4.refs_7_), channel_id=1, source_target_pairs={{0,3},{1,0},{2,1},{3,2},{4,7},{5,4},{6,5},{7,6},{8,11},{9,8},{10,9... | collective-permute-start | bytes 786440 | tf_op jit(solution)/shard_map/ppermute | solution.py:38
  21.6 0.5 collective-permute-start.7
  22.2 0.4 collective-permute-start.9
  22.6 0.0 collective-permute-done.1.refs_1_.refs_2_
  22.6 3.1 %all-to-all-done.coupled = f32[8,80,256]{2,1,0:T(8,128)S(1)} async-done(((f32[8,80,256]{2,1,0:T(8,128)}), f32[8,80,256]{2,1,0:T(8,128)S(1)}, u32[]{:S(2)}, u32[]{:S(2)}) %all-to-all-start) | async-done | bytes 655392 | tf_op jit(solution)/shard_map/all_to_all | solution.py:362
  25.7 0.0 collective-permute-done.5.refs_3_.refs_2_
  25.7 0.0 copy-done.1
  25.7 0.0 copy-done.3
  25.8 0.0 copy-done.4
  25.8 0.0 copy-done.5
  25.8 1.8 %shard_map.74 = (f32[8,40,128]{2,1,0:T(8,128)S(1)}, f32[8,32,128]{2,1,0:T(8,128)S(1)}) custom-call(s32[8,8]{1,0:T(8,128)S(1)} %copy-done.3, f32[8,8]{1,0:T(8,128)S(1)} %copy-done.4, f32[8,16]{1,0:T(8,128)S(1)} %copy-done.5, f32[8,64,256]{2,1,0:T(8,128)S(1)} %copy-done, f32[8,4096]{1,0:T(8,128)S(1)} %copy-done.1, f32[8,80,256]{2,1,0:T(8,128)S(1)} %all-to-all-done.coupled), custom_call_target="tpu_custom_call" | custom-call | flops 4000000000 | bytes 1048576 | tf_op jit(solution)/shard_map/pallas_call | solution.py:121
  27.6 0.3 collective-permute-start.10
  27.8 0.3 collective-permute-start.12
  28.2 0.5 collective-permute-done.6.refs_6_
  28.7 0.5 collective-permute-start.8
  29.2 0.9 %copy-done.2 = f32[2,2,64,256]{3,2,1,0:T(8,128)S(1)} copy-done((f32[2,2,64,256]{3,2,1,0:T(8,128)S(1)}, f32[2,2,64,256]{3,2,1,0:T(8,128)}, u32[]{:S(2)}) %copy-start.2) | copy-done | bytes 262168
  30.2 7.1 %shard_map.75 = (bf16[32,128,128]{2,1,0:T(8,128)(2,1)S(1)}, bf16[32,128,256]{2,1,0:T(8,128)(2,1)S(1)}) custom-call(f32[8,64,256]{2,1,0:T(8,128)S(1)} %copy-done, f32[8,64,256]{2,1,0:T(8,128)S(1)} %collective-permute-done.1.refs_1_.refs_2_, f32[8,64,256]{2,1,0:T(8,128)S(1)} %collective-permute-done.2.refs_2_, ...), custom_call_target="tpu_custom_call" | custom-call | flops 4026531840 | bytes 1048576 | tf_op jit(solution)/shard_map/pallas_call | solution.py:251
  37.2 0.0 collective-permute-done.7.refs_4_
  37.3 0.6 %collective-permute-start.14 = (f32[8,40,128]{2,1,0:T(8,128)S(1)}, f32[8,40,128]{2,1,0:T(8,128)S(1)}, u32[]{:S(2)}, u32[]{:S(2)}) collective-permute-start(f32[8,40,128]{2,1,0:T(8,128)S(1)} %get-tuple-element.48.refs_7_), channel_id=1, source_target_pairs={{0,4},{4,0},{8,12},{12,8},{16,20},{20,16},{24,28},{28,24},{1,5},{5... | collective-permute-start | bytes 491528 | tf_op jit(solution)/shard_map/ppermute | solution.py:33
  37.9 0.0 collective-permute-done.9.refs_6_
  37.9 0.0 collective-permute-done.10.refs_7_
  37.9 0.0 collective-permute-done.8.refs_5_
  37.9 3.4 %shard_map.76 = f32[8,32,128]{2,1,0:T(8,128)S(1)} custom-call(bf16[32,128,128]{2,1,0:T(8,128)(2,1)S(1)} %get-tuple-element.53.refs_0_, bf16[32,128,256]{2,1,0:T(8,128)(2,1)S(1)} %get-tuple-element.54.refs_1_, f32[8,64,256]{2,1,0:T(8,128)} %collective-permute-done.5.refs_3_.refs_2_, f32[2,2,64,256]{3,2,1,0:T(8,128)S(1)} %collective-permute-done.refs_3_, ...), custom_call_target="tpu_custom_call" | custom-call | flops 1107296256 | bytes 1048576 | tf_op jit(solution)/shard_map/pallas_call | solution.py:323
  41.3 0.0 collective-permute-done.12.refs_7_
  41.3 2.4 %shard_map.77 = f32[8,32,128]{2,1,0:T(8,128)S(1)} custom-call(bf16[32,128,128]{2,1,0:T(8,128)(2,1)S(1)} %get-tuple-element.53.refs_0_, bf16[32,128,256]{2,1,0:T(8,128)(2,1)S(1)} %get-tuple-element.54.refs_1_, f32[8,64,256]{2,1,0:T(8,128)S(1)} %collective-permute-done.2.refs_2_, f32[2,2,64,256]{3,2,1,0:T(8,128)S(1)} %collective-permute-done.refs_3_, ...), custom_call_target="tpu_custom_call" | custom-call | flops 1107296256 | bytes 1048576 | tf_op jit(solution)/shard_map/pallas_call | solution.py:323
  43.7 0.6 %collective-permute-start.13 = (f32[8,32,128]{2,1,0:T(8,128)S(1)}, f32[8,32,128]{2,1,0:T(8,128)S(1)}, u32[]{:S(2)}, u32[]{:S(2)}) collective-permute-start(f32[8,32,128]{2,1,0:T(8,128)S(1)} %shard_map.77), channel_id=1, source_target_pairs={{0,8},{4,12},{8,0},{12,4},{16,24},{20,28},{24,16},{28,20},{1,9},{5... | collective-permute-start | bytes 393224 | tf_op jit(solution)/shard_map/ppermute | solution.py:33
  44.3 0.8 %collective-permute-start.11 = (f32[8,32,128]{2,1,0:T(8,128)S(1)}, f32[8,32,128]{2,1,0:T(8,128)S(1)}, u32[]{:S(2)}, u32[]{:S(2)}) collective-permute-start(f32[8,32,128]{2,1,0:T(8,128)S(1)} %shard_map.76), channel_id=1, source_target_pairs={{0,12},{4,8},{8,4},{12,0},{16,28},{20,24},{24,20},{28,16},{1,13},{... | collective-permute-start | bytes 393224 | tf_op jit(solution)/shard_map/ppermute | solution.py:33
  45.1 0.0 collective-permute-done.14.refs_7_
  45.1 2.5 %shard_map.78 = f32[8,32,128]{2,1,0:T(8,128)S(1)} custom-call(bf16[32,128,128]{2,1,0:T(8,128)(2,1)S(1)} %get-tuple-element.53.refs_0_, bf16[32,128,256]{2,1,0:T(8,128)(2,1)S(1)} %get-tuple-element.54.refs_1_, f32[8,64,256]{2,1,0:T(8,128)S(1)} %collective-permute-done.1.refs_1_.refs_2_, f32[2,2,64,256]{3,2,1,0:T(8,128)S(1)} %collective-permute-done.refs_3_, ...), custom_call_target="tpu_custom_call" | custom-call | flops 1107296256 | bytes 1048576 | tf_op jit(solution)/shard_map/pallas_call | solution.py:323
  47.7 0.9 %collective-permute-start.15 = (f32[8,32,128]{2,1,0:T(8,128)S(1)}, f32[8,32,128]{2,1,0:T(8,128)S(1)}, u32[]{:S(2)}, u32[]{:S(2)}) collective-permute-start(f32[8,32,128]{2,1,0:T(8,128)S(1)} %shard_map.78), channel_id=1, source_target_pairs={{0,4},{4,0},{8,12},{12,8},{16,20},{20,16},{24,28},{28,24},{1,5},{5... | collective-permute-start | bytes 393224 | tf_op jit(solution)/shard_map/ppermute | solution.py:33
  48.5 2.3 %shard_map.79 = f32[8,32,128]{2,1,0:T(8,128)S(1)} custom-call(bf16[32,128,128]{2,1,0:T(8,128)(2,1)S(1)} %get-tuple-element.53.refs_0_, bf16[32,128,256]{2,1,0:T(8,128)(2,1)S(1)} %get-tuple-element.54.refs_1_, f32[8,64,256]{2,1,0:T(8,128)S(1)} %copy-done, f32[2,2,64,256]{3,2,1,0:T(8,128)S(1)} %collective-permute-done.refs_3_, ...), custom_call_target="tpu_custom_call" | custom-call | flops 1107296256 | bytes 1048576 | tf_op jit(solution)/shard_map/pallas_call | solution.py:323
  50.9 0.0 collective-permute-done.13
  50.9 0.1 collective-permute-done.11
  51.0 0.0 collective-permute-done.15
  51.1 0.7 %copy.10 = f32[1,8,32,128]{3,1,2,0:T(8,128)} copy(f32[1,8,32,128]{3,2,1,0:T(8,128)S(1)} %add_bitcast_fusion) | data formatting | bytes 262144
  (8 shorter events, 0.1 us)
Async XLA Ops:
  0.0 14.6 %copy-start = (f32[8,64,256]{2,1,0:T(8,128)S(1)}, f32[8,64,256]{2,1,0:T(8,128)}, u32[]{:S(2)}) copy-start(f32[8,64,256]{2,1,0:T(8,128)} %refs_2_) | copy-start | bytes 1572868
  0.0 25.7 %copy-start.1 = (f32[8,4096]{1,0:T(8,128)S(1)}, f32[8,4096]{1,0:T(8,128)}, u32[]{:S(2)}) copy-start(f32[8,4096]{1,0:T(8,128)} %amps.3) | copy-start | bytes 393220
  0.0 25.7 %copy-start.3 = (s32[8,8]{1,0:T(8,128)S(1)}, s32[8,8]{1,0:T(8,128)}, u32[]{:S(2)}) copy-start(s32[8,8]{1,0:T(8,128)} %couple.1) | copy-start | bytes 772
  0.0 25.8 %copy-start.4 = (f32[8,8]{1,0:T(8,128)S(1)}, f32[8,8]{1,0:T(8,128)}, u32[]{:S(2)}) copy-start(f32[8,8]{1,0:T(8,128)} %couple_weight.1) | copy-start | bytes 772
  0.0 25.8 %copy-start.5 = (f32[8,16]{1,0:T(8,128)S(1)}, f32[8,16]{1,0:T(8,128)}, u32[]{:S(2)}) copy-start(f32[8,16]{1,0:T(8,128)} %fit_weight.1) | copy-start | bytes 1540
  0.0 19.3 %collective-permute-start.2 = (f32[8,64,256]{2,1,0:T(8,128)}, f32[8,64,256]{2,1,0:T(8,128)S(1)}, u32[]{:S(2)}, u32[]{:S(2)}) collective-permute-start(f32[8,64,256]{2,1,0:T(8,128)} %refs_2_), channel_id=1, source_target_pairs={{0,8},{4,12},{8,0},{12,4},{16,24},{20,28},{24,16},{28,20},{1,9},{5... | collective-permute-start | bytes 1572872 | tf_op jit(solution)/shard_map/ppermute | solution.py:33
  3.0 8.0 %collective-permute-start = (f32[2,2,64,256]{3,2,1,0:T(8,128)}, f32[2,2,64,256]{3,2,1,0:T(8,128)S(1)}, u32[]{:S(2)}, u32[]{:S(2)}) collective-permute-start(f32[2,2,64,256]{3,2,1,0:T(8,128)} %refs_4_.1), channel_id=1, source_target_pairs={{0,16},{4,20},{8,24},{12,28},{16,0},{20,4},{24,8},{28,12},{1,17},{... | collective-permute-start | bytes 786440 | tf_op jit(solution)/shard_map/ppermute | solution.py:38
  4.6 11.4 %collective-permute-start.3 = (f32[2,2,64,256]{3,2,1,0:T(8,128)}, f32[2,2,64,256]{3,2,1,0:T(8,128)}, u32[]{:S(2)}, u32[]{:S(2)}) collective-permute-start(f32[2,2,64,256]{3,2,1,0:T(8,128)} %refs_4_.1), channel_id=1, source_target_pairs={{0,1},{1,2},{2,3},{3,0},{4,5},{5,6},{6,7},{7,4},{8,9},{9,10},{10,1... | collective-permute-start | bytes 786440 | tf_op jit(solution)/shard_map/ppermute | solution.py:38
  6.1 13.1 %collective-permute-start.4 = (f32[2,2,64,256]{3,2,1,0:T(8,128)}, f32[2,2,64,256]{3,2,1,0:T(8,128)}, u32[]{:S(2)}, u32[]{:S(2)}) collective-permute-start(f32[2,2,64,256]{3,2,1,0:T(8,128)} %refs_4_.1), channel_id=1, source_target_pairs={{0,3},{1,0},{2,1},{3,2},{4,7},{5,4},{6,5},{7,6},{8,11},{9,8},{10,9... | collective-permute-start | bytes 786440 | tf_op jit(solution)/shard_map/ppermute | solution.py:38
  11.0 14.7 %all-to-all-start = ((f32[8,80,256]{2,1,0:T(8,128)}), f32[8,80,256]{2,1,0:T(8,128)S(1)}, u32[]{:S(2)}, u32[]{:S(2)}) async-start(f32[8,80,256]{2,1,0:T(8,128)} %shard_map.73), calls=%async_computation | async-start | bytes 1310720 | tf_op jit(solution)/shard_map/all_to_all | solution.py:362
  14.6 8.0 %collective-permute-start.1 = (f32[8,64,256]{2,1,0:T(8,128)S(1)}, f32[8,64,256]{2,1,0:T(8,128)S(1)}, u32[]{:S(2)}, u32[]{:S(2)}) collective-permute-start(f32[8,64,256]{2,1,0:T(8,128)S(1)} %copy-done), channel_id=1, source_target_pairs={{0,4},{4,0},{8,12},{12,8},{16,20},{20,16},{24,28},{28,24},{1,5},{5... | collective-permute-start | bytes 1572872 | tf_op jit(solution)/shard_map/ppermute | solution.py:33
  19.3 6.5 %collective-permute-start.5 = (f32[8,64,256]{2,1,0:T(8,128)S(1)}, f32[8,64,256]{2,1,0:T(8,128)}, u32[]{:S(2)}, u32[]{:S(2)}) collective-permute-start(f32[8,64,256]{2,1,0:T(8,128)S(1)} %collective-permute-done.2.refs_2_), channel_id=1, source_target_pairs={{0,4},{4,0},{8,12},{12,8},{16,20},{20,16},{24,28},{28,24},{1,5},{5... | collective-permute-start | bytes 1572872 | tf_op jit(solution)/shard_map/ppermute | solution.py:33
  19.3 9.4 %collective-permute-start.6 = (f32[2,2,64,256]{3,2,1,0:T(8,128)}, f32[2,2,64,256]{3,2,1,0:T(8,128)}, u32[]{:S(2)}, u32[]{:S(2)}) collective-permute-start(f32[2,2,64,256]{3,2,1,0:T(8,128)} %collective-permute-done.4.refs_7_), channel_id=1, source_target_pairs={{0,3},{1,0},{2,1},{3,2},{4,7},{5,4},{6,5},{7,6},{8,11},{9,8},{10,9... | collective-permute-start | bytes 786440 | tf_op jit(solution)/shard_map/ppermute | solution.py:38
  21.6 15.6 %collective-permute-start.7 = (f32[2,2,64,256]{3,2,1,0:T(8,128)}, f32[2,2,64,256]{3,2,1,0:T(8,128)S(1)}, u32[]{:S(2)}, u32[]{:S(2)}) collective-permute-start(f32[2,2,64,256]{3,2,1,0:T(8,128)} %collective-permute-done.3.refs_5_), channel_id=1, source_target_pairs={{0,16},{4,20},{8,24},{12,28},{16,0},{20,4},{24,8},{28,12},{1,17},{... | collective-permute-start | bytes 786440 | tf_op jit(solution)/shard_map/ppermute | solution.py:38
  22.2 15.7 %collective-permute-start.9 = (f32[2,2,64,256]{3,2,1,0:T(8,128)S(1)}, f32[2,2,64,256]{3,2,1,0:T(8,128)S(1)}, u32[]{:S(2)}, u32[]{:S(2)}) collective-permute-start(f32[2,2,64,256]{3,2,1,0:T(8,128)S(1)} %collective-permute-done.refs_3_), channel_id=1, source_target_pairs={{0,3},{1,0},{2,1},{3,2},{4,7},{5,4},{6,5},{7,6},{8,11},{9,8},{10,9... | collective-permute-start | bytes 786440 | tf_op jit(solution)/shard_map/ppermute | solution.py:38
  27.6 10.3 %collective-permute-start.10 = (f32[8,40,128]{2,1,0:T(8,128)S(1)}, f32[8,40,128]{2,1,0:T(8,128)S(1)}, u32[]{:S(2)}, u32[]{:S(2)}) collective-permute-start(f32[8,40,128]{2,1,0:T(8,128)S(1)} %get-tuple-element.48.refs_7_), channel_id=1, source_target_pairs={{0,12},{4,8},{8,4},{12,0},{16,28},{20,24},{24,20},{28,16},{1,13},{... | collective-permute-start | bytes 491528 | tf_op jit(solution)/shard_map/ppermute | solution.py:33
  27.8 13.5 %collective-permute-start.12 = (f32[8,40,128]{2,1,0:T(8,128)S(1)}, f32[8,40,128]{2,1,0:T(8,128)S(1)}, u32[]{:S(2)}, u32[]{:S(2)}) collective-permute-start(f32[8,40,128]{2,1,0:T(8,128)S(1)} %get-tuple-element.48.refs_7_), channel_id=1, source_target_pairs={{0,8},{4,12},{8,0},{12,4},{16,24},{20,28},{24,16},{28,20},{1,9},{5... | collective-permute-start | bytes 491528 | tf_op jit(solution)/shard_map/ppermute | solution.py:33
  28.7 9.2 %collective-permute-start.8 = (f32[2,2,64,256]{3,2,1,0:T(8,128)}, f32[2,2,64,256]{3,2,1,0:T(8,128)S(1)}, u32[]{:S(2)}, u32[]{:S(2)}) collective-permute-start(f32[2,2,64,256]{3,2,1,0:T(8,128)} %collective-permute-done.6.refs_6_), channel_id=1, source_target_pairs={{0,16},{4,20},{8,24},{12,28},{16,0},{20,4},{24,8},{28,12},{1,17},{... | collective-permute-start | bytes 786440 | tf_op jit(solution)/shard_map/ppermute | solution.py:38
  29.2 0.9 %copy-start.2 = (f32[2,2,64,256]{3,2,1,0:T(8,128)S(1)}, f32[2,2,64,256]{3,2,1,0:T(8,128)}, u32[]{:S(2)}) copy-start(f32[2,2,64,256]{3,2,1,0:T(8,128)} %refs_4_.1) | copy-start | bytes 786436
  37.3 7.9 %collective-permute-start.14 = (f32[8,40,128]{2,1,0:T(8,128)S(1)}, f32[8,40,128]{2,1,0:T(8,128)S(1)}, u32[]{:S(2)}, u32[]{:S(2)}) collective-permute-start(f32[8,40,128]{2,1,0:T(8,128)S(1)} %get-tuple-element.48.refs_7_), channel_id=1, source_target_pairs={{0,4},{4,0},{8,12},{12,8},{16,20},{20,16},{24,28},{28,24},{1,5},{5... | collective-permute-start | bytes 491528 | tf_op jit(solution)/shard_map/ppermute | solution.py:33
  43.7 7.2 %collective-permute-start.13 = (f32[8,32,128]{2,1,0:T(8,128)S(1)}, f32[8,32,128]{2,1,0:T(8,128)S(1)}, u32[]{:S(2)}, u32[]{:S(2)}) collective-permute-start(f32[8,32,128]{2,1,0:T(8,128)S(1)} %shard_map.77), channel_id=1, source_target_pairs={{0,8},{4,12},{8,0},{12,4},{16,24},{20,28},{24,16},{28,20},{1,9},{5... | collective-permute-start | bytes 393224 | tf_op jit(solution)/shard_map/ppermute | solution.py:33
  44.3 6.7 %collective-permute-start.11 = (f32[8,32,128]{2,1,0:T(8,128)S(1)}, f32[8,32,128]{2,1,0:T(8,128)S(1)}, u32[]{:S(2)}, u32[]{:S(2)}) collective-permute-start(f32[8,32,128]{2,1,0:T(8,128)S(1)} %shard_map.76), channel_id=1, source_target_pairs={{0,12},{4,8},{8,4},{12,0},{16,28},{20,24},{24,20},{28,16},{1,13},{... | collective-permute-start | bytes 393224 | tf_op jit(solution)/shard_map/ppermute | solution.py:33
  47.7 3.4 %collective-permute-start.15 = (f32[8,32,128]{2,1,0:T(8,128)S(1)}, f32[8,32,128]{2,1,0:T(8,128)S(1)}, u32[]{:S(2)}, u32[]{:S(2)}) collective-permute-start(f32[8,32,128]{2,1,0:T(8,128)S(1)} %shard_map.78), channel_id=1, source_target_pairs={{0,4},{4,0},{8,12},{12,8},{16,20},{20,16},{24,28},{28,24},{1,5},{5... | collective-permute-start | bytes 393224 | tf_op jit(solution)/shard_map/ppermute | solution.py:33

commit v5 on v4

--- a/solution.py
+++ b/solution.py
@@ -254,7 +254,7 @@
         in_specs=vmem(len(bases) + len(pieces)),
         out_specs=tuple(vmem(2)),
         scratch_shapes=project_scratch(bases, pieces),
-        compiler_params=pltpu.CompilerParams(vmem_limit_bytes=28 * 2**20),
+        compiler_params=pltpu.CompilerParams(vmem_limit_bytes=24 * 2**20),
         cost_estimate=pl.CostEstimate(flops=project_flops(bases, pieces), bytes_accessed=2**20, transcendentals=0),
     )(*bases, *pieces)
 
@@ -332,7 +332,7 @@
             pltpu.VMEM((pairs, pno_count, lane_count), jnp.float32),
             *project_scratch(bases, pieces),
         ],
-        compiler_params=pltpu.CompilerParams(vmem_limit_bytes=24 * 2**20),
+        compiler_params=pltpu.CompilerParams(vmem_limit_bytes=14 * 2**20),
         cost_estimate=pl.CostEstimate(
             flops=project_flops(bases, pieces) + 6 * products, bytes_accessed=2**20, transcendentals=0
         ),

time: 52.5 us -> 52.5 us (level)
  no operation moved by 1% of the time
where the time goes in v5:
time: 52.5 us; the launch traced here: 51.8 us
  Pallas kernels  21.5 us (41%)
  starting transfers between devices  19.6 us (37%)
  waiting for transfers between devices  8.74 us (17%)
  local copies, waits for them, and re-layouts  1.7 us (3%)
    pallas_call x4, Pallas kernels, finish(): pl.pallas_call(lambda *refs: finish_kernel(members, group_count, len(piec...  10.6 us
    ppermute x7, starting transfers between devices, from_behind(): return lax.ppermute(x, axis, [(i, (i + by) % count) for i in range(count)])  9.17 us
    pallas_call x1, Pallas kernels, project(): pl.pallas_call(lambda *refs: project_kernel(len(bases), *refs), out_shape...  7.08 us
    ppermute x9, starting transfers between devices, from_partner(): lax.ppermute(x, axis, [(i, i ^ flip) for i in range(lax.axis_size(axis))])  6.93 us
    ppermute x7, waiting for transfers between devices, from_behind(): return lax.ppermute(x, axis, [(i, (i + by) % count) for i in range(count)])  5.45 us
    all_to_all x1, starting transfers between devices, on_device_shared(): lax.all_to_all(sent, 'blk', split_axis=0, concat_axis=0, tiled=True)  3.54 us
    all_to_all x1, waiting for transfers between devices, on_device_shared(): lax.all_to_all(sent, 'blk', split_axis=0, concat_axis=0, tiled=True)  3.14 us
    pallas_call x1, Pallas kernels, pack_pairs(): pl.pallas_call(pack_kernel, out_shape=jax.ShapeDtypeStruct((send_order.sh...  2.03 us
  transfers between devices with their start and end apart: 17, of which 6 were waited for; matrix products, arithmetic and copies ran while one was open for 0% of the time, Pallas kernels for 42%

profile of v5, /device:TPU:0, one launch (start us, length us, event | category | flops | bytes accessed | tf_op | source)
XLA Modules:
  0.0 51.8 jit_solution(7515848737991318011)
XLA Ops:
  0.0 3.0 %collective-permute-start.2 = (f32[8,64,256]{2,1,0:T(8,128)}, f32[8,64,256]{2,1,0:T(8,128)S(1)}, u32[]{:S(2)}, u32[]{:S(2)}) collective-permute-start(f32[8,64,256]{2,1,0:T(8,128)} %refs_2_), channel_id=1, source_target_pairs={{0,8},{4,12},{8,0},{12,4},{16,24},{20,28},{24,16},{28,20},{1,9},{5... | collective-permute-start | bytes 1572872 | tf_op jit(solution)/shard_map/ppermute | solution.py:33
  3.0 1.5 %collective-permute-start = (f32[2,2,64,256]{3,2,1,0:T(8,128)}, f32[2,2,64,256]{3,2,1,0:T(8,128)S(1)}, u32[]{:S(2)}, u32[]{:S(2)}) collective-permute-start(f32[2,2,64,256]{3,2,1,0:T(8,128)} %refs_4_.1), channel_id=1, source_target_pairs={{0,16},{4,20},{8,24},{12,28},{16,0},{20,4},{24,8},{28,12},{1,17},{... | collective-permute-start | bytes 786440 | tf_op jit(solution)/shard_map/ppermute | solution.py:38
  4.6 1.6 %collective-permute-start.3 = (f32[2,2,64,256]{3,2,1,0:T(8,128)}, f32[2,2,64,256]{3,2,1,0:T(8,128)}, u32[]{:S(2)}, u32[]{:S(2)}) collective-permute-start(f32[2,2,64,256]{3,2,1,0:T(8,128)} %refs_4_.1), channel_id=1, source_target_pairs={{0,1},{1,2},{2,3},{3,0},{4,5},{5,6},{6,7},{7,4},{8,9},{9,10},{10,1... | collective-permute-start | bytes 786440 | tf_op jit(solution)/shard_map/ppermute | solution.py:38
  6.1 2.2 %collective-permute-start.4 = (f32[2,2,64,256]{3,2,1,0:T(8,128)}, f32[2,2,64,256]{3,2,1,0:T(8,128)}, u32[]{:S(2)}, u32[]{:S(2)}) collective-permute-start(f32[2,2,64,256]{3,2,1,0:T(8,128)} %refs_4_.1), channel_id=1, source_target_pairs={{0,3},{1,0},{2,1},{3,2},{4,7},{5,4},{6,5},{7,6},{8,11},{9,8},{10,9... | collective-permute-start | bytes 786440 | tf_op jit(solution)/shard_map/ppermute | solution.py:38
  8.4 2.0 %shard_map.73 = f32[8,80,256]{2,1,0:T(8,128)} custom-call(s32[8]{0:T(128)} %bitcast.6, f32[8,64,256]{2,1,0:T(8,128)} %refs_2_, f32[8,4096]{1,0:T(8,128)} %amps.3), custom_call_target="tpu_custom_call" | custom-call | bytes 524288 | tf_op jit(solution)/shard_map/pallas_call | solution.py:59
  10.4 0.6 %collective-permute-done.refs_3_ = f32[2,2,64,256]{3,2,1,0:T(8,128)S(1)} collective-permute-done((f32[2,2,64,256]{3,2,1,0:T(8,128)}, f32[2,2,64,256]{3,2,1,0:T(8,128)S(1)}, u32[]{:S(2)}, u32[]{:S(2)}) %collective-permute-start) | collective-permute-done | bytes 262176 | tf_op jit(solution)/shard_map/ppermute | solution.py:38
  11.0 3.5 %all-to-all-start = ((f32[8,80,256]{2,1,0:T(8,128)}), f32[8,80,256]{2,1,0:T(8,128)S(1)}, u32[]{:S(2)}, u32[]{:S(2)}) async-start(f32[8,80,256]{2,1,0:T(8,128)} %shard_map.73), calls=%async_computation | async-start | bytes 1310720 | tf_op jit(solution)/shard_map/all_to_all | solution.py:362
  14.6 0.0 copy-done
  14.6 0.4 collective-permute-start.1
  15.0 1.0 %collective-permute-done.3.refs_5_ = f32[2,2,64,256]{3,2,1,0:T(8,128)} collective-permute-done((f32[2,2,64,256]{3,2,1,0:T(8,128)}, f32[2,2,64,256]{3,2,1,0:T(8,128)}, u32[]{:S(2)}, u32[]{:S(2)}) %collective-permute-start.3) | collective-permute-done | bytes 262176 | tf_op jit(solution)/shard_map/ppermute | solution.py:38
  16.0 3.3 %collective-permute-done.4.refs_7_ = f32[2,2,64,256]{3,2,1,0:T(8,128)} collective-permute-done((f32[2,2,64,256]{3,2,1,0:T(8,128)}, f32[2,2,64,256]{3,2,1,0:T(8,128)}, u32[]{:S(2)}, u32[]{:S(2)}) %collective-permute-start.4) | collective-permute-done | bytes 262176 | tf_op jit(solution)/shard_map/ppermute | solution.py:38
  19.3 0.0 collective-permute-done.2.refs_2_
  19.3 0.0 collective-permute-start.5
  19.3 2.4 %collective-permute-start.6 = (f32[2,2,64,256]{3,2,1,0:T(8,128)}, f32[2,2,64,256]{3,2,1,0:T(8,128)}, u32[]{:S(2)}, u32[]{:S(2)}) collective-permute-start(f32[2,2,64,256]{3,2,1,0:T(8,128)} %collective-permute-done.4.refs_7_), channel_id=1, source_target_pairs={{0,3},{1,0},{2,1},{3,2},{4,7},{5,4},{6,5},{7,6},{8,11},{9,8},{10,9... | collective-permute-start | bytes 786440 | tf_op jit(solution)/shard_map/ppermute | solution.py:38
  21.6 0.5 collective-permute-start.7
  22.2 0.4 collective-permute-start.9
  22.6 0.0 collective-permute-done.1.refs_1_.refs_2_
  22.6 3.1 %all-to-all-done.coupled = f32[8,80,256]{2,1,0:T(8,128)S(1)} async-done(((f32[8,80,256]{2,1,0:T(8,128)}), f32[8,80,256]{2,1,0:T(8,128)S(1)}, u32[]{:S(2)}, u32[]{:S(2)}) %all-to-all-start) | async-done | bytes 655392 | tf_op jit(solution)/shard_map/all_to_all | solution.py:362
  25.7 0.0 collective-permute-done.5.refs_3_.refs_2_
  25.7 0.0 copy-done.1
  25.7 0.0 copy-done.3
  25.8 0.0 copy-done.4
  25.8 0.0 copy-done.5
  25.8 1.8 %shard_map.74 = (f32[8,40,128]{2,1,0:T(8,128)S(1)}, f32[8,32,128]{2,1,0:T(8,128)S(1)}) custom-call(s32[8,8]{1,0:T(8,128)S(1)} %copy-done.3, f32[8,8]{1,0:T(8,128)S(1)} %copy-done.4, f32[8,16]{1,0:T(8,128)S(1)} %copy-done.5, f32[8,64,256]{2,1,0:T(8,128)S(1)} %copy-done, f32[8,4096]{1,0:T(8,128)S(1)} %copy-done.1, f32[8,80,256]{2,1,0:T(8,128)S(1)} %all-to-all-done.coupled), custom_call_target="tpu_custom_call" | custom-call | flops 4000000000 | bytes 1048576 | tf_op jit(solution)/shard_map/pallas_call | solution.py:121
  27.6 0.3 collective-permute-start.10
  27.8 0.3 collective-permute-start.12
  28.2 0.5 collective-permute-done.6.refs_6_
  28.7 0.5 collective-permute-start.8
  29.2 0.9 %copy-done.2 = f32[2,2,64,256]{3,2,1,0:T(8,128)S(1)} copy-done((f32[2,2,64,256]{3,2,1,0:T(8,128)S(1)}, f32[2,2,64,256]{3,2,1,0:T(8,128)}, u32[]{:S(2)}) %copy-start.2) | copy-done | bytes 262168
  30.2 7.1 %shard_map.75 = (bf16[32,128,128]{2,1,0:T(8,128)(2,1)S(1)}, bf16[32,128,256]{2,1,0:T(8,128)(2,1)S(1)}) custom-call(f32[8,64,256]{2,1,0:T(8,128)S(1)} %copy-done, f32[8,64,256]{2,1,0:T(8,128)S(1)} %collective-permute-done.1.refs_1_.refs_2_, f32[8,64,256]{2,1,0:T(8,128)S(1)} %collective-permute-done.2.refs_2_, ...), custom_call_target="tpu_custom_call" | custom-call | flops 4026531840 | bytes 1048576 | tf_op jit(solution)/shard_map/pallas_call | solution.py:251
  37.2 0.0 collective-permute-done.7.refs_4_
  37.3 0.6 %collective-permute-start.14 = (f32[8,40,128]{2,1,0:T(8,128)S(1)}, f32[8,40,128]{2,1,0:T(8,128)S(1)}, u32[]{:S(2)}, u32[]{:S(2)}) collective-permute-start(f32[8,40,128]{2,1,0:T(8,128)S(1)} %get-tuple-element.48.refs_7_), channel_id=1, source_target_pairs={{0,4},{4,0},{8,12},{12,8},{16,20},{20,16},{24,28},{28,24},{1,5},{5... | collective-permute-start | bytes 491528 | tf_op jit(solution)/shard_map/ppermute | solution.py:33
  37.9 0.0 collective-permute-done.9.refs_6_
  37.9 0.0 collective-permute-done.10.refs_7_
  37.9 0.0 collective-permute-done.8.refs_5_
  37.9 3.4 %shard_map.76 = f32[8,32,128]{2,1,0:T(8,128)S(1)} custom-call(bf16[32,128,128]{2,1,0:T(8,128)(2,1)S(1)} %get-tuple-element.53.refs_0_, bf16[32,128,256]{2,1,0:T(8,128)(2,1)S(1)} %get-tuple-element.54.refs_1_, f32[8,64,256]{2,1,0:T(8,128)} %collective-permute-done.5.refs_3_.refs_2_, f32[2,2,64,256]{3,2,1,0:T(8,128)S(1)} %collective-permute-done.refs_3_, ...), custom_call_target="tpu_custom_call" | custom-call | flops 1107296256 | bytes 1048576 | tf_op jit(solution)/shard_map/pallas_call | solution.py:323
  41.3 0.0 collective-permute-done.12.refs_7_
  41.3 2.4 %shard_map.77 = f32[8,32,128]{2,1,0:T(8,128)S(1)} custom-call(bf16[32,128,128]{2,1,0:T(8,128)(2,1)S(1)} %get-tuple-element.53.refs_0_, bf16[32,128,256]{2,1,0:T(8,128)(2,1)S(1)} %get-tuple-element.54.refs_1_, f32[8,64,256]{2,1,0:T(8,128)S(1)} %collective-permute-done.2.refs_2_, f32[2,2,64,256]{3,2,1,0:T(8,128)S(1)} %collective-permute-done.refs_3_, ...), custom_call_target="tpu_custom_call" | custom-call | flops 1107296256 | bytes 1048576 | tf_op jit(solution)/shard_map/pallas_call | solution.py:323
  43.7 0.6 %collective-permute-start.13 = (f32[8,32,128]{2,1,0:T(8,128)S(1)}, f32[8,32,128]{2,1,0:T(8,128)S(1)}, u32[]{:S(2)}, u32[]{:S(2)}) collective-permute-start(f32[8,32,128]{2,1,0:T(8,128)S(1)} %shard_map.77), channel_id=1, source_target_pairs={{0,8},{4,12},{8,0},{12,4},{16,24},{20,28},{24,16},{28,20},{1,9},{5... | collective-permute-start | bytes 393224 | tf_op jit(solution)/shard_map/ppermute | solution.py:33
  44.3 0.8 %collective-permute-start.11 = (f32[8,32,128]{2,1,0:T(8,128)S(1)}, f32[8,32,128]{2,1,0:T(8,128)S(1)}, u32[]{:S(2)}, u32[]{:S(2)}) collective-permute-start(f32[8,32,128]{2,1,0:T(8,128)S(1)} %shard_map.76), channel_id=1, source_target_pairs={{0,12},{4,8},{8,4},{12,0},{16,28},{20,24},{24,20},{28,16},{1,13},{... | collective-permute-start | bytes 393224 | tf_op jit(solution)/shard_map/ppermute | solution.py:33
  45.1 0.0 collective-permute-done.14.refs_7_
  45.1 2.5 %shard_map.78 = f32[8,32,128]{2,1,0:T(8,128)S(1)} custom-call(bf16[32,128,128]{2,1,0:T(8,128)(2,1)S(1)} %get-tuple-element.53.refs_0_, bf16[32,128,256]{2,1,0:T(8,128)(2,1)S(1)} %get-tuple-element.54.refs_1_, f32[8,64,256]{2,1,0:T(8,128)S(1)} %collective-permute-done.1.refs_1_.refs_2_, f32[2,2,64,256]{3,2,1,0:T(8,128)S(1)} %collective-permute-done.refs_3_, ...), custom_call_target="tpu_custom_call" | custom-call | flops 1107296256 | bytes 1048576 | tf_op jit(solution)/shard_map/pallas_call | solution.py:323
  47.7 0.9 %collective-permute-start.15 = (f32[8,32,128]{2,1,0:T(8,128)S(1)}, f32[8,32,128]{2,1,0:T(8,128)S(1)}, u32[]{:S(2)}, u32[]{:S(2)}) collective-permute-start(f32[8,32,128]{2,1,0:T(8,128)S(1)} %shard_map.78), channel_id=1, source_target_pairs={{0,4},{4,0},{8,12},{12,8},{16,20},{20,16},{24,28},{28,24},{1,5},{5... | collective-permute-start | bytes 393224 | tf_op jit(solution)/shard_map/ppermute | solution.py:33
  48.5 2.3 %shard_map.79 = f32[8,32,128]{2,1,0:T(8,128)S(1)} custom-call(bf16[32,128,128]{2,1,0:T(8,128)(2,1)S(1)} %get-tuple-element.53.refs_0_, bf16[32,128,256]{2,1,0:T(8,128)(2,1)S(1)} %get-tuple-element.54.refs_1_, f32[8,64,256]{2,1,0:T(8,128)S(1)} %copy-done, f32[2,2,64,256]{3,2,1,0:T(8,128)S(1)} %collective-permute-done.refs_3_, ...), custom_call_target="tpu_custom_call" | custom-call | flops 1107296256 | bytes 1048576 | tf_op jit(solution)/shard_map/pallas_call | solution.py:323
  50.9 0.0 collective-permute-done.13
  50.9 0.1 collective-permute-done.11
  51.0 0.0 collective-permute-done.15
  51.1 0.7 %copy.10 = f32[1,8,32,128]{3,1,2,0:T(8,128)} copy(f32[1,8,32,128]{3,2,1,0:T(8,128)S(1)} %add_bitcast_fusion) | data formatting | bytes 262144
  (8 shorter events, 0.1 us)
Async XLA Ops:
  0.0 14.6 %copy-start = (f32[8,64,256]{2,1,0:T(8,128)S(1)}, f32[8,64,256]{2,1,0:T(8,128)}, u32[]{:S(2)}) copy-start(f32[8,64,256]{2,1,0:T(8,128)} %refs_2_) | copy-start | bytes 1572868
  0.0 25.7 %copy-start.1 = (f32[8,4096]{1,0:T(8,128)S(1)}, f32[8,4096]{1,0:T(8,128)}, u32[]{:S(2)}) copy-start(f32[8,4096]{1,0:T(8,128)} %amps.3) | copy-start | bytes 393220
  0.0 25.7 %copy-start.3 = (s32[8,8]{1,0:T(8,128)S(1)}, s32[8,8]{1,0:T(8,128)}, u32[]{:S(2)}) copy-start(s32[8,8]{1,0:T(8,128)} %couple.1) | copy-start | bytes 772
  0.0 25.8 %copy-start.4 = (f32[8,8]{1,0:T(8,128)S(1)}, f32[8,8]{1,0:T(8,128)}, u32[]{:S(2)}) copy-start(f32[8,8]{1,0:T(8,128)} %couple_weight.1) | copy-start | bytes 772
  0.0 25.8 %copy-start.5 = (f32[8,16]{1,0:T(8,128)S(1)}, f32[8,16]{1,0:T(8,128)}, u32[]{:S(2)}) copy-start(f32[8,16]{1,0:T(8,128)} %fit_weight.1) | copy-start | bytes 1540
  0.0 19.3 %collective-permute-start.2 = (f32[8,64,256]{2,1,0:T(8,128)}, f32[8,64,256]{2,1,0:T(8,128)S(1)}, u32[]{:S(2)}, u32[]{:S(2)}) collective-permute-start(f32[8,64,256]{2,1,0:T(8,128)} %refs_2_), channel_id=1, source_target_pairs={{0,8},{4,12},{8,0},{12,4},{16,24},{20,28},{24,16},{28,20},{1,9},{5... | collective-permute-start | bytes 1572872 | tf_op jit(solution)/shard_map/ppermute | solution.py:33
  3.0 8.0 %collective-permute-start = (f32[2,2,64,256]{3,2,1,0:T(8,128)}, f32[2,2,64,256]{3,2,1,0:T(8,128)S(1)}, u32[]{:S(2)}, u32[]{:S(2)}) collective-permute-start(f32[2,2,64,256]{3,2,1,0:T(8,128)} %refs_4_.1), channel_id=1, source_target_pairs={{0,16},{4,20},{8,24},{12,28},{16,0},{20,4},{24,8},{28,12},{1,17},{... | collective-permute-start | bytes 786440 | tf_op jit(solution)/shard_map/ppermute | solution.py:38
  4.6 11.4 %collective-permute-start.3 = (f32[2,2,64,256]{3,2,1,0:T(8,128)}, f32[2,2,64,256]{3,2,1,0:T(8,128)}, u32[]{:S(2)}, u32[]{:S(2)}) collective-permute-start(f32[2,2,64,256]{3,2,1,0:T(8,128)} %refs_4_.1), channel_id=1, source_target_pairs={{0,1},{1,2},{2,3},{3,0},{4,5},{5,6},{6,7},{7,4},{8,9},{9,10},{10,1... | collective-permute-start | bytes 786440 | tf_op jit(solution)/shard_map/ppermute | solution.py:38
  6.1 13.1 %collective-permute-start.4 = (f32[2,2,64,256]{3,2,1,0:T(8,128)}, f32[2,2,64,256]{3,2,1,0:T(8,128)}, u32[]{:S(2)}, u32[]{:S(2)}) collective-permute-start(f32[2,2,64,256]{3,2,1,0:T(8,128)} %refs_4_.1), channel_id=1, source_target_pairs={{0,3},{1,0},{2,1},{3,2},{4,7},{5,4},{6,5},{7,6},{8,11},{9,8},{10,9... | collective-permute-start | bytes 786440 | tf_op jit(solution)/shard_map/ppermute | solution.py:38
  11.0 14.7 %all-to-all-start = ((f32[8,80,256]{2,1,0:T(8,128)}), f32[8,80,256]{2,1,0:T(8,128)S(1)}, u32[]{:S(2)}, u32[]{:S(2)}) async-start(f32[8,80,256]{2,1,0:T(8,128)} %shard_map.73), calls=%async_computation | async-start | bytes 1310720 | tf_op jit(solution)/shard_map/all_to_all | solution.py:362
  14.6 8.0 %collective-permute-start.1 = (f32[8,64,256]{2,1,0:T(8,128)S(1)}, f32[8,64,256]{2,1,0:T(8,128)S(1)}, u32[]{:S(2)}, u32[]{:S(2)}) collective-permute-start(f32[8,64,256]{2,1,0:T(8,128)S(1)} %copy-done), channel_id=1, source_target_pairs={{0,4},{4,0},{8,12},{12,8},{16,20},{20,16},{24,28},{28,24},{1,5},{5... | collective-permute-start | bytes 1572872 | tf_op jit(solution)/shard_map/ppermute | solution.py:33
  19.3 6.5 %collective-permute-start.5 = (f32[8,64,256]{2,1,0:T(8,128)S(1)}, f32[8,64,256]{2,1,0:T(8,128)}, u32[]{:S(2)}, u32[]{:S(2)}) collective-permute-start(f32[8,64,256]{2,1,0:T(8,128)S(1)} %collective-permute-done.2.refs_2_), channel_id=1, source_target_pairs={{0,4},{4,0},{8,12},{12,8},{16,20},{20,16},{24,28},{28,24},{1,5},{5... | collective-permute-start | bytes 1572872 | tf_op jit(solution)/shard_map/ppermute | solution.py:33
  19.3 9.4 %collective-permute-start.6 = (f32[2,2,64,256]{3,2,1,0:T(8,128)}, f32[2,2,64,256]{3,2,1,0:T(8,128)}, u32[]{:S(2)}, u32[]{:S(2)}) collective-permute-start(f32[2,2,64,256]{3,2,1,0:T(8,128)} %collective-permute-done.4.refs_7_), channel_id=1, source_target_pairs={{0,3},{1,0},{2,1},{3,2},{4,7},{5,4},{6,5},{7,6},{8,11},{9,8},{10,9... | collective-permute-start | bytes 786440 | tf_op jit(solution)/shard_map/ppermute | solution.py:38
  21.6 15.6 %collective-permute-start.7 = (f32[2,2,64,256]{3,2,1,0:T(8,128)}, f32[2,2,64,256]{3,2,1,0:T(8,128)S(1)}, u32[]{:S(2)}, u32[]{:S(2)}) collective-permute-start(f32[2,2,64,256]{3,2,1,0:T(8,128)} %collective-permute-done.3.refs_5_), channel_id=1, source_target_pairs={{0,16},{4,20},{8,24},{12,28},{16,0},{20,4},{24,8},{28,12},{1,17},{... | collective-permute-start | bytes 786440 | tf_op jit(solution)/shard_map/ppermute | solution.py:38
  22.2 15.7 %collective-permute-start.9 = (f32[2,2,64,256]{3,2,1,0:T(8,128)S(1)}, f32[2,2,64,256]{3,2,1,0:T(8,128)S(1)}, u32[]{:S(2)}, u32[]{:S(2)}) collective-permute-start(f32[2,2,64,256]{3,2,1,0:T(8,128)S(1)} %collective-permute-done.refs_3_), channel_id=1, source_target_pairs={{0,3},{1,0},{2,1},{3,2},{4,7},{5,4},{6,5},{7,6},{8,11},{9,8},{10,9... | collective-permute-start | bytes 786440 | tf_op jit(solution)/shard_map/ppermute | solution.py:38
  27.6 10.3 %collective-permute-start.10 = (f32[8,40,128]{2,1,0:T(8,128)S(1)}, f32[8,40,128]{2,1,0:T(8,128)S(1)}, u32[]{:S(2)}, u32[]{:S(2)}) collective-permute-start(f32[8,40,128]{2,1,0:T(8,128)S(1)} %get-tuple-element.48.refs_7_), channel_id=1, source_target_pairs={{0,12},{4,8},{8,4},{12,0},{16,28},{20,24},{24,20},{28,16},{1,13},{... | collective-permute-start | bytes 491528 | tf_op jit(solution)/shard_map/ppermute | solution.py:33
  27.8 13.5 %collective-permute-start.12 = (f32[8,40,128]{2,1,0:T(8,128)S(1)}, f32[8,40,128]{2,1,0:T(8,128)S(1)}, u32[]{:S(2)}, u32[]{:S(2)}) collective-permute-start(f32[8,40,128]{2,1,0:T(8,128)S(1)} %get-tuple-element.48.refs_7_), channel_id=1, source_target_pairs={{0,8},{4,12},{8,0},{12,4},{16,24},{20,28},{24,16},{28,20},{1,9},{5... | collective-permute-start | bytes 491528 | tf_op jit(solution)/shard_map/ppermute | solution.py:33
  28.7 9.2 %collective-permute-start.8 = (f32[2,2,64,256]{3,2,1,0:T(8,128)}, f32[2,2,64,256]{3,2,1,0:T(8,128)S(1)}, u32[]{:S(2)}, u32[]{:S(2)}) collective-permute-start(f32[2,2,64,256]{3,2,1,0:T(8,128)} %collective-permute-done.6.refs_6_), channel_id=1, source_target_pairs={{0,16},{4,20},{8,24},{12,28},{16,0},{20,4},{24,8},{28,12},{1,17},{... | collective-permute-start | bytes 786440 | tf_op jit(solution)/shard_map/ppermute | solution.py:38
  29.2 0.9 %copy-start.2 = (f32[2,2,64,256]{3,2,1,0:T(8,128)S(1)}, f32[2,2,64,256]{3,2,1,0:T(8,128)}, u32[]{:S(2)}) copy-start(f32[2,2,64,256]{3,2,1,0:T(8,128)} %refs_4_.1) | copy-start | bytes 786436
  37.3 7.9 %collective-permute-start.14 = (f32[8,40,128]{2,1,0:T(8,128)S(1)}, f32[8,40,128]{2,1,0:T(8,128)S(1)}, u32[]{:S(2)}, u32[]{:S(2)}) collective-permute-start(f32[8,40,128]{2,1,0:T(8,128)S(1)} %get-tuple-element.48.refs_7_), channel_id=1, source_target_pairs={{0,4},{4,0},{8,12},{12,8},{16,20},{20,16},{24,28},{28,24},{1,5},{5... | collective-permute-start | bytes 491528 | tf_op jit(solution)/shard_map/ppermute | solution.py:33
  43.7 7.2 %collective-permute-start.13 = (f32[8,32,128]{2,1,0:T(8,128)S(1)}, f32[8,32,128]{2,1,0:T(8,128)S(1)}, u32[]{:S(2)}, u32[]{:S(2)}) collective-permute-start(f32[8,32,128]{2,1,0:T(8,128)S(1)} %shard_map.77), channel_id=1, source_target_pairs={{0,8},{4,12},{8,0},{12,4},{16,24},{20,28},{24,16},{28,20},{1,9},{5... | collective-permute-start | bytes 393224 | tf_op jit(solution)/shard_map/ppermute | solution.py:33
  44.3 6.7 %collective-permute-start.11 = (f32[8,32,128]{2,1,0:T(8,128)S(1)}, f32[8,32,128]{2,1,0:T(8,128)S(1)}, u32[]{:S(2)}, u32[]{:S(2)}) collective-permute-start(f32[8,32,128]{2,1,0:T(8,128)S(1)} %shard_map.76), channel_id=1, source_target_pairs={{0,12},{4,8},{8,4},{12,0},{16,28},{20,24},{24,20},{28,16},{1,13},{... | collective-permute-start | bytes 393224 | tf_op jit(solution)/shard_map/ppermute | solution.py:33
  47.7 3.4 %collective-permute-start.15 = (f32[8,32,128]{2,1,0:T(8,128)S(1)}, f32[8,32,128]{2,1,0:T(8,128)S(1)}, u32[]{:S(2)}, u32[]{:S(2)}) collective-permute-start(f32[8,32,128]{2,1,0:T(8,128)S(1)} %shard_map.78), channel_id=1, source_target_pairs={{0,4},{4,0},{8,12},{12,8},{16,20},{20,16},{24,28},{28,24},{1,5},{5... | collective-permute-start | bytes 393224 | tf_op jit(solution)/shard_map/ppermute | solution.py:33
